TPU v7x, 32 devices: a whole 2x2x4 slice. The times are simulated.
32 devices in a mesh: row: 16 (over z, y, core), col: 2 (over x).
Axes of the slice: x: 2, y: 2, z: 4, core: 2. Of those that a mesh axis runs over, the one named last changes fastest.
Arguments:
- stem_slab: float32 [2, 256, 256, 256], P(None, 'row', None, 'col'), may hold values from -6 to 6
- factors: float32 [32, 2, 2, 256, 256], P(('row', 'col')), may hold values from -0.25 to 0.25
- branch_owner: int32 [4], replicated, may hold values from 0 to 31
- entangle_phase: float32 [4, 256, 256], replicated, may hold values from -3.140625 to 3.140625
Outputs:
- contracted: float32 [2, 256, 256, 256], P(None, 'row', None, 'col')
All inputs are finite; a program needn't handle non-finite values.
Results may differ from a plain program's by a relative error of at most 0.000039.
Values sent between devices are 32-bit elements; how exact they have to be, the bound alone decides.
No kernel may reach another device: no remote copies, remote signals or barrier semaphores. Data moves between devices by JAX's collectives and lax.ppermute only.
A program may use at most 64 MiB of HBM per device.

v0:
```python
from functools import partial

import jax
import jax.numpy as jnp
from jax import lax
from jax.sharding import PartitionSpec as P

STEPS = 4


def from_root(array, axis, root):
    mine = lax.axis_index(axis) == root
    return lax.psum(jnp.where(mine, array, jnp.zeros_like(array)), axis)


def complex_mix(stacked, branch, form):
    mix = partial(jnp.einsum, form, precision=lax.Precision.HIGHEST)
    real_part, imag_part = (stacked[0], stacked[1])
    branch_real, branch_imag = (branch[0], branch[1])
    return jnp.stack(
        [
            mix(real_part, branch_real) - mix(imag_part, branch_imag),
            mix(real_part, branch_imag) + mix(imag_part, branch_real),
        ]
    )


def rotate(stacked, angles):
    cosine = jnp.cos(angles)[:, :, None]
    sine = jnp.sin(angles)[:, :, None]
    real_part, imag_part = (stacked[0], stacked[1])
    return jnp.stack([real_part * cosine - imag_part * sine, real_part * sine + imag_part * cosine])


def build_branch(owned):
    dot_high = partial(jnp.dot, precision=lax.Precision.HIGHEST)
    left_real, left_imag = (owned[0, 0], owned[0, 1])
    right_real, right_imag = (owned[1, 0], owned[1, 1])
    return jnp.stack(
        [
            dot_high(left_real, right_real) - dot_high(left_imag, right_imag),
            dot_high(left_real, right_imag) + dot_high(left_imag, right_real),
        ]
    )


def first_group(stem_local, branch, angles_all, row_index):
    pieces = lax.all_to_all(stem_local, "row", split_axis=2, concat_axis=1, tiled=True)
    pieces = complex_mix(pieces, branch, "akb,al->lkb")
    width_part = pieces.shape[2]
    angles = lax.dynamic_slice_in_dim(angles_all, row_index * width_part, width_part, 1)
    pieces = rotate(pieces, angles)
    return lax.all_to_all(pieces, "row", split_axis=1, concat_axis=2, tiled=True)


def on_device(stem_slab, factors, branch_owner, entangle_phase):
    own_branch = build_branch(factors[0])
    row_index = lax.axis_index("row")
    branches = []
    for step in range(STEPS):
        branches.append(from_root(own_branch, ("row", "col"), branch_owner[step]))
    rows_local = stem_slab.shape[1]
    stem_local = stem_slab
    for step in range(STEPS):
        if step % 2 == 0:
            stem_local = complex_mix(stem_local, branches[step], "akb,kl->alb")
            angles = lax.dynamic_slice_in_dim(
                entangle_phase[step], row_index * rows_local, rows_local, 0
            )
            stem_local = rotate(stem_local, angles)
        else:
            stem_local = first_group(stem_local, branches[step], entangle_phase[step], row_index)
    return stem_local


def solution(mesh):
    return jax.shard_map(
        on_device,
        mesh=mesh,
        in_specs=(P(None, "row", None, "col"), P(("row", "col"), None, None, None, None), P(), P()),
        out_specs=P(None, "row", None, "col"),
        check_vma=False,
    )
```

profile of v0, /device:TPU:13, one launch (start us, length us, event | category | flops | bytes accessed | tf_op | source)
XLA Modules:
  0.0 624.0 jit_solution(14502299552992795895)
XLA Ops:
  6.5 1.5 fusion.28
  9.5 1.5 fusion.40
  17.4 133.4 %all-reduce.3.cloned.1.call-done = (f32[2,256,256]{2,1,0:T(8,128)}, f32[2,256,256]{2,1,0:T(8,128)}, f32[2,256,256]{2,1,0:T(8,128)}, f32[2,256,256]{2,1,0:T(8,128)}) async-done(((f32[2,256,256]{2,1,0:T(8,128)}, f32[2,256,256]{2,1,0:T(8,128)}, f32[2,256,256]{2,1,0:T(8,128)}, f32[2,256,256]{2,1,0:T(8,128)}), (f32[2,256,256]{2,1,0:T(8,128)}, f32[2,256,256]{2,1,0:T(8,128)}, f32[2,256,256]{2,1,0:T(8,128)}, ...) | async-done | bytes 2097168 | tf_op jit(solution)/shard_map/psum | solution.py:13
  150.8 3.7 fusion.8
  154.5 2.9 fusion.10
  157.5 2.1 fusion.20
  159.6 3.0 fusion.5
  163.1 4.7 copy.36
  167.8 7.0 %all-to-all-start = ((f32[2,16,256,128]{3,1,0,2:T(8,128)}), f32[2,16,256,128]{3,1,0,2:T(8,128)}, u32[]{:S(2)}, u32[]{:S(2)}) async-start(f32[2,16,256,128]{3,1,0,2:T(8,128)} %copy.36), calls=%async_computation | async-start | bytes 8388608 | tf_op jit(solution)/shard_map/all_to_all | solution.py:48
  176.0 91.2 %all-to-all-done = f32[2,16,256,128]{3,1,0,2:T(8,128)} async-done(((f32[2,16,256,128]{3,1,0,2:T(8,128)}), f32[2,16,256,128]{3,1,0,2:T(8,128)}, u32[]{:S(2)}, u32[]{:S(2)}) %all-to-all-start) | async-done | bytes 4194336 | tf_op jit(solution)/shard_map/all_to_all | solution.py:48
  267.2 2.7 copy.97
  271.0 1.9 fusion.33
  272.9 1.9 fusion.32
  274.8 2.1 convolution_add_fusion.2
  276.9 2.8 subtract_bitcast_fusion.1
  280.2 11.4 %copy.44 = f32[2,256,16,128]{3,2,0,1:T(8,128)S(1)} copy(f32[2,256,16,128]{3,1,2,0:T(8,128)S(1)} %pad_maximum_fusion.1) | data formatting | bytes 8388608 | tf_op jit(solution)/shard_map/stack | solution.py:32
  291.6 96.9 %all_to_all.63 = f32[2,256,16,128]{3,2,0,1:T(8,128)S(1)} all-to-all(f32[2,256,16,128]{3,2,0,1:T(8,128)S(1)} %copy.44), channel_id=1, replica_groups=mesh['row'=16,'col'=2] {'row'}, dimensions={1} | all-to-all | bytes 8388608 | tf_op jit(solution)/shard_map/all_to_all | solution.py:53
  390.2 1.9 fusion.34
  392.1 1.9 fusion.31
  394.0 2.1 convolution_add_fusion.1
  396.1 2.8 fusion.1
  399.4 4.7 copy.50
  404.0 5.3 all-to-all-start.2
  409.5 92.3 %all-to-all-done.2 = f32[2,16,256,128]{3,1,0,2:T(8,128)} async-done(((f32[2,16,256,128]{3,1,0,2:T(8,128)}), f32[2,16,256,128]{3,1,0,2:T(8,128)}, u32[]{:S(2)}, u32[]{:S(2)}) %all-to-all-start.2) | async-done | bytes 4194336 | tf_op jit(solution)/shard_map/all_to_all | solution.py:48
  501.8 2.7 copy.95
  505.6 1.9 fusion.35
  507.5 1.9 fusion.30
  509.4 2.1 convolution_add_fusion
  511.5 2.8 subtract_bitcast_fusion
  514.8 2.4 copy.58
  517.3 97.0 %all_to_all.64 = f32[2,256,16,128]{3,2,0,1:T(8,128)S(1)} all-to-all(f32[2,256,16,128]{3,2,0,1:T(8,128)S(1)} %copy.58), channel_id=1, replica_groups=mesh['row'=16,'col'=2] {'row'}, dimensions={1} | all-to-all | bytes 8388608 | tf_op jit(solution)/shard_map/all_to_all | solution.py:53
  614.2 2.6 copy.59
  (35 shorter events, 12.0 us)
Async XLA Ops:
  6.5 8.4 %copy-start.1 = (f32[1,2,2,256,256]{4,3,2,1,0:T(8,128)S(1)}, f32[1,2,2,256,256]{4,3,2,1,0:T(8,128)}, u32[]{:S(2)}) copy-start(f32[1,2,2,256,256]{4,3,2,1,0:T(8,128)} %param.5) | copy-start | bytes 3145732
  6.5 144.3 %all-reduce.3.cloned.1.call-start = ((), (), s32[]{:S(2)}) async-start(), calls=%async_computation.4 | async-start | bytes 4194304 | tf_op jit(solution)/shard_map/psum | solution.py:13
  15.3 1.8 copy-start.6
  150.8 3.7 copy-start
  154.5 3.0 copy-start.5
  167.8 99.5 %all-to-all-start = ((f32[2,16,256,128]{3,1,0,2:T(8,128)}), f32[2,16,256,128]{3,1,0,2:T(8,128)}, u32[]{:S(2)}, u32[]{:S(2)}) async-start(f32[2,16,256,128]{3,1,0,2:T(8,128)} %copy.36), calls=%async_computation | async-start | bytes 8388608 | tf_op jit(solution)/shard_map/all_to_all | solution.py:48
  270.0 1.0 copy-start.4
  389.1 1.0 copy-start.3
  404.0 97.8 %all-to-all-start.2 = ((f32[2,16,256,128]{3,1,0,2:T(8,128)}), f32[2,16,256,128]{3,1,0,2:T(8,128)}, u32[]{:S(2)}, u32[]{:S(2)}) async-start(f32[2,16,256,128]{3,1,0,2:T(8,128)} %copy.50), calls=%async_computation.2 | async-start | bytes 8388608 | tf_op jit(solution)/shard_map/all_to_all | solution.py:48
  504.6 1.0 copy-start.2
Sparse Core Ops, SparseCore 0:
  16.8 133.9 all-reduce.2
where the time goes:
time: 634 us; the launch traced here: 624 us
  waiting for transfers between devices  317 us (50%)
  blocking collectives  194 us (31%)
  matrix products  42.6 us (7%)
  local copies, waits for them, and re-layouts  38.4 us (6%)
  between operations  16.7 us (3%)
  starting transfers between devices  12.3 us (2%)
    all_to_all x2, blocking collectives, first_group(): lax.all_to_all(pieces, 'row', split_axis=1, concat_axis=2, tiled=True)  194 us
    all_to_all x2, waiting for transfers between devices, first_group(): lax.all_to_all(stem_local, 'row', split_axis=2, concat_axis=1, tiled=True)  184 us
    psum x1, waiting for transfers between devices, from_root(): return lax.psum(jnp.where(mine, array, jnp.zeros_like(array)), axis)  133 us
    another operation x4, local copies, waits for them, and re-layouts, rotate(): jnp.stack([real_part * cosine - imag_part * sine, real_part * sine + imag...  23.2 us
  transfers between devices with their start and end apart: 3, of which 3 were waited for; matrix products, arithmetic and copies ran while one was open for 0% of the time, Pallas kernels for 0%

commit v1 on v0

v1 whole, which is shorter than its diff:
```python
from functools import partial

import jax
import jax.numpy as jnp
from jax import lax
from jax.experimental import pallas as pl
from jax.experimental.pallas import tpu as pltpu
from jax.sharding import PartitionSpec as P

STEPS = 4
MIB = 1024 * 1024
DOT = partial(jnp.dot, precision=lax.Precision.HIGHEST)


def build_branch(owned):
    left_real, left_imag = (owned[0, 0], owned[0, 1])
    right_real, right_imag = (owned[1, 0], owned[1, 1])
    return jnp.stack(
        [
            DOT(left_real, right_real) - DOT(left_imag, right_imag),
            DOT(left_real, right_imag) + DOT(left_imag, right_real),
        ]
    )


def swap(array, axis, size, bit):
    return lax.ppermute(array, axis, [(i, i ^ bit) for i in range(size)])


def bits_of(size):
    return [1 << i for i in range(size.bit_length() - 1)]


def broadcast_branches(own, owners, rows, cols):
    row, col = lax.axis_index("row"), lax.axis_index("col")
    mine = (owners == row * cols + col).reshape(STEPS, 1, 1, 1)
    width = own.shape[-1]
    held = jnp.where(mine, own[None], 0.0).reshape(-1, width)
    row_bits = bits_of(rows)
    halved = [("row", rows, row, b) for b in row_bits[:1]]
    halved += [("col", cols, col, b) for b in bits_of(cols)]
    halved += [("row", rows, row, b) for b in row_bits[1:2]]
    for axis, size, index, bit in halved:
        half = held.shape[0] // 2
        high = (index & bit) // bit
        keep = lax.dynamic_slice_in_dim(held, high * half, half, 0)
        send = lax.dynamic_slice_in_dim(held, (1 - high) * half, half, 0)
        held = keep + swap(send, axis, size, bit)
    for bit in row_bits[2:]:
        held = held + swap(held, "row", rows, bit)
    for axis, size, index, bit in reversed(halved):
        other = swap(held, axis, size, bit)
        high = (index & bit) != 0
        held = jnp.concatenate([jnp.where(high, other, held), jnp.where(high, held, other)], 0)
    return held.reshape(STEPS, 2, width, width)


def split(value):
    high = value.astype(jnp.bfloat16)
    low = (value - high.astype(jnp.float32)).astype(jnp.bfloat16)
    return high, low


def prepare_kernel(branch_ref, even_ref, odd_ref):
    for step in range(STEPS):
        real, imag = branch_ref[step, 0], branch_ref[step, 1]
        if step % 2:
            real, imag = real.T, imag.T
        axis = 1 if step % 2 else 0
        (rh, rl), (ih, il) = split(real), split(imag)
        to_real = jnp.concatenate([rh, rh, rl, -ih, -ih, -il], axis)
        to_imag = jnp.concatenate([ih, ih, il, rh, rh, rl], axis)
        out = jnp.concatenate([to_real, to_imag], 1 - axis)
        if step % 2:
            odd_ref[step // 2] = out
        else:
            even_ref[step // 2] = out


def prepare(branches):
    width = branches.shape[-1]
    pairs = STEPS // 2
    return pl.pallas_call(
        prepare_kernel,
        out_shape=(
            jax.ShapeDtypeStruct((pairs, 6 * width, 2 * width), jnp.bfloat16),
            jax.ShapeDtypeStruct((pairs, 2 * width, 6 * width), jnp.bfloat16),
        ),
        compiler_params=pltpu.CompilerParams(vmem_limit_bytes=48 * MIB),
        name="prepare",
    )(branches)


def absorb_kernel(stem_ref, even_ref, odd_ref, cos_ref, sin_ref, out_ref):
    width = cos_ref.shape[1]
    for item in range(stem_ref.shape[1]):
        real = stem_ref[:, item, 0].reshape(width, width)
        imag = stem_ref[:, item, 1].reshape(width, width)
        for step in range(STEPS):
            (rh, rl), (ih, il) = split(real), split(imag)
            if step % 2 == 0:
                stacked = jnp.concatenate([rh, rl, rh, ih, il, ih], 1)
                both = jnp.dot(stacked, even_ref[step // 2], preferred_element_type=jnp.float32)
                real, imag = both[:, :width], both[:, width:]
            else:
                stacked = jnp.concatenate([rh, rl, rh, ih, il, ih], 0)
                both = jnp.dot(odd_ref[step // 2], stacked, preferred_element_type=jnp.float32)
                real, imag = both[:width], both[width:]
            cosine, sine = cos_ref[step], sin_ref[step]
            real, imag = real * cosine - imag * sine, real * sine + imag * cosine
        shape = (stem_ref.shape[0], stem_ref.shape[3], width)
        out_ref[:, item, 0] = real.reshape(shape)
        out_ref[:, item, 1] = imag.reshape(shape)


def absorb(stem, even, odd, cosine, sine):
    peers, items, _, block, width = stem.shape
    per = 2 if items % 2 == 0 else 1
    spec = pl.BlockSpec((peers, per, 2, block, width), lambda i: (0, i, 0, 0, 0))
    whole = pl.BlockSpec(memory_space=pltpu.VMEM)
    flops = items * STEPS * 12 * 2 * width**3
    return pl.pallas_call(
        absorb_kernel,
        grid=(items // per,),
        in_specs=[spec, whole, whole, whole, whole],
        out_specs=spec,
        out_shape=jax.ShapeDtypeStruct(stem.shape, jnp.float32),
        cost_estimate=pl.CostEstimate(flops=flops, bytes_accessed=8 * stem.size, transcendentals=0),
        compiler_params=pltpu.CompilerParams(vmem_limit_bytes=56 * MIB),
        name="absorb",
    )(stem, even, odd, cosine, sine)


def batch_first_kernel(stem_ref, out_ref):
    for i in range(stem_ref.shape[1]):
        out_ref[:, 0, i, :] = stem_ref[0, i].T


def batch_first(stem):
    parts, rows, width, batch = stem.shape
    return pl.pallas_call(
        batch_first_kernel,
        grid=(parts, rows // 8),
        in_specs=[pl.BlockSpec((1, 8, width, batch), lambda p, r: (p, r, 0, 0))],
        out_specs=pl.BlockSpec((batch, 1, 8, width), lambda p, r: (0, p, r, 0)),
        out_shape=jax.ShapeDtypeStruct((batch, parts, rows, width), jnp.float32),
        compiler_params=pltpu.CompilerParams(vmem_limit_bytes=48 * MIB),
        name="batch_first",
    )(stem)


def batch_last_kernel(stem_ref, out_ref):
    for i in range(out_ref.shape[1]):
        out_ref[0, i] = stem_ref[:, 0, i, :].T


def batch_last(stem):
    batch, parts, rows, width = stem.shape
    return pl.pallas_call(
        batch_last_kernel,
        grid=(parts, rows // 8),
        in_specs=[pl.BlockSpec((batch, 1, 8, width), lambda p, r: (0, p, r, 0))],
        out_specs=pl.BlockSpec((1, 8, width, batch), lambda p, r: (p, r, 0, 0)),
        out_shape=jax.ShapeDtypeStruct((parts, rows, width, batch), jnp.float32),
        compiler_params=pltpu.CompilerParams(vmem_limit_bytes=48 * MIB),
        name="batch_last",
    )(stem)


def on_device(stem_slab, factors, branch_owner, entangle_phase, *, rows, cols):
    parts, block, width, batch = stem_slab.shape
    items = batch // rows
    sent = batch_first(stem_slab).reshape(rows, items, parts, block, width)
    stem = lax.all_to_all(sent, "row", 0, 0, tiled=True)
    branches = broadcast_branches(build_branch(factors[0]), branch_owner, rows, cols)
    even, odd = prepare(branches)
    stem = absorb(stem, even, odd, jnp.cos(entangle_phase), jnp.sin(entangle_phase))
    stem = lax.all_to_all(stem, "row", 0, 0, tiled=True)
    return batch_last(stem.reshape(batch, parts, block, width))


def solution(mesh):
    return jax.shard_map(
        partial(on_device, rows=mesh.shape["row"], cols=mesh.shape["col"]),
        mesh=mesh,
        in_specs=(P(None, "row", None, "col"), P(("row", "col"), None, None, None, None), P(), P()),
        out_specs=P(None, "row", None, "col"),
        check_vma=False,
    )
```

time: 634 us -> 278 us (0.44); the launches traced: 624 us -> 276 us
  waiting for transfers between devices: 317 us -> 112 us
  blocking collectives: 194 us -> 99 us
  matrix products: 42.6 us -> 1.52 us
  Pallas kernels: 0 us -> 36.8 us
  local copies, waits for them, and re-layouts: 38.4 us -> 8.49 us
  between operations: 16.7 us -> 0.16 us
    all_to_all x2 -> x1, waiting for transfers between devices: 184 us -> 0.01 us  [on_device(): stem = lax.all_to_all(sent, 'row', 0, 0, tiled=True)]
    psum x1 -> x0, waiting for transfers between devices: 133 us -> none  [from_root(): return lax.psum(jnp.where(mine, array, jnp.zeros_like(array)), axis)]
    ppermute x0 -> x8, waiting for transfers between devices: none -> 112 us  [swap(): return lax.ppermute(array, axis, [(i, i ^ bit) for i in range(size)])]
    all_to_all x2 -> x1, blocking collectives: 194 us -> 99 us  [on_device(): stem = lax.all_to_all(stem, 'row', 0, 0, tiled=True)]
    dot_general x20 -> x4, matrix products: 42.6 us -> 1.52 us  [the longest x1 0.38 us: build_branch(): DOT(left_imag, right_real)]
    pallas_call x0 -> x4, Pallas kernels: none -> 36.8 us  [the longest x1 27.3 us: absorb(): pl.pallas_call(absorb_kernel, grid=(items // per,), in_specs=[spec, whole...]
    another operation x4 -> x0, local copies, waits for them, and re-layouts: 23.2 us -> none  [rotate(): jnp.stack([real_part * cosine - imag_part * sine, real_part * sine + imag...]
    all_to_all x4 -> x0, local copies, waits for them, and re-layouts: 8.59 us -> none  [the longest x2 5.47 us: first_group(): lax.all_to_all(stem_local, 'row', split_axis=2, concat_axis=1, tiled=True)]
  transfers between devices with their start and end apart: 3 -> 9, of which waited for: 3 -> 7; matrix products, arithmetic and copies ran while one was open for 0% -> 4% of each run, Pallas kernels for 0% -> 1%
where the time goes in v1:
time: 278 us; the launch traced here: 276 us
  waiting for transfers between devices  112 us (40%)
  blocking collectives  99 us (36%)
  Pallas kernels  36.8 us (13%)
  starting transfers between devices  14.1 us (5%)
  local copies, waits for them, and re-layouts  8.49 us (3%)
  other arithmetic  4.59 us (2%)
    ppermute x8, waiting for transfers between devices, swap(): return lax.ppermute(array, axis, [(i, i ^ bit) for i in range(size)])  112 us
    all_to_all x1, blocking collectives, on_device(): stem = lax.all_to_all(stem, 'row', 0, 0, tiled=True)  99 us
    pallas_call x1, Pallas kernels, absorb(): pl.pallas_call(absorb_kernel, grid=(items // per,), in_specs=[spec, whole...  27.3 us
    ppermute x8, starting transfers between devices, swap(): return lax.ppermute(array, axis, [(i, i ^ bit) for i in range(size)])  7.37 us
    all_to_all x1, starting transfers between devices, on_device(): stem = lax.all_to_all(sent, 'row', 0, 0, tiled=True)  6.69 us
  transfers between devices with their start and end apart: 9, of which 7 were waited for; matrix products, arithmetic and copies ran while one was open for 4% of the time, Pallas kernels for 1%

profile of v1, /device:TPU:13, one launch (start us, length us, event | category | flops | bytes accessed | tf_op | source)
XLA Modules:
  0.0 276.3 jit_solution(11533764388514999740)
XLA Ops:
  0.0 4.0 %batch_first.1 = f32[128,2,16,256]{3,2,1,0:T(8,128)S(1)} custom-call(f32[2,16,256,128]{3,2,1,0:T(8,128)} %stem_ref.1), custom_call_target="tpu_custom_call" | custom-call | tf_op jit(solution)/shard_map/batch_first/pallas_call | solution.py:141
  4.0 2.0 copy-done
  6.0 6.7 %all-to-all-start = ((f32[16,8,2,16,256]{4,3,2,1,0:T(8,128)}), f32[16,8,2,16,256]{4,3,2,1,0:T(8,128)}, u32[]{:S(2)}, u32[]{:S(2)}) async-start(f32[16,8,2,16,256]{4,3,2,1,0:T(8,128)} %bitcast.26), calls=%async_computation | async-start | bytes 8388608 | tf_op jit(solution)/shard_map/all_to_all | solution.py:174
  12.8 0.4 fusion.2
  13.2 0.4 fusion
  13.6 0.4 fusion.3
  14.0 0.4 fusion.1
  14.4 0.3 bitcast_select_fusion
  14.9 0.4 collective-permute-start
  15.3 2.4 collective-permute-done
  17.7 1.4 dynamic-slice_add_fusion
  19.2 1.3 collective-permute-start.1
  20.4 12.0 %collective-permute-done.1 = f32[512,256]{1,0:T(8,128)S(1)} collective-permute-done((f32[512,256]{1,0:T(8,128)S(1)}, f32[512,256]{1,0:T(8,128)S(1)}, u32[]{:S(2)}, u32[]{:S(2)}) %collective-permute-start.1) | collective-permute-done | bytes 524320 | tf_op jit(solution)/shard_map/ppermute | solution.py:27
  32.6 0.3 collective-permute-start.2
  32.9 11.5 %collective-permute-done.2 = f32[256,256]{1,0:T(8,128)S(1)} collective-permute-done((f32[256,256]{1,0:T(8,128)S(1)}, f32[256,256]{1,0:T(8,128)S(1)}, u32[]{:S(2)}, u32[]{:S(2)}) %collective-permute-start.2) | collective-permute-done | bytes 262176 | tf_op jit(solution)/shard_map/ppermute | solution.py:27
  44.5 0.6 collective-permute-start.3
  45.1 43.0 %collective-permute-done.3 = f32[256,256]{1,0:T(8,128)S(1)} collective-permute-done((f32[256,256]{1,0:T(8,128)S(1)}, f32[256,256]{1,0:T(8,128)S(1)}, u32[]{:S(2)}, u32[]{:S(2)}) %collective-permute-start.3) | collective-permute-done | bytes 262176 | tf_op jit(solution)/shard_map/ppermute | solution.py:27
  88.2 0.3 collective-permute-start.4
  88.5 25.6 %collective-permute-done.4 = f32[256,256]{1,0:T(8,128)S(1)} collective-permute-done((f32[256,256]{1,0:T(8,128)S(1)}, f32[256,256]{1,0:T(8,128)S(1)}, u32[]{:S(2)}, u32[]{:S(2)}) %collective-permute-start.4) | collective-permute-done | bytes 262176 | tf_op jit(solution)/shard_map/ppermute | solution.py:27
  114.2 0.4 collective-permute-start.5
  114.6 6.6 %collective-permute-done.5 = f32[256,256]{1,0:T(8,128)S(1)} collective-permute-done((f32[256,256]{1,0:T(8,128)S(1)}, f32[256,256]{1,0:T(8,128)S(1)}, u32[]{:S(2)}, u32[]{:S(2)}) %collective-permute-start.5) | collective-permute-done | bytes 262176 | tf_op jit(solution)/shard_map/ppermute | solution.py:27
  121.3 1.3 collective-permute-start.6
  122.5 10.4 %collective-permute-done.6 = f32[512,256]{1,0:T(8,128)S(1)} collective-permute-done((f32[512,256]{1,0:T(8,128)S(1)}, f32[512,256]{1,0:T(8,128)S(1)}, u32[]{:S(2)}, u32[]{:S(2)}) %collective-permute-start.6) | collective-permute-done | bytes 524320 | tf_op jit(solution)/shard_map/ppermute | solution.py:27
  133.0 1.0 pad_maximum_fusion.1
  134.1 2.7 collective-permute-start.7
  136.8 4.5 %fusion.4 = (f32[4,256,256]{2,1,0:T(8,128)}, f32[4,256,256]{2,1,0:T(8,128)}) fusion(f32[4,256,256]{2,1,0:T(8,128)S(1)} %copy-done.3), kind=kLoop, calls=%fused_computation.28 | loop fusion | bytes 3145728 | tf_op jit(solution)/shard_map/sin | solution.py:177
  141.3 1.4 broadcast_select_fusion.1
  142.8 2.1 prepare.1
  144.9 1.7 copy-done.1
  146.6 27.3 %absorb.1 = f32[16,8,2,16,256]{4,3,2,1,0:T(8,128)} custom-call(f32[16,8,2,16,256]{4,3,2,1,0:T(8,128)} %all-to-all-done.stem_ref, bf16[2,1536,512]{2,1,0:T(8,128)(2,1)} %copy-done.1, bf16[2,512,1536]{2,1,0:T(8,128)(2,1)} %get-tuple-element.8.odd_ref, f32[4,256,256]{2,1,0:T(8,128)} %get-tuple-element.12.cos_ref, f32[4,256,256]{2,1,0:T(8,128)} %get-tuple-element.11.sin_ref), custom_call_target="tpu_custom_call" | custom-call | flops 12884901888 | bytes 8388608 | tf_op jit(solution)/shard_map/absorb/pallas_call | solution.py:122
  173.9 99.0 %all_to_all.10 = f32[16,8,2,16,256]{4,3,2,1,0:T(8,128)S(1)} all-to-all(f32[16,8,2,16,256]{4,3,2,1,0:T(8,128)} %absorb.1), channel_id=1, replica_groups=mesh['row'=16,'col'=2] {'row'}, dimensions={0} | all-to-all | bytes 8388608 | tf_op jit(solution)/shard_map/all_to_all | solution.py:178
  272.9 3.4 %batch_last.1 = f32[2,16,256,128]{3,2,1,0:T(8,128)} custom-call(f32[128,2,16,256]{3,2,1,0:T(8,128)S(1)} %bitcast.27), custom_call_target="tpu_custom_call" | custom-call | tf_op jit(solution)/shard_map/batch_last/pallas_call | solution.py:159
  (25 shorter events, 0.8 us)
Async XLA Ops:
  4.0 2.0 copy-start
  6.0 6.7 %copy-start.4 = (s32[4]{0:T(128)S(1)}, s32[4]{0:T(128)}, u32[]{:S(2)}) copy-start(s32[4]{0:T(128)} %param.6) | copy-start | bytes 52
  6.0 6.8 %copy-start.2 = (f32[1,2,2,256,256]{4,3,2,1,0:T(8,128)S(1)}, f32[1,2,2,256,256]{4,3,2,1,0:T(8,128)}, u32[]{:S(2)}) copy-start(f32[1,2,2,256,256]{4,3,2,1,0:T(8,128)} %param.5) | copy-start | bytes 3145732
  6.0 140.6 %all-to-all-start = ((f32[16,8,2,16,256]{4,3,2,1,0:T(8,128)}), f32[16,8,2,16,256]{4,3,2,1,0:T(8,128)}, u32[]{:S(2)}, u32[]{:S(2)}) async-start(f32[16,8,2,16,256]{4,3,2,1,0:T(8,128)} %bitcast.26), calls=%async_computation | async-start | bytes 8388608 | tf_op jit(solution)/shard_map/all_to_all | solution.py:174
  14.9 2.9 %collective-permute-start = (f32[1024,256]{1,0:T(8,128)S(1)}, f32[1024,256]{1,0:T(8,128)}, u32[]{:S(2)}, u32[]{:S(2)}) collective-permute-start(f32[1024,256]{1,0:T(8,128)S(1)} %constant_dynamic-slice_fusion.2), channel_id=1, source_target_pairs={{0,2},{2,0},{4,6},{6,4},{8,10},{10,8},{12,14},{14,12},{16,18},{18,... | collective-permute-start | bytes 3145736 | tf_op jit(solution)/shard_map/ppermute | solution.py:27
  19.2 13.3 %collective-permute-start.1 = (f32[512,256]{1,0:T(8,128)S(1)}, f32[512,256]{1,0:T(8,128)S(1)}, u32[]{:S(2)}, u32[]{:S(2)}) collective-permute-start(f32[512,256]{1,0:T(8,128)S(1)} %constant_dynamic-slice_fusion.1), channel_id=1, source_target_pairs={{0,1},{1,0},{2,3},{3,2},{4,5},{5,4},{6,7},{7,6},{8,9},{9,8},{10,11... | collective-permute-start | bytes 1572872 | tf_op jit(solution)/shard_map/ppermute | solution.py:27
  32.6 11.9 %collective-permute-start.2 = (f32[256,256]{1,0:T(8,128)S(1)}, f32[256,256]{1,0:T(8,128)S(1)}, u32[]{:S(2)}, u32[]{:S(2)}) collective-permute-start(f32[256,256]{1,0:T(8,128)S(1)} %constant_dynamic-slice_fusion), channel_id=1, source_target_pairs={{0,4},{2,6},{4,0},{6,2},{8,12},{10,14},{12,8},{14,10},{16,20},{18,... | collective-permute-start | bytes 786440 | tf_op jit(solution)/shard_map/ppermute | solution.py:27
  44.5 43.7 %collective-permute-start.3 = (f32[256,256]{1,0:T(8,128)S(1)}, f32[256,256]{1,0:T(8,128)S(1)}, u32[]{:S(2)}, u32[]{:S(2)}) collective-permute-start(f32[256,256]{1,0:T(8,128)S(1)} %dynamic-slice_add_fusion.2), channel_id=1, source_target_pairs={{0,8},{2,10},{4,12},{6,14},{8,0},{10,2},{12,4},{14,6},{16,24},{18,... | collective-permute-start | bytes 786440 | tf_op jit(solution)/shard_map/ppermute | solution.py:27
  88.2 25.9 %collective-permute-start.4 = (f32[256,256]{1,0:T(8,128)S(1)}, f32[256,256]{1,0:T(8,128)S(1)}, u32[]{:S(2)}, u32[]{:S(2)}) collective-permute-start(f32[256,256]{1,0:T(8,128)S(1)} %add.53), channel_id=1, source_target_pairs={{0,16},{2,18},{4,20},{6,22},{8,24},{10,26},{12,28},{14,30},{16,0},... | collective-permute-start | bytes 786440 | tf_op jit(solution)/shard_map/ppermute | solution.py:27
  114.2 7.0 %collective-permute-start.5 = (f32[256,256]{1,0:T(8,128)S(1)}, f32[256,256]{1,0:T(8,128)S(1)}, u32[]{:S(2)}, u32[]{:S(2)}) collective-permute-start(f32[256,256]{1,0:T(8,128)S(1)} %add.54), channel_id=1, source_target_pairs={{0,4},{2,6},{4,0},{6,2},{8,12},{10,14},{12,8},{14,10},{16,20},{18,... | collective-permute-start | bytes 786440 | tf_op jit(solution)/shard_map/ppermute | solution.py:27
  121.3 11.7 %collective-permute-start.6 = (f32[512,256]{1,0:T(8,128)S(1)}, f32[512,256]{1,0:T(8,128)S(1)}, u32[]{:S(2)}, u32[]{:S(2)}) collective-permute-start(f32[512,256]{1,0:T(8,128)S(1)} %pad_maximum_fusion.3), channel_id=1, source_target_pairs={{0,1},{1,0},{2,3},{3,2},{4,5},{5,4},{6,7},{7,6},{8,9},{9,8},{10,11... | collective-permute-start | bytes 1572872 | tf_op jit(solution)/shard_map/ppermute | solution.py:27
  122.5 14.2 %copy-start.3 = (f32[4,256,256]{2,1,0:T(8,128)S(1)}, f32[4,256,256]{2,1,0:T(8,128)}, u32[]{:S(2)}) copy-start(f32[4,256,256]{2,1,0:T(8,128)} %param.7) | copy-start | bytes 3145732
  134.1 7.2 %collective-permute-start.7 = (f32[1024,256]{1,0:T(8,128)}, f32[1024,256]{1,0:T(8,128)}, u32[]{:S(2)}, u32[]{:S(2)}) collective-permute-start(f32[1024,256]{1,0:T(8,128)} %pad_maximum_fusion.1), channel_id=1, source_target_pairs={{0,2},{2,0},{4,6},{6,4},{8,10},{10,8},{12,14},{14,12},{16,18},{18,... | collective-permute-start | bytes 3145736 | tf_op jit(solution)/shard_map/ppermute | solution.py:27
  144.9 1.7 copy-start.1

commit v2 on v1

--- a/solution.py
+++ b/solution.py
@@ -31,27 +31,53 @@
     return [1 << i for i in range(size.bit_length() - 1)]
 
 
-def broadcast_branches(own, owners, rows, cols):
+def halve(held, stage):
+    axis, size, index, bit = stage
+    half = held.shape[0] // 2
+    high = (index & bit) // bit
+    keep = lax.dynamic_slice_in_dim(held, high * half, half, 0)
+    send = lax.dynamic_slice_in_dim(held, (1 - high) * half, half, 0)
+    return keep + swap(send, axis, size, bit)
+
+
+def double(held, stage):
+    axis, size, index, bit = stage
+    other = swap(held, axis, size, bit)
+    high = (index & bit) != 0
+    return jnp.concatenate([jnp.where(high, other, held), jnp.where(high, held, other)], 0)
+
+
+def broadcast_orders(rows, cols):
     row, col = lax.axis_index("row"), lax.axis_index("col")
-    mine = (owners == row * cols + col).reshape(STEPS, 1, 1, 1)
-    width = own.shape[-1]
-    held = jnp.where(mine, own[None], 0.0).reshape(-1, width)
     row_bits = bits_of(rows)
-    halved = [("row", rows, row, b) for b in row_bits[:1]]
-    halved += [("col", cols, col, b) for b in bits_of(cols)]
-    halved += [("row", rows, row, b) for b in row_bits[1:2]]
-    for axis, size, index, bit in halved:
-        half = held.shape[0] // 2
-        high = (index & bit) // bit
-        keep = lax.dynamic_slice_in_dim(held, high * half, half, 0)
-        send = lax.dynamic_slice_in_dim(held, (1 - high) * half, half, 0)
-        held = keep + swap(send, axis, size, bit)
-    for bit in row_bits[2:]:
-        held = held + swap(held, "row", rows, bit)
-    for axis, size, index, bit in reversed(halved):
-        other = swap(held, axis, size, bit)
-        high = (index & bit) != 0
-        held = jnp.concatenate([jnp.where(high, other, held), jnp.where(high, held, other)], 0)
+    first = [("row", rows, row, b) for b in row_bits[:1]]
+    along_col = [("col", cols, col, b) for b in bits_of(cols)]
+    along_row = [("row", rows, row, b) for b in row_bits[1:2]]
+    return first, (along_col + along_row, along_row + along_col), row_bits[2:]
+
+
+def scatter_branches(own, owners, rows, cols):
+    first, orders, _ = broadcast_orders(rows, cols)
+    me = lax.axis_index("row") * cols + lax.axis_index("col")
+    mine = (owners == me).reshape(STEPS, 1, 1, 1)
+    held = jnp.where(mine, own[None], 0.0).reshape(-1, own.shape[-1])
+    for stage in first:
+        held = halve(held, stage)
+    halves = list(jnp.split(held, 2))
+    for at in range(len(orders[0])):
+        halves = [halve(part, order[at]) for part, order in zip(halves, orders)]
+    return jnp.concatenate(halves, 0)
+
+
+def gather_branches(held, rows, cols):
+    first, orders, _ = broadcast_orders(rows, cols)
+    halves = list(jnp.split(held, 2))
+    for at in reversed(range(len(orders[0]))):
+        halves = [double(part, order[at]) for part, order in zip(halves, orders)]
+    held = jnp.concatenate(halves, 0)
+    for stage in reversed(first):
+        held = double(held, stage)
+    width = held.shape[-1]
     return held.reshape(STEPS, 2, width, width)
 
 
@@ -86,7 +112,7 @@
             jax.ShapeDtypeStruct((pairs, 6 * width, 2 * width), jnp.bfloat16),
             jax.ShapeDtypeStruct((pairs, 2 * width, 6 * width), jnp.bfloat16),
         ),
-        compiler_params=pltpu.CompilerParams(vmem_limit_bytes=48 * MIB),
+        compiler_params=pltpu.CompilerParams(vmem_limit_bytes=60 * MIB),
         name="prepare",
     )(branches)
 
@@ -115,68 +141,109 @@
 
 def absorb(stem, even, odd, cosine, sine):
     peers, items, _, block, width = stem.shape
-    per = 2 if items % 2 == 0 else 1
-    spec = pl.BlockSpec((peers, per, 2, block, width), lambda i: (0, i, 0, 0, 0))
+    spec = pl.BlockSpec((peers, 1, 2, block, width), lambda i: (0, i, 0, 0, 0))
     whole = pl.BlockSpec(memory_space=pltpu.VMEM)
     flops = items * STEPS * 12 * 2 * width**3
     return pl.pallas_call(
         absorb_kernel,
-        grid=(items // per,),
+        grid=(items,),
         in_specs=[spec, whole, whole, whole, whole],
         out_specs=spec,
         out_shape=jax.ShapeDtypeStruct(stem.shape, jnp.float32),
         cost_estimate=pl.CostEstimate(flops=flops, bytes_accessed=8 * stem.size, transcendentals=0),
-        compiler_params=pltpu.CompilerParams(vmem_limit_bytes=56 * MIB),
+        compiler_params=pltpu.CompilerParams(vmem_limit_bytes=60 * MIB),
         name="absorb",
     )(stem, even, odd, cosine, sine)
 
 
-def batch_first_kernel(stem_ref, out_ref):
+def batch_first_kernel(start, stem_ref, out_ref):
+    batch = out_ref.shape[0]
     for i in range(stem_ref.shape[1]):
-        out_ref[:, 0, i, :] = stem_ref[0, i].T
-
-
-def batch_first(stem):
-    parts, rows, width, batch = stem.shape
-    return pl.pallas_call(
-        batch_first_kernel,
+        out_ref[:, 0, i, :] = stem_ref[0, i][:, start : start + batch].T
+
+
+def batch_first(stem, start, batch):
+    parts, rows, width, lanes = stem.shape
+    return pl.pallas_call(
+        partial(batch_first_kernel, start),
         grid=(parts, rows // 8),
-        in_specs=[pl.BlockSpec((1, 8, width, batch), lambda p, r: (p, r, 0, 0))],
+        in_specs=[pl.BlockSpec((1, 8, width, lanes), lambda p, r: (p, r, 0, 0))],
         out_specs=pl.BlockSpec((batch, 1, 8, width), lambda p, r: (0, p, r, 0)),
         out_shape=jax.ShapeDtypeStruct((batch, parts, rows, width), jnp.float32),
-        compiler_params=pltpu.CompilerParams(vmem_limit_bytes=48 * MIB),
+        cost_estimate=pl.CostEstimate(flops=0, bytes_accessed=8 * stem.size, transcendentals=0),
+        compiler_params=pltpu.CompilerParams(vmem_limit_bytes=60 * MIB),
         name="batch_first",
     )(stem)
 
 
-def batch_last_kernel(stem_ref, out_ref):
+def rows_first_kernel(stem_ref, out_ref):
     for i in range(out_ref.shape[1]):
-        out_ref[0, i] = stem_ref[:, 0, i, :].T
-
-
-def batch_last(stem):
+        out_ref[0, i] = stem_ref[:, 0, i, :]
+
+
+def rows_first(stem):
     batch, parts, rows, width = stem.shape
+    return pl.pallas_call(
+        rows_first_kernel,
+        grid=(parts, rows // 8),
+        in_specs=[pl.BlockSpec((batch, 1, 8, width), lambda p, r: (0, p, r, 0))],
+        out_specs=pl.BlockSpec((1, 8, batch, width), lambda p, r: (p, r, 0, 0)),
+        out_shape=jax.ShapeDtypeStruct((parts, rows, batch, width), jnp.float32),
+        cost_estimate=pl.CostEstimate(flops=0, bytes_accessed=8 * stem.size, transcendentals=0),
+        compiler_params=pltpu.CompilerParams(vmem_limit_bytes=60 * MIB),
+        name="rows_first",
+    )(stem)
+
+
+def batch_last_kernel(low_ref, high_ref, out_ref):
+    low = low_ref.shape[2]
+    for i in range(out_ref.shape[1]):
+        out_ref[0, i, :, :low] = low_ref[0, i].T
+        out_ref[0, i, :, low:] = high_ref[:, 0, i, :].T
+
+
+def batch_last(low, high):
+    parts, rows, low_batch, width = low.shape
+    high_batch = high.shape[0]
+    batch = low_batch + high_batch
     return pl.pallas_call(
         batch_last_kernel,
         grid=(parts, rows // 8),
-        in_specs=[pl.BlockSpec((batch, 1, 8, width), lambda p, r: (0, p, r, 0))],
+        in_specs=[
+            pl.BlockSpec((1, 8, low_batch, width), lambda p, r: (p, r, 0, 0)),
+            pl.BlockSpec((high_batch, 1, 8, width), lambda p, r: (0, p, r, 0)),
+        ],
         out_specs=pl.BlockSpec((1, 8, width, batch), lambda p, r: (p, r, 0, 0)),
         out_shape=jax.ShapeDtypeStruct((parts, rows, width, batch), jnp.float32),
-        compiler_params=pltpu.CompilerParams(vmem_limit_bytes=48 * MIB),
+        compiler_params=pltpu.CompilerParams(vmem_limit_bytes=60 * MIB),
         name="batch_last",
-    )(stem)
+    )(low, high)
+
+
+def exchange(parts):
+    return lax.all_to_all(parts, "row", 0, 0, tiled=True)
 
 
 def on_device(stem_slab, factors, branch_owner, entangle_phase, *, rows, cols):
     parts, block, width, batch = stem_slab.shape
     items = batch // rows
-    sent = batch_first(stem_slab).reshape(rows, items, parts, block, width)
-    stem = lax.all_to_all(sent, "row", 0, 0, tiled=True)
-    branches = broadcast_branches(build_branch(factors[0]), branch_owner, rows, cols)
-    even, odd = prepare(branches)
-    stem = absorb(stem, even, odd, jnp.cos(entangle_phase), jnp.sin(entangle_phase))
-    stem = lax.all_to_all(stem, "row", 0, 0, tiled=True)
-    return batch_last(stem.reshape(batch, parts, block, width))
+    low = max(1, items // 4)
+    high = items - low
+    sent_low = batch_first(stem_slab, 0, rows * low).reshape(rows, low, parts, block, width)
+    sent_low, factors = lax.optimization_barrier((sent_low, factors))
+    stem_low = exchange(sent_low)
+    held = scatter_branches(build_branch(factors[0]), branch_owner, rows, cols)
+    cosine, sine = jnp.cos(entangle_phase), jnp.sin(entangle_phase)
+    for bit in broadcast_orders(rows, cols)[2]:
+        held = held + swap(held, "row", rows, bit)
+    sent_high = batch_first(stem_slab, rows * low, rows * high).reshape(rows, high, parts, block, width)
+    held, sent_high, cosine, sine = lax.optimization_barrier((held, sent_high, cosine, sine))
+    stem_high = exchange(sent_high)
+    even, odd = prepare(gather_branches(held, rows, cols))
+    back_low = exchange(absorb(stem_low, even, odd, cosine, sine))
+    back_high = exchange(absorb(stem_high, even, odd, cosine, sine))
+    back_low = rows_first(back_low.reshape(rows * low, parts, block, width))
+    return batch_last(back_low, back_high.reshape(rows * high, parts, block, width))
 
 
 def solution(mesh):

time: 278 us -> 252 us (0.906)
  blocking collectives: 99 us -> 0 us
  starting transfers between devices: 14.1 us -> 39.1 us
  waiting for transfers between devices: 112 us -> 134 us
  Pallas kernels: 36.8 us -> 57.9 us
  local copies, waits for them, and re-layouts: 8.49 us -> 11.5 us
    all_to_all x1 -> x0, blocking collectives: 99 us -> none  [on_device(): stem = lax.all_to_all(stem, 'row', 0, 0, tiled=True)]
    all_to_all x1 -> x4, waiting for transfers between devices: 0.01 us -> 79.2 us  [exchange(): return lax.all_to_all(parts, 'row', 0, 0, tiled=True)]
    ppermute x8 -> x12, waiting for transfers between devices: 112 us -> 54.3 us  [swap(): return lax.ppermute(array, axis, [(i, i ^ bit) for i in range(size)])]
    all_to_all x1 -> x4, starting transfers between devices: 6.69 us -> 23.8 us  [exchange(): return lax.all_to_all(parts, 'row', 0, 0, tiled=True)]
    pallas_call x2 -> x5, Pallas kernels: 31.3 us -> 46.6 us  [the longest x2 32.7 us: absorb(): pl.pallas_call(absorb_kernel, grid=(items,), in_specs=[spec, whole, whole...]
    ppermute x8 -> x12, starting transfers between devices: 7.37 us -> 15.3 us  [swap(): return lax.ppermute(array, axis, [(i, i ^ bit) for i in range(size)])]
    pallas_call x1, Pallas kernels: 3.41 us -> 6.57 us  [batch_last(): pl.pallas_call(batch_last_kernel, grid=(parts, rows // 8), in_specs=[pl.B...]
    unnamed x10 -> x20, local copies, waits for them, and re-layouts: 3.75 us -> 5.98 us
  transfers between devices with their start and end apart: 9 -> 16, of which waited for: 7 -> 12; matrix products, arithmetic and copies ran while one was open for 4% -> 4% of each run, Pallas kernels for 1% -> 19%
where the time goes in v2:
time: 252 us; the launch traced here: 251 us
  waiting for transfers between devices  134 us (53%)
  Pallas kernels  57.9 us (23%)
  starting transfers between devices  39.1 us (16%)
  local copies, waits for them, and re-layouts  11.5 us (5%)
  other arithmetic  7.12 us (3%)
    all_to_all x4, waiting for transfers between devices, exchange(): return lax.all_to_all(parts, 'row', 0, 0, tiled=True)  79.2 us
    ppermute x12, waiting for transfers between devices, swap(): return lax.ppermute(array, axis, [(i, i ^ bit) for i in range(size)])  54.3 us
    pallas_call x2, Pallas kernels, absorb(): pl.pallas_call(absorb_kernel, grid=(items,), in_specs=[spec, whole, whole...  32.7 us
    all_to_all x4, starting transfers between devices, exchange(): return lax.all_to_all(parts, 'row', 0, 0, tiled=True)  23.8 us
    ppermute x12, starting transfers between devices, swap(): return lax.ppermute(array, axis, [(i, i ^ bit) for i in range(size)])  15.3 us
    pallas_call x2, Pallas kernels, batch_first(): pl.pallas_call(partial(batch_first_kernel, start), grid=(parts, rows // 8...  10.4 us
    pallas_call x1, Pallas kernels, batch_last(): pl.pallas_call(batch_last_kernel, grid=(parts, rows // 8), in_specs=[pl.B...  6.57 us
    unnamed x20, local copies, waits for them, and re-layouts  5.98 us
  transfers between devices with their start and end apart: 16, of which 12 were waited for; matrix products, arithmetic and copies ran while one was open for 4% of the time, Pallas kernels for 19%

profile of v2, /device:TPU:13, one launch (start us, length us, event | category | flops | bytes accessed | tf_op | source)
XLA Modules:
  0.0 250.9 jit_solution(3889246476309462197)
XLA Ops:
  0.0 4.7 %batch_first.2 = f32[32,2,16,256]{3,2,1,0:T(8,128)} custom-call(f32[2,16,256,128]{3,2,1,0:T(8,128)} %stem_ref.3), custom_call_target="tpu_custom_call" | custom-call | bytes 8388608 | tf_op jit(solution)/shard_map/batch_first/pallas_call | solution.py:167
  7.6 2.4 collective-permute-done
  10.0 1.4 dynamic-slice_add_fusion
  11.8 6.6 %all-to-all-start = ((f32[16,2,2,16,256]{4,3,2,1,0:T(8,128)}), f32[16,2,2,16,256]{4,3,2,1,0:T(8,128)S(1)}, u32[]{:S(2)}, u32[]{:S(2)}) async-start(f32[16,2,2,16,256]{4,3,2,1,0:T(8,128)} %bitcast), calls=%async_computation | async-start | bytes 2097152 | tf_op jit(solution)/shard_map/all_to_all | solution.py:224
  18.4 1.3 collective-permute-start.1
  20.4 5.6 %collective-permute-done.1 = f32[256,256]{1,0:T(8,128)S(1)} collective-permute-done((f32[256,256]{1,0:T(8,128)S(1)}, f32[256,256]{1,0:T(8,128)S(1)}, u32[]{:S(2)}, u32[]{:S(2)}) %collective-permute-start.1) | collective-permute-done | bytes 262176 | tf_op jit(solution)/shard_map/ppermute | solution.py:27
  26.4 2.4 collective-permute-done.4
  28.8 3.1 %collective-permute-done.2 = f32[128,256]{1,0:T(8,128)S(1)} collective-permute-done((f32[128,256]{1,0:T(8,128)S(1)}, f32[128,256]{1,0:T(8,128)S(1)}, u32[]{:S(2)}, u32[]{:S(2)}) %collective-permute-start.2) | collective-permute-done | bytes 131104 | tf_op jit(solution)/shard_map/ppermute | solution.py:27
  33.0 5.7 %batch_first.3 = f32[96,2,16,256]{3,2,1,0:T(8,128)} custom-call(f32[2,16,256,128]{3,2,1,0:T(8,128)} %stem_ref.3), custom_call_target="tpu_custom_call" | custom-call | bytes 8388608 | tf_op jit(solution)/shard_map/batch_first/pallas_call | solution.py:167
  38.7 3.0 %collective-permute-done.5 = f32[256,256]{1,0:T(8,128)S(1)} collective-permute-done((f32[256,256]{1,0:T(8,128)S(1)}, f32[256,256]{1,0:T(8,128)S(1)}, u32[]{:S(2)}, u32[]{:S(2)}) %collective-permute-start.5) | collective-permute-done | bytes 262176 | tf_op jit(solution)/shard_map/ppermute | solution.py:27
  41.8 3.9 %collective-permute-start.6 = (f32[256,256]{1,0:T(8,128)S(1)}, f32[256,256]{1,0:T(8,128)S(1)}, u32[]{:S(2)}, u32[]{:S(2)}) collective-permute-start(f32[256,256]{1,0:T(8,128)S(1)} %fusion.4), channel_id=1, source_target_pairs={{0,16},{2,18},{4,20},{6,22},{8,24},{10,26},{12,28},{14,30},{16,0},... | collective-permute-start | bytes 786440 | tf_op jit(solution)/shard_map/ppermute | solution.py:27
  45.7 4.5 %fusion.5 = (f32[4,256,256]{2,1,0:T(8,128)}, f32[4,256,256]{2,1,0:T(8,128)}) fusion(f32[4,256,256]{2,1,0:T(8,128)S(1)} %copy-done.7), kind=kLoop, calls=%fused_computation.39 | loop fusion | bytes 3145728 | tf_op jit(solution)/shard_map/sin | solution.py:236
  50.2 6.8 %collective-permute-done.6 = f32[256,256]{1,0:T(8,128)S(1)} collective-permute-done((f32[256,256]{1,0:T(8,128)S(1)}, f32[256,256]{1,0:T(8,128)S(1)}, u32[]{:S(2)}, u32[]{:S(2)}) %collective-permute-start.6) | collective-permute-done | bytes 262176 | tf_op jit(solution)/shard_map/ppermute | solution.py:27
  58.0 7.4 %all-to-all-start.2 = ((f32[16,6,2,16,256]{4,3,2,1,0:T(8,128)}), f32[16,6,2,16,256]{4,3,2,1,0:T(8,128)S(1)}, u32[]{:S(2)}, u32[]{:S(2)}) async-start(f32[16,6,2,16,256]{4,3,2,1,0:T(8,128)} %bitcast.9), calls=%async_computation.2 | async-start | bytes 6291456 | tf_op jit(solution)/shard_map/all_to_all | solution.py:224
  67.6 18.6 %collective-permute-done.7 = f32[128,256]{1,0:T(8,128)S(1)} collective-permute-done((f32[128,256]{1,0:T(8,128)}, f32[128,256]{1,0:T(8,128)S(1)}, u32[]{:S(2)}, u32[]{:S(2)}) %collective-permute-start.7) | collective-permute-done | bytes 131104 | tf_op jit(solution)/shard_map/ppermute | solution.py:27
  88.6 9.8 %collective-permute-done.10 = f32[256,256]{1,0:T(8,128)S(1)} collective-permute-done((f32[256,256]{1,0:T(8,128)S(1)}, f32[256,256]{1,0:T(8,128)S(1)}, u32[]{:S(2)}, u32[]{:S(2)}) %collective-permute-start.10) | collective-permute-done | bytes 262176 | tf_op jit(solution)/shard_map/ppermute | solution.py:27
  100.2 4.2 %collective-permute-start.11 = (f32[1024,256]{1,0:T(8,128)}, f32[1024,256]{1,0:T(8,128)}, u32[]{:S(2)}, u32[]{:S(2)}) collective-permute-start(f32[1024,256]{1,0:T(8,128)} %pad_maximum_fusion.1), channel_id=1, source_target_pairs={{0,2},{2,0},{4,6},{6,4},{8,10},{10,8},{12,14},{14,12},{16,18},{18,... | collective-permute-start | bytes 3145736 | tf_op jit(solution)/shard_map/ppermute | solution.py:27
  104.3 2.6 %collective-permute-done.11 = f32[1024,256]{1,0:T(8,128)} collective-permute-done((f32[1024,256]{1,0:T(8,128)}, f32[1024,256]{1,0:T(8,128)}, u32[]{:S(2)}, u32[]{:S(2)}) %collective-permute-start.11) | collective-permute-done | bytes 1048608 | tf_op jit(solution)/shard_map/ppermute | solution.py:27
  107.0 1.6 broadcast_select_fusion.1
  108.5 1.5 pad_maximum_fusion
  110.1 4.7 %prepare.1 = (bf16[2,1536,512]{2,1,0:T(8,128)(2,1)}, bf16[2,512,1536]{2,1,0:T(8,128)(2,1)}) custom-call(f32[4,2,256,256]{3,2,1,0:T(8,128)} %bitcast.29), custom_call_target="tpu_custom_call" | custom-call | tf_op jit(solution)/shard_map/prepare/pallas_call | solution.py:109
  114.8 10.3 %absorb.2 = f32[16,2,2,16,256]{4,3,2,1,0:T(8,128)} custom-call(f32[16,2,2,16,256]{4,3,2,1,0:T(8,128)} %copy-done.8, bf16[2,1536,512]{2,1,0:T(8,128)(2,1)} %get-tuple-element.16.even_ref, bf16[2,512,1536]{2,1,0:T(8,128)(2,1)} %get-tuple-element.17.odd_ref, f32[4,256,256]{2,1,0:T(8,128)} %get-tuple-element.18.cos_ref, f32[4,256,256]{2,1,0:T(8,128)} %get-tuple-element.19.sin_ref), custom_call_target="tpu_custom_call" | custom-call | flops 3221225472 | bytes 2097152 | tf_op jit(solution)/shard_map/absorb/pallas_call | solution.py:147
  125.1 10.3 %all-to-all-done.2.stem_ref = f32[16,6,2,16,256]{4,3,2,1,0:T(8,128)S(1)} async-done(((f32[16,6,2,16,256]{4,3,2,1,0:T(8,128)}), f32[16,6,2,16,256]{4,3,2,1,0:T(8,128)S(1)}, u32[]{:S(2)}, u32[]{:S(2)}) %all-to-all-start.2) | async-done | bytes 3145760 | tf_op jit(solution)/shard_map/all_to_all | solution.py:224
  135.4 1.7 copy-done.3
  137.1 4.9 %all-to-all-start.1 = ((f32[16,2,2,16,256]{4,3,2,1,0:T(8,128)}), f32[16,2,2,16,256]{4,3,2,1,0:T(8,128)S(1)}, u32[]{:S(2)}, u32[]{:S(2)}) async-start(f32[16,2,2,16,256]{4,3,2,1,0:T(8,128)} %absorb.2), calls=%async_computation.1 | async-start | bytes 2097152 | tf_op jit(solution)/shard_map/all_to_all | solution.py:224
  142.0 22.4 %absorb.3 = f32[16,6,2,16,256]{4,3,2,1,0:T(8,128)} custom-call(f32[16,6,2,16,256]{4,3,2,1,0:T(8,128)} %copy-done.3, bf16[2,1536,512]{2,1,0:T(8,128)(2,1)} %get-tuple-element.16.even_ref, bf16[2,512,1536]{2,1,0:T(8,128)(2,1)} %get-tuple-element.17.odd_ref, f32[4,256,256]{2,1,0:T(8,128)} %get-tuple-element.18.cos_ref, f32[4,256,256]{2,1,0:T(8,128)} %get-tuple-element.19.sin_ref), custom_call_target="tpu_custom_call" | custom-call | flops 9663676416 | bytes 6291456 | tf_op jit(solution)/shard_map/absorb/pallas_call | solution.py:147
  164.3 2.5 %all-to-all-done.1 = f32[16,2,2,16,256]{4,3,2,1,0:T(8,128)S(1)} async-done(((f32[16,2,2,16,256]{4,3,2,1,0:T(8,128)}), f32[16,2,2,16,256]{4,3,2,1,0:T(8,128)S(1)}, u32[]{:S(2)}, u32[]{:S(2)}) %all-to-all-start.1) | async-done | bytes 1048608 | tf_op jit(solution)/shard_map/all_to_all | solution.py:224
  167.8 4.9 %all-to-all-start.3 = ((f32[16,6,2,16,256]{4,3,2,1,0:T(8,128)}), f32[16,6,2,16,256]{4,3,2,1,0:T(8,128)S(1)}, u32[]{:S(2)}, u32[]{:S(2)}) async-start(f32[16,6,2,16,256]{4,3,2,1,0:T(8,128)} %absorb.3), calls=%async_computation.3 | async-start | bytes 6291456 | tf_op jit(solution)/shard_map/all_to_all | solution.py:224
  172.8 3.5 %rows_first.1.low_ref = f32[2,16,32,256]{3,2,1,0:T(8,128)} custom-call(f32[32,2,16,256]{3,2,1,0:T(8,128)} %bitcast.34), custom_call_target="tpu_custom_call" | custom-call | bytes 2097152 | tf_op jit(solution)/shard_map/rows_first/pallas_call | solution.py:186
  176.3 66.4 %all-to-all-done.3 = f32[16,6,2,16,256]{4,3,2,1,0:T(8,128)S(1)} async-done(((f32[16,6,2,16,256]{4,3,2,1,0:T(8,128)}), f32[16,6,2,16,256]{4,3,2,1,0:T(8,128)S(1)}, u32[]{:S(2)}, u32[]{:S(2)}) %all-to-all-start.3) | async-done | bytes 3145760 | tf_op jit(solution)/shard_map/all_to_all | solution.py:224
  242.7 1.6 copy-done
  244.3 6.6 %batch_last.1 = f32[2,16,256,128]{3,2,1,0:T(8,128)} custom-call(f32[2,16,32,256]{3,2,1,0:T(8,128)} %rows_first.1.low_ref, f32[96,2,16,256]{3,2,1,0:T(8,128)} %bitcast.28), custom_call_target="tpu_custom_call" | custom-call | tf_op jit(solution)/shard_map/batch_last/pallas_call | solution.py:209
  (60 shorter events, 13.8 us)
Async XLA Ops:
  0.0 4.7 %copy-start.1 = (f32[1,2,2,256,256]{4,3,2,1,0:T(8,128)S(1)}, f32[1,2,2,256,256]{4,3,2,1,0:T(8,128)}, u32[]{:S(2)}) copy-start(f32[1,2,2,256,256]{4,3,2,1,0:T(8,128)} %param.5) | copy-start | bytes 3145732
  0.0 5.5 %copy-start.9 = (s32[4]{0:T(128)S(1)}, s32[4]{0:T(128)}, u32[]{:S(2)}) copy-start(s32[4]{0:T(128)} %param.6) | copy-start | bytes 52
  6.8 3.2 %collective-permute-start = (f32[1024,256]{1,0:T(8,128)S(1)}, f32[1024,256]{1,0:T(8,128)}, u32[]{:S(2)}, u32[]{:S(2)}) collective-permute-start(f32[1024,256]{1,0:T(8,128)S(1)} %constant_dynamic-slice_fusion.4), channel_id=1, source_target_pairs={{0,2},{2,0},{4,6},{6,4},{8,10},{10,8},{12,14},{14,12},{16,18},{18,... | collective-permute-start | bytes 3145736 | tf_op jit(solution)/shard_map/ppermute | solution.py:27
  11.5 8.2 %collective-permute-start.3 = (f32[256,256]{1,0:T(8,128)S(1)}, f32[256,256]{1,0:T(8,128)S(1)}, u32[]{:S(2)}, u32[]{:S(2)}) collective-permute-start(f32[256,256]{1,0:T(8,128)S(1)} %constant_dynamic-slice_fusion.1), channel_id=1, source_target_pairs={{0,4},{2,6},{4,0},{6,2},{8,12},{10,14},{12,8},{14,10},{16,20},{18,... | collective-permute-start | bytes 786440 | tf_op jit(solution)/shard_map/ppermute | solution.py:27
  11.8 45.2 %all-to-all-start = ((f32[16,2,2,16,256]{4,3,2,1,0:T(8,128)}), f32[16,2,2,16,256]{4,3,2,1,0:T(8,128)S(1)}, u32[]{:S(2)}, u32[]{:S(2)}) async-start(f32[16,2,2,16,256]{4,3,2,1,0:T(8,128)} %bitcast), calls=%async_computation | async-start | bytes 2097152 | tf_op jit(solution)/shard_map/all_to_all | solution.py:224
  18.4 7.6 %collective-permute-start.1 = (f32[256,256]{1,0:T(8,128)S(1)}, f32[256,256]{1,0:T(8,128)S(1)}, u32[]{:S(2)}, u32[]{:S(2)}) collective-permute-start(f32[256,256]{1,0:T(8,128)S(1)} %constant_dynamic-slice_fusion.3), channel_id=1, source_target_pairs={{0,1},{1,0},{2,3},{3,2},{4,5},{5,4},{6,7},{7,6},{8,9},{9,8},{10,11... | collective-permute-start | bytes 786440 | tf_op jit(solution)/shard_map/ppermute | solution.py:27
  19.7 9.1 %collective-permute-start.4 = (f32[128,256]{1,0:T(8,128)S(1)}, f32[128,256]{1,0:T(8,128)S(1)}, u32[]{:S(2)}, u32[]{:S(2)}) collective-permute-start(f32[128,256]{1,0:T(8,128)S(1)} %constant_dynamic-slice_fusion), channel_id=1, source_target_pairs={{0,1},{1,0},{2,3},{3,2},{4,5},{5,4},{6,7},{7,6},{8,9},{9,8},{10,11... | collective-permute-start | bytes 393224 | tf_op jit(solution)/shard_map/ppermute | solution.py:27
  26.0 5.8 %collective-permute-start.2 = (f32[128,256]{1,0:T(8,128)S(1)}, f32[128,256]{1,0:T(8,128)S(1)}, u32[]{:S(2)}, u32[]{:S(2)}) collective-permute-start(f32[128,256]{1,0:T(8,128)S(1)} %constant_dynamic-slice_fusion.2), channel_id=1, source_target_pairs={{0,4},{2,6},{4,0},{6,2},{8,12},{10,14},{12,8},{14,10},{16,20},{18,... | collective-permute-start | bytes 393224 | tf_op jit(solution)/shard_map/ppermute | solution.py:27
  31.9 13.8 %copy-start.7 = (f32[4,256,256]{2,1,0:T(8,128)S(1)}, f32[4,256,256]{2,1,0:T(8,128)}, u32[]{:S(2)}) copy-start(f32[4,256,256]{2,1,0:T(8,128)} %param.7) | copy-start | bytes 3145732
  31.9 9.8 %collective-permute-start.5 = (f32[256,256]{1,0:T(8,128)S(1)}, f32[256,256]{1,0:T(8,128)S(1)}, u32[]{:S(2)}, u32[]{:S(2)}) collective-permute-start(f32[256,256]{1,0:T(8,128)S(1)} %pad_maximum_fusion.3), channel_id=1, source_target_pairs={{0,8},{2,10},{4,12},{6,14},{8,0},{10,2},{12,4},{14,6},{16,24},{18,... | collective-permute-start | bytes 786440 | tf_op jit(solution)/shard_map/ppermute | solution.py:27
  41.8 15.2 %collective-permute-start.6 = (f32[256,256]{1,0:T(8,128)S(1)}, f32[256,256]{1,0:T(8,128)S(1)}, u32[]{:S(2)}, u32[]{:S(2)}) collective-permute-start(f32[256,256]{1,0:T(8,128)S(1)} %fusion.4), channel_id=1, source_target_pairs={{0,16},{2,18},{4,20},{6,22},{8,24},{10,26},{12,28},{14,30},{16,0},... | collective-permute-start | bytes 786440 | tf_op jit(solution)/shard_map/ppermute | solution.py:27
  57.0 1.0 copy-start.8
  58.0 77.4 %all-to-all-start.2 = ((f32[16,6,2,16,256]{4,3,2,1,0:T(8,128)}), f32[16,6,2,16,256]{4,3,2,1,0:T(8,128)S(1)}, u32[]{:S(2)}, u32[]{:S(2)}) async-start(f32[16,6,2,16,256]{4,3,2,1,0:T(8,128)} %bitcast.9), calls=%async_computation.2 | async-start | bytes 6291456 | tf_op jit(solution)/shard_map/all_to_all | solution.py:224
  66.1 20.1 %collective-permute-start.7 = (f32[128,256]{1,0:T(8,128)}, f32[128,256]{1,0:T(8,128)S(1)}, u32[]{:S(2)}, u32[]{:S(2)}) collective-permute-start(f32[128,256]{1,0:T(8,128)} %get-tuple-element.37), channel_id=1, source_target_pairs={{0,4},{2,6},{4,0},{6,2},{8,12},{10,14},{12,8},{14,10},{16,20},{18,... | collective-permute-start | bytes 393224 | tf_op jit(solution)/shard_map/ppermute | solution.py:27
  66.4 19.8 %collective-permute-start.9 = (f32[128,256]{1,0:T(8,128)}, f32[128,256]{1,0:T(8,128)}, u32[]{:S(2)}, u32[]{:S(2)}) collective-permute-start(f32[128,256]{1,0:T(8,128)} %get-tuple-element.38), channel_id=1, source_target_pairs={{0,1},{1,0},{2,3},{3,2},{4,5},{5,4},{6,7},{7,6},{8,9},{9,8},{10,11... | collective-permute-start | bytes 393224 | tf_op jit(solution)/shard_map/ppermute | solution.py:27
  87.2 11.2 %collective-permute-start.10 = (f32[256,256]{1,0:T(8,128)S(1)}, f32[256,256]{1,0:T(8,128)S(1)}, u32[]{:S(2)}, u32[]{:S(2)}) collective-permute-start(f32[256,256]{1,0:T(8,128)S(1)} %pad_maximum_fusion.5), channel_id=1, source_target_pairs={{0,4},{2,6},{4,0},{6,2},{8,12},{10,14},{12,8},{14,10},{16,20},{18,... | collective-permute-start | bytes 786440 | tf_op jit(solution)/shard_map/ppermute | solution.py:27
  87.3 11.1 %collective-permute-start.8 = (f32[256,256]{1,0:T(8,128)S(1)}, f32[256,256]{1,0:T(8,128)S(1)}, u32[]{:S(2)}, u32[]{:S(2)}) collective-permute-start(f32[256,256]{1,0:T(8,128)S(1)} %pad_maximum_fusion.4), channel_id=1, source_target_pairs={{0,1},{1,0},{2,3},{3,2},{4,5},{5,4},{6,7},{7,6},{8,9},{9,8},{10,11... | collective-permute-start | bytes 786440 | tf_op jit(solution)/shard_map/ppermute | solution.py:27
  98.4 0.7 copy-start.4
  98.5 1.7 copy-start.5
  98.5 1.7 copy-start.6
  100.2 6.8 %collective-permute-start.11 = (f32[1024,256]{1,0:T(8,128)}, f32[1024,256]{1,0:T(8,128)}, u32[]{:S(2)}, u32[]{:S(2)}) collective-permute-start(f32[1024,256]{1,0:T(8,128)} %pad_maximum_fusion.1), channel_id=1, source_target_pairs={{0,2},{2,0},{4,6},{6,4},{8,10},{10,8},{12,14},{14,12},{16,18},{18,... | collective-permute-start | bytes 3145736 | tf_op jit(solution)/shard_map/ppermute | solution.py:27
  135.4 1.7 copy-start.3
  137.1 29.7 %all-to-all-start.1 = ((f32[16,2,2,16,256]{4,3,2,1,0:T(8,128)}), f32[16,2,2,16,256]{4,3,2,1,0:T(8,128)S(1)}, u32[]{:S(2)}, u32[]{:S(2)}) async-start(f32[16,2,2,16,256]{4,3,2,1,0:T(8,128)} %absorb.2), calls=%async_computation.1 | async-start | bytes 2097152 | tf_op jit(solution)/shard_map/all_to_all | solution.py:224
  166.9 1.0 copy-start.2
  167.8 74.8 %all-to-all-start.3 = ((f32[16,6,2,16,256]{4,3,2,1,0:T(8,128)}), f32[16,6,2,16,256]{4,3,2,1,0:T(8,128)S(1)}, u32[]{:S(2)}, u32[]{:S(2)}) async-start(f32[16,6,2,16,256]{4,3,2,1,0:T(8,128)} %absorb.3), calls=%async_computation.3 | async-start | bytes 6291456 | tf_op jit(solution)/shard_map/all_to_all | solution.py:224
  242.7 1.6 copy-start

commit v3 on v2

--- a/solution.py
+++ b/solution.py
@@ -87,7 +87,7 @@
     return high, low
 
 
-def prepare_kernel(branch_ref, even_ref, odd_ref):
+def stack_branches(branch_ref, even_ref, odd_ref):
     for step in range(STEPS):
         real, imag = branch_ref[step, 0], branch_ref[step, 1]
         if step % 2:
@@ -103,22 +103,13 @@
             even_ref[step // 2] = out
 
 
-def prepare(branches):
-    width = branches.shape[-1]
-    pairs = STEPS // 2
-    return pl.pallas_call(
-        prepare_kernel,
-        out_shape=(
-            jax.ShapeDtypeStruct((pairs, 6 * width, 2 * width), jnp.bfloat16),
-            jax.ShapeDtypeStruct((pairs, 2 * width, 6 * width), jnp.bfloat16),
-        ),
-        compiler_params=pltpu.CompilerParams(vmem_limit_bytes=60 * MIB),
-        name="prepare",
-    )(branches)
-
-
-def absorb_kernel(stem_ref, even_ref, odd_ref, cos_ref, sin_ref, out_ref):
+def absorb_kernel(stem_ref, branch_ref, cos_ref, sin_ref, out_ref, even_ref, odd_ref):
     width = cos_ref.shape[1]
+
+    @pl.when(pl.program_id(0) == 0)
+    def _():
+        stack_branches(branch_ref, even_ref, odd_ref)
+
     for item in range(stem_ref.shape[1]):
         real = stem_ref[:, item, 0].reshape(width, width)
         imag = stem_ref[:, item, 1].reshape(width, width)
@@ -139,41 +130,75 @@
         out_ref[:, item, 1] = imag.reshape(shape)
 
 
-def absorb(stem, even, odd, cosine, sine):
+def in_hbm(*arrays):
+    return [pltpu.with_memory_space_constraint(array, pltpu.HBM) for array in arrays]
+
+
+def whole(array):
+    return pl.BlockSpec(array.shape, lambda i: (0,) * array.ndim, pipeline_mode=pl.Buffered(1))
+
+
+def absorb(stem, branches, cosine, sine):
     peers, items, _, block, width = stem.shape
-    spec = pl.BlockSpec((peers, 1, 2, block, width), lambda i: (0, i, 0, 0, 0))
-    whole = pl.BlockSpec(memory_space=pltpu.VMEM)
+    per = 2 if items % 2 == 0 else 1
+    spec = pl.BlockSpec((peers, per, 2, block, width), lambda i: (0, i, 0, 0, 0))
     flops = items * STEPS * 12 * 2 * width**3
     return pl.pallas_call(
         absorb_kernel,
-        grid=(items,),
-        in_specs=[spec, whole, whole, whole, whole],
+        grid=(items // per,),
+        in_specs=[spec, whole(branches), whole(cosine), whole(sine)],
         out_specs=spec,
-        out_shape=jax.ShapeDtypeStruct(stem.shape, jnp.float32),
+        out_shape=pltpu.HBM(stem.shape, jnp.float32),
+        scratch_shapes=[
+            pltpu.VMEM((STEPS // 2, 6 * width, 2 * width), jnp.bfloat16),
+            pltpu.VMEM((STEPS // 2, 2 * width, 6 * width), jnp.bfloat16),
+        ],
         cost_estimate=pl.CostEstimate(flops=flops, bytes_accessed=8 * stem.size, transcendentals=0),
-        compiler_params=pltpu.CompilerParams(vmem_limit_bytes=60 * MIB),
+        compiler_params=pltpu.CompilerParams(vmem_limit_bytes=32 * MIB),
         name="absorb",
-    )(stem, even, odd, cosine, sine)
-
-
-def batch_first_kernel(start, stem_ref, out_ref):
+    )(*in_hbm(stem, branches, cosine, sine))
+
+
+def row_groups(parts, rows):
+    return [(part, row) for part in range(parts) for row in range(0, rows, 8)]
+
+
+def batch_first_kernel(start, stem_ref, out_ref, held, made, in_sem, out_sem):
+    parts, rows = stem_ref.shape[:2]
     batch = out_ref.shape[0]
-    for i in range(stem_ref.shape[1]):
-        out_ref[:, 0, i, :] = stem_ref[0, i][:, start : start + batch].T
+    ins, outs = [], []
+    for g, (part, row) in enumerate(row_groups(parts, rows)):
+        ins.append(pltpu.make_async_copy(stem_ref.at[part, pl.ds(row, 8)], held.at[g], in_sem.at[g]))
+        outs.append(pltpu.make_async_copy(made.at[g], out_ref.at[:, part, pl.ds(row, 8), :], out_sem.at[g]))
+    for copy in ins:
+        copy.start()
+    for g, copy in enumerate(ins):
+        copy.wait()
+        for i in range(8):
+            made[g, :, i, :] = held[g, i][:, start : start + batch].T
+        outs[g].start()
+    for copy in outs:
+        copy.wait()
 
 
 def batch_first(stem, start, batch):
     parts, rows, width, lanes = stem.shape
+    groups = parts * rows // 8
     return pl.pallas_call(
         partial(batch_first_kernel, start),
-        grid=(parts, rows // 8),
-        in_specs=[pl.BlockSpec((1, 8, width, lanes), lambda p, r: (p, r, 0, 0))],
-        out_specs=pl.BlockSpec((batch, 1, 8, width), lambda p, r: (0, p, r, 0)),
-        out_shape=jax.ShapeDtypeStruct((batch, parts, rows, width), jnp.float32),
+        in_specs=[pl.BlockSpec(memory_space=pl.ANY)],
+        out_specs=pl.BlockSpec(memory_space=pl.ANY),
+        out_shape=pltpu.HBM((batch, parts, rows, width), jnp.float32),
+        scratch_shapes=[
+            pltpu.VMEM((groups, 8, width, lanes), jnp.float32),
+            pltpu.VMEM((groups, batch, 8, width), jnp.float32),
+            pltpu.SemaphoreType.DMA((groups,)),
+            pltpu.SemaphoreType.DMA((groups,)),
+        ],
         cost_estimate=pl.CostEstimate(flops=0, bytes_accessed=8 * stem.size, transcendentals=0),
-        compiler_params=pltpu.CompilerParams(vmem_limit_bytes=60 * MIB),
+        compiler_params=pltpu.CompilerParams(vmem_limit_bytes=24 * MIB),
         name="batch_first",
-    )(stem)
+    )(*in_hbm(stem))
 
 
 def rows_first_kernel(stem_ref, out_ref):
@@ -188,36 +213,49 @@
         grid=(parts, rows // 8),
         in_specs=[pl.BlockSpec((batch, 1, 8, width), lambda p, r: (0, p, r, 0))],
         out_specs=pl.BlockSpec((1, 8, batch, width), lambda p, r: (p, r, 0, 0)),
-        out_shape=jax.ShapeDtypeStruct((parts, rows, batch, width), jnp.float32),
+        out_shape=pltpu.HBM((parts, rows, batch, width), jnp.float32),
         cost_estimate=pl.CostEstimate(flops=0, bytes_accessed=8 * stem.size, transcendentals=0),
-        compiler_params=pltpu.CompilerParams(vmem_limit_bytes=60 * MIB),
+        compiler_params=pltpu.CompilerParams(vmem_limit_bytes=24 * MIB),
         name="rows_first",
-    )(stem)
-
-
-def batch_last_kernel(low_ref, high_ref, out_ref):
-    low = low_ref.shape[2]
-    for i in range(out_ref.shape[1]):
-        out_ref[0, i, :, :low] = low_ref[0, i].T
-        out_ref[0, i, :, low:] = high_ref[:, 0, i, :].T
+    )(*in_hbm(stem))
+
+
+def batch_last_kernel(low_ref, high_ref, out_ref, low, made, low_sem, out_sem):
+    parts, rows = out_ref.shape[:2]
+    ins, outs = [], []
+    for g, (part, row) in enumerate(row_groups(parts, rows)):
+        ins.append(pltpu.make_async_copy(low_ref.at[part, pl.ds(row, 8)], low.at[g], low_sem.at[g]))
+        outs.append(pltpu.make_async_copy(made.at[g], out_ref.at[part, pl.ds(row, 8)], out_sem.at[g]))
+    for copy in ins:
+        copy.start()
+    for g, (part, row) in enumerate(row_groups(parts, rows)):
+        ins[g].wait()
+        for i in range(8):
+            made[g, i] = jnp.concatenate([low[g, i], high_ref[:, part, row + i, :]], 0).T
+        outs[g].start()
+    for copy in outs:
+        copy.wait()
 
 
 def batch_last(low, high):
     parts, rows, low_batch, width = low.shape
     high_batch = high.shape[0]
     batch = low_batch + high_batch
+    groups = parts * rows // 8
     return pl.pallas_call(
         batch_last_kernel,
-        grid=(parts, rows // 8),
-        in_specs=[
-            pl.BlockSpec((1, 8, low_batch, width), lambda p, r: (p, r, 0, 0)),
-            pl.BlockSpec((high_batch, 1, 8, width), lambda p, r: (0, p, r, 0)),
+        in_specs=[pl.BlockSpec(memory_space=pl.ANY), pl.BlockSpec(memory_space=pltpu.VMEM)],
+        out_specs=pl.BlockSpec(memory_space=pl.ANY),
+        out_shape=jax.ShapeDtypeStruct((parts, rows, width, batch), jnp.float32),
+        scratch_shapes=[
+            pltpu.VMEM((groups, 8, low_batch, width), jnp.float32),
+            pltpu.VMEM((groups, 8, width, batch), jnp.float32),
+            pltpu.SemaphoreType.DMA((groups,)),
+            pltpu.SemaphoreType.DMA((groups,)),
         ],
-        out_specs=pl.BlockSpec((1, 8, width, batch), lambda p, r: (p, r, 0, 0)),
-        out_shape=jax.ShapeDtypeStruct((parts, rows, width, batch), jnp.float32),
-        compiler_params=pltpu.CompilerParams(vmem_limit_bytes=60 * MIB),
+        compiler_params=pltpu.CompilerParams(vmem_limit_bytes=24 * MIB),
         name="batch_last",
-    )(low, high)
+    )(*in_hbm(low), high)
 
 
 def exchange(parts):
@@ -227,7 +265,7 @@
 def on_device(stem_slab, factors, branch_owner, entangle_phase, *, rows, cols):
     parts, block, width, batch = stem_slab.shape
     items = batch // rows
-    low = max(1, items // 4)
+    low = max(1, items * 3 // 8)
     high = items - low
     sent_low = batch_first(stem_slab, 0, rows * low).reshape(rows, low, parts, block, width)
     sent_low, factors = lax.optimization_barrier((sent_low, factors))
@@ -239,9 +277,9 @@
     sent_high = batch_first(stem_slab, rows * low, rows * high).reshape(rows, high, parts, block, width)
     held, sent_high, cosine, sine = lax.optimization_barrier((held, sent_high, cosine, sine))
     stem_high = exchange(sent_high)
-    even, odd = prepare(gather_branches(held, rows, cols))
-    back_low = exchange(absorb(stem_low, even, odd, cosine, sine))
-    back_high = exchange(absorb(stem_high, even, odd, cosine, sine))
+    branches = gather_branches(held, rows, cols)
+    back_low = exchange(absorb(stem_low, branches, cosine, sine))
+    back_high = exchange(absorb(stem_high, branches, cosine, sine))
     back_low = rows_first(back_low.reshape(rows * low, parts, block, width))
     return batch_last(back_low, back_high.reshape(rows * high, parts, block, width))
 

time: 252 us -> 240 us (0.952)
  Pallas kernels: 57.9 us -> 47.3 us
  waiting for transfers between devices: 134 us -> 140 us
  local copies, waits for them, and re-layouts: 11.5 us -> 8.15 us
  starting transfers between devices: 39.1 us -> 36 us
    pallas_call x6 -> x5, Pallas kernels: 54.4 us -> 43.6 us  [the longest x2 31.9 us: absorb(): pl.pallas_call(absorb_kernel, grid=(items // per,), in_specs=[spec, whole...]
    ppermute x12, waiting for transfers between devices: 54.3 us -> 62 us  [swap(): return lax.ppermute(array, axis, [(i, i ^ bit) for i in range(size)])]
    unnamed x20 -> x12, local copies, waits for them, and re-layouts: 5.98 us -> 3.33 us
  transfers between devices with their start and end apart: 16 -> 16, of which waited for: 12 -> 11; matrix products, arithmetic and copies ran while one was open for 4% -> 4% of each run, Pallas kernels for 19% -> 17%
where the time goes in v3:
time: 240 us
  waiting for transfers between devices  140 us (58%)
  Pallas kernels  47.3 us (20%)
  starting transfers between devices  36 us (15%)
  local copies, waits for them, and re-layouts  8.15 us (3%)
  other arithmetic  6.05 us (3%)
    all_to_all x4, waiting for transfers between devices, exchange(): return lax.all_to_all(parts, 'row', 0, 0, tiled=True)  78.2 us
    ppermute x12, waiting for transfers between devices, swap(): return lax.ppermute(array, axis, [(i, i ^ bit) for i in range(size)])  62 us
    pallas_call x2, Pallas kernels, absorb(): pl.pallas_call(absorb_kernel, grid=(items // per,), in_specs=[spec, whole...  31.9 us
    all_to_all x4, starting transfers between devices, exchange(): return lax.all_to_all(parts, 'row', 0, 0, tiled=True)  23 us
    ppermute x12, starting transfers between devices, swap(): return lax.ppermute(array, axis, [(i, i ^ bit) for i in range(size)])  12.9 us
    pallas_call x2, Pallas kernels, batch_first(): pl.pallas_call(partial(batch_first_kernel, start), in_specs=[pl.BlockSpec...  8.18 us
  transfers between devices with their start and end apart: 16, of which 11 were waited for; matrix products, arithmetic and copies ran while one was open for 4% of the time, Pallas kernels for 17%

profile of v3, /device:TPU:13, one launch (start us, length us, event | category | flops | bytes accessed | tf_op | source)
XLA Modules:
  0.0 239.7 jit_solution(4095743867180771764)
XLA Ops:
  0.0 3.5 %batch_first.2 = f32[48,2,16,256]{3,2,1,0:T(8,128)} custom-call(f32[2,16,256,128]{3,2,1,0:T(8,128)} %stem_ref.3), custom_call_target="tpu_custom_call" | custom-call | bytes 8388608 | tf_op jit(solution)/shard_map/batch_first/pallas_call | solution.py:187
  6.4 6.0 %all-to-all-start = ((f32[16,3,2,16,256]{4,3,2,1,0:T(8,128)}), f32[16,3,2,16,256]{4,3,2,1,0:T(8,128)}, u32[]{:S(2)}, u32[]{:S(2)}) async-start(f32[16,3,2,16,256]{4,3,2,1,0:T(8,128)} %bitcast.30), calls=%async_computation | async-start | bytes 3145728 | tf_op jit(solution)/shard_map/all_to_all | solution.py:262
  12.4 1.4 dynamic-slice_add_fusion
  14.3 1.3 collective-permute-start.1
  15.5 12.3 %collective-permute-done.3 = f32[256,256]{1,0:T(8,128)S(1)} collective-permute-done((f32[256,256]{1,0:T(8,128)S(1)}, f32[256,256]{1,0:T(8,128)S(1)}, u32[]{:S(2)}, u32[]{:S(2)}) %collective-permute-start.3) | collective-permute-done | bytes 262176 | tf_op jit(solution)/shard_map/ppermute | solution.py:27
  27.9 1.3 collective-permute-start.4
  29.2 2.3 collective-permute-start.2
  32.2 2.3 collective-permute-done.2
  34.5 3.7 %collective-permute-start.5 = (f32[256,256]{1,0:T(8,128)S(1)}, f32[256,256]{1,0:T(8,128)S(1)}, u32[]{:S(2)}, u32[]{:S(2)}) collective-permute-start(f32[256,256]{1,0:T(8,128)S(1)} %pad_maximum_fusion.3), channel_id=1, source_target_pairs={{0,8},{2,10},{4,12},{6,14},{8,0},{10,2},{12,4},{14,6},{16,24},{18,... | collective-permute-start | bytes 786440 | tf_op jit(solution)/shard_map/ppermute | solution.py:27
  38.2 4.7 %batch_first.3 = f32[80,2,16,256]{3,2,1,0:T(8,128)} custom-call(f32[2,16,256,128]{3,2,1,0:T(8,128)} %stem_ref.3), custom_call_target="tpu_custom_call" | custom-call | bytes 8388608 | tf_op jit(solution)/shard_map/batch_first/pallas_call | solution.py:187
  42.9 6.3 %collective-permute-done.5 = f32[256,256]{1,0:T(8,128)S(1)} collective-permute-done((f32[256,256]{1,0:T(8,128)S(1)}, f32[256,256]{1,0:T(8,128)S(1)}, u32[]{:S(2)}, u32[]{:S(2)}) %collective-permute-start.5) | collective-permute-done | bytes 262176 | tf_op jit(solution)/shard_map/ppermute | solution.py:27
  49.3 1.9 collective-permute-start.6
  51.2 4.5 %fusion.5 = (f32[4,256,256]{2,1,0:T(8,128)}, f32[4,256,256]{2,1,0:T(8,128)}) fusion(f32[4,256,256]{2,1,0:T(8,128)S(1)} %copy-done.4), kind=kLoop, calls=%fused_computation.39 | loop fusion | bytes 3145728 | tf_op jit(solution)/shard_map/sin | solution.py:274
  55.6 7.1 %collective-permute-done.6 = f32[256,256]{1,0:T(8,128)S(1)} collective-permute-done((f32[256,256]{1,0:T(8,128)S(1)}, f32[256,256]{1,0:T(8,128)S(1)}, u32[]{:S(2)}, u32[]{:S(2)}) %collective-permute-start.6) | collective-permute-done | bytes 262176 | tf_op jit(solution)/shard_map/ppermute | solution.py:27
  62.8 7.3 %all-to-all-start.2 = ((f32[16,5,2,16,256]{4,3,2,1,0:T(8,128)}), f32[16,5,2,16,256]{4,3,2,1,0:T(8,128)S(1)}, u32[]{:S(2)}, u32[]{:S(2)}) async-start(f32[16,5,2,16,256]{4,3,2,1,0:T(8,128)} %bitcast.9), calls=%async_computation.2 | async-start | bytes 5242880 | tf_op jit(solution)/shard_map/all_to_all | solution.py:262
  70.4 17.6 %collective-permute-done.7 = f32[128,256]{1,0:T(8,128)S(1)} collective-permute-done((f32[128,256]{1,0:T(8,128)S(1)}, f32[128,256]{1,0:T(8,128)S(1)}, u32[]{:S(2)}, u32[]{:S(2)}) %collective-permute-start.7) | collective-permute-done | bytes 131104 | tf_op jit(solution)/shard_map/ppermute | solution.py:27
  88.3 13.3 %collective-permute-done.10 = f32[256,256]{1,0:T(8,128)S(1)} collective-permute-done((f32[256,256]{1,0:T(8,128)S(1)}, f32[256,256]{1,0:T(8,128)S(1)}, u32[]{:S(2)}, u32[]{:S(2)}) %collective-permute-start.10) | collective-permute-done | bytes 262176 | tf_op jit(solution)/shard_map/ppermute | solution.py:27
  102.3 1.1 pad_maximum_fusion.1
  104.2 2.6 %collective-permute-done.11 = f32[1024,256]{1,0:T(8,128)} collective-permute-done((f32[1024,256]{1,0:T(8,128)}, f32[1024,256]{1,0:T(8,128)}, u32[]{:S(2)}, u32[]{:S(2)}) %collective-permute-start.11) | collective-permute-done | bytes 1048608 | tf_op jit(solution)/shard_map/ppermute | solution.py:27
  106.9 1.4 broadcast_select_fusion.1
  108.3 1.5 pad_maximum_fusion
  109.8 12.9 %absorb.2 = f32[16,3,2,16,256]{4,3,2,1,0:T(8,128)} custom-call(f32[16,3,2,16,256]{4,3,2,1,0:T(8,128)} %all-to-all-done.stem_ref, f32[4,2,256,256]{3,2,1,0:T(8,128)} %bitcast.35, f32[4,256,256]{2,1,0:T(8,128)} %get-tuple-element.14.cos_ref, f32[4,256,256]{2,1,0:T(8,128)} %get-tuple-element.15.sin_ref), custom_call_target="tpu_custom_call" | custom-call | flops 4831838208 | bytes 3145728 | tf_op jit(solution)/shard_map/absorb/pallas_call | solution.py:146
  122.7 6.1 %all-to-all-done.2.stem_ref = f32[16,5,2,16,256]{4,3,2,1,0:T(8,128)S(1)} async-done(((f32[16,5,2,16,256]{4,3,2,1,0:T(8,128)}), f32[16,5,2,16,256]{4,3,2,1,0:T(8,128)S(1)}, u32[]{:S(2)}, u32[]{:S(2)}) %all-to-all-start.2) | async-done | bytes 2621472 | tf_op jit(solution)/shard_map/all_to_all | solution.py:262
  128.8 1.5 copy-done.2
  130.3 4.9 %all-to-all-start.1 = ((f32[16,3,2,16,256]{4,3,2,1,0:T(8,128)}), f32[16,3,2,16,256]{4,3,2,1,0:T(8,128)S(1)}, u32[]{:S(2)}, u32[]{:S(2)}) async-start(f32[16,3,2,16,256]{4,3,2,1,0:T(8,128)} %absorb.2), calls=%async_computation.1 | async-start | bytes 3145728 | tf_op jit(solution)/shard_map/all_to_all | solution.py:262
  135.1 18.9 %absorb.3 = f32[16,5,2,16,256]{4,3,2,1,0:T(8,128)} custom-call(f32[16,5,2,16,256]{4,3,2,1,0:T(8,128)} %copy-done.2, f32[4,2,256,256]{3,2,1,0:T(8,128)} %bitcast.36, f32[4,256,256]{2,1,0:T(8,128)} %get-tuple-element.14.cos_ref, f32[4,256,256]{2,1,0:T(8,128)} %get-tuple-element.15.sin_ref), custom_call_target="tpu_custom_call" | custom-call | flops 8053063680 | bytes 5242880 | tf_op jit(solution)/shard_map/absorb/pallas_call | solution.py:146
  154.1 17.2 %all-to-all-done.1 = f32[16,3,2,16,256]{4,3,2,1,0:T(8,128)S(1)} async-done(((f32[16,3,2,16,256]{4,3,2,1,0:T(8,128)}), f32[16,3,2,16,256]{4,3,2,1,0:T(8,128)S(1)}, u32[]{:S(2)}, u32[]{:S(2)}) %all-to-all-start.1) | async-done | bytes 1572896 | tf_op jit(solution)/shard_map/all_to_all | solution.py:262
  171.3 1.1 copy-done
  172.5 4.9 %all-to-all-start.3 = ((f32[16,5,2,16,256]{4,3,2,1,0:T(8,128)}), f32[16,5,2,16,256]{4,3,2,1,0:T(8,128)S(1)}, u32[]{:S(2)}, u32[]{:S(2)}) async-start(f32[16,5,2,16,256]{4,3,2,1,0:T(8,128)} %absorb.3), calls=%async_computation.3 | async-start | bytes 5242880 | tf_op jit(solution)/shard_map/all_to_all | solution.py:262
  177.4 3.8 %rows_first.1.low_ref = f32[2,16,48,256]{3,2,1,0:T(8,128)} custom-call(f32[48,2,16,256]{3,2,1,0:T(8,128)} %bitcast.29), custom_call_target="tpu_custom_call" | custom-call | bytes 3145728 | tf_op jit(solution)/shard_map/rows_first/pallas_call | solution.py:211
  181.1 54.9 %all-to-all-done.3 = f32[16,5,2,16,256]{4,3,2,1,0:T(8,128)S(1)} async-done(((f32[16,5,2,16,256]{4,3,2,1,0:T(8,128)}), f32[16,5,2,16,256]{4,3,2,1,0:T(8,128)S(1)}, u32[]{:S(2)}, u32[]{:S(2)}) %all-to-all-start.3) | async-done | bytes 2621472 | tf_op jit(solution)/shard_map/all_to_all | solution.py:262
  236.0 3.5 %batch_last.1 = f32[2,16,256,128]{3,2,1,0:T(8,128)} custom-call(f32[2,16,48,256]{3,2,1,0:T(8,128)} %rows_first.1.low_ref, f32[80,2,16,256]{3,2,1,0:T(8,128)S(1)} %bitcast.28), custom_call_target="tpu_custom_call" | custom-call | tf_op jit(solution)/shard_map/batch_last/pallas_call | solution.py:245
  (51 shorter events, 6.4 us)
Async XLA Ops:
  0.0 3.5 %copy-start.1 = (f32[1,2,2,256,256]{4,3,2,1,0:T(8,128)S(1)}, f32[1,2,2,256,256]{4,3,2,1,0:T(8,128)}, u32[]{:S(2)}) copy-start(f32[1,2,2,256,256]{4,3,2,1,0:T(8,128)} %param.5) | copy-start | bytes 3145732
  0.0 4.3 %copy-start.5 = (s32[4]{0:T(128)S(1)}, s32[4]{0:T(128)}, u32[]{:S(2)}) copy-start(s32[4]{0:T(128)} %param.6) | copy-start | bytes 52
  5.7 6.7 %collective-permute-start = (f32[1024,256]{1,0:T(8,128)S(1)}, f32[1024,256]{1,0:T(8,128)}, u32[]{:S(2)}, u32[]{:S(2)}) collective-permute-start(f32[1024,256]{1,0:T(8,128)S(1)} %constant_dynamic-slice_fusion.4), channel_id=1, source_target_pairs={{0,2},{2,0},{4,6},{6,4},{8,10},{10,8},{12,14},{14,12},{16,18},{18,... | collective-permute-start | bytes 3145736 | tf_op jit(solution)/shard_map/ppermute | solution.py:27
  6.4 56.3 %all-to-all-start = ((f32[16,3,2,16,256]{4,3,2,1,0:T(8,128)}), f32[16,3,2,16,256]{4,3,2,1,0:T(8,128)}, u32[]{:S(2)}, u32[]{:S(2)}) async-start(f32[16,3,2,16,256]{4,3,2,1,0:T(8,128)} %bitcast.30), calls=%async_computation | async-start | bytes 3145728 | tf_op jit(solution)/shard_map/all_to_all | solution.py:262
  13.9 13.9 %collective-permute-start.3 = (f32[256,256]{1,0:T(8,128)S(1)}, f32[256,256]{1,0:T(8,128)S(1)}, u32[]{:S(2)}, u32[]{:S(2)}) collective-permute-start(f32[256,256]{1,0:T(8,128)S(1)} %constant_dynamic-slice_fusion.1), channel_id=1, source_target_pairs={{0,4},{2,6},{4,0},{6,2},{8,12},{10,14},{12,8},{14,10},{16,20},{18,... | collective-permute-start | bytes 786440 | tf_op jit(solution)/shard_map/ppermute | solution.py:27
  14.3 14.9 %collective-permute-start.1 = (f32[256,256]{1,0:T(8,128)S(1)}, f32[256,256]{1,0:T(8,128)S(1)}, u32[]{:S(2)}, u32[]{:S(2)}) collective-permute-start(f32[256,256]{1,0:T(8,128)S(1)} %constant_dynamic-slice_fusion.3), channel_id=1, source_target_pairs={{0,1},{1,0},{2,3},{3,2},{4,5},{5,4},{6,7},{7,6},{8,9},{9,8},{10,11... | collective-permute-start | bytes 786440 | tf_op jit(solution)/shard_map/ppermute | solution.py:27
  27.9 4.3 %collective-permute-start.4 = (f32[128,256]{1,0:T(8,128)S(1)}, f32[128,256]{1,0:T(8,128)S(1)}, u32[]{:S(2)}, u32[]{:S(2)}) collective-permute-start(f32[128,256]{1,0:T(8,128)S(1)} %constant_dynamic-slice_fusion), channel_id=1, source_target_pairs={{0,1},{1,0},{2,3},{3,2},{4,5},{5,4},{6,7},{7,6},{8,9},{9,8},{10,11... | collective-permute-start | bytes 393224 | tf_op jit(solution)/shard_map/ppermute | solution.py:27
  29.2 5.2 %collective-permute-start.2 = (f32[128,256]{1,0:T(8,128)S(1)}, f32[128,256]{1,0:T(8,128)S(1)}, u32[]{:S(2)}, u32[]{:S(2)}) collective-permute-start(f32[128,256]{1,0:T(8,128)S(1)} %constant_dynamic-slice_fusion.2), channel_id=1, source_target_pairs={{0,4},{2,6},{4,0},{6,2},{8,12},{10,14},{12,8},{14,10},{16,20},{18,... | collective-permute-start | bytes 393224 | tf_op jit(solution)/shard_map/ppermute | solution.py:27
  34.5 16.7 %copy-start.4 = (f32[4,256,256]{2,1,0:T(8,128)S(1)}, f32[4,256,256]{2,1,0:T(8,128)}, u32[]{:S(2)}) copy-start(f32[4,256,256]{2,1,0:T(8,128)} %param.7) | copy-start | bytes 3145732
  34.5 14.7 %collective-permute-start.5 = (f32[256,256]{1,0:T(8,128)S(1)}, f32[256,256]{1,0:T(8,128)S(1)}, u32[]{:S(2)}, u32[]{:S(2)}) collective-permute-start(f32[256,256]{1,0:T(8,128)S(1)} %pad_maximum_fusion.3), channel_id=1, source_target_pairs={{0,8},{2,10},{4,12},{6,14},{8,0},{10,2},{12,4},{14,6},{16,24},{18,... | collective-permute-start | bytes 786440 | tf_op jit(solution)/shard_map/ppermute | solution.py:27
  49.3 13.5 %collective-permute-start.6 = (f32[256,256]{1,0:T(8,128)S(1)}, f32[256,256]{1,0:T(8,128)S(1)}, u32[]{:S(2)}, u32[]{:S(2)}) collective-permute-start(f32[256,256]{1,0:T(8,128)S(1)} %fusion.4), channel_id=1, source_target_pairs={{0,16},{2,18},{4,20},{6,22},{8,24},{10,26},{12,28},{14,30},{16,0},... | collective-permute-start | bytes 786440 | tf_op jit(solution)/shard_map/ppermute | solution.py:27
  62.8 66.0 %all-to-all-start.2 = ((f32[16,5,2,16,256]{4,3,2,1,0:T(8,128)}), f32[16,5,2,16,256]{4,3,2,1,0:T(8,128)S(1)}, u32[]{:S(2)}, u32[]{:S(2)}) async-start(f32[16,5,2,16,256]{4,3,2,1,0:T(8,128)} %bitcast.9), calls=%async_computation.2 | async-start | bytes 5242880 | tf_op jit(solution)/shard_map/all_to_all | solution.py:262
  70.0 17.9 %collective-permute-start.7 = (f32[128,256]{1,0:T(8,128)S(1)}, f32[128,256]{1,0:T(8,128)S(1)}, u32[]{:S(2)}, u32[]{:S(2)}) collective-permute-start(f32[128,256]{1,0:T(8,128)S(1)} %get-tuple-element.33), channel_id=1, source_target_pairs={{0,4},{2,6},{4,0},{6,2},{8,12},{10,14},{12,8},{14,10},{16,20},{18,... | collective-permute-start | bytes 393224 | tf_op jit(solution)/shard_map/ppermute | solution.py:27
  70.4 17.6 %collective-permute-start.9 = (f32[128,256]{1,0:T(8,128)S(1)}, f32[128,256]{1,0:T(8,128)S(1)}, u32[]{:S(2)}, u32[]{:S(2)}) collective-permute-start(f32[128,256]{1,0:T(8,128)S(1)} %get-tuple-element.34), channel_id=1, source_target_pairs={{0,1},{1,0},{2,3},{3,2},{4,5},{5,4},{6,7},{7,6},{8,9},{9,8},{10,11... | collective-permute-start | bytes 393224 | tf_op jit(solution)/shard_map/ppermute | solution.py:27
  88.1 13.5 %collective-permute-start.10 = (f32[256,256]{1,0:T(8,128)S(1)}, f32[256,256]{1,0:T(8,128)S(1)}, u32[]{:S(2)}, u32[]{:S(2)}) collective-permute-start(f32[256,256]{1,0:T(8,128)S(1)} %pad_maximum_fusion.5), channel_id=1, source_target_pairs={{0,4},{2,6},{4,0},{6,2},{8,12},{10,14},{12,8},{14,10},{16,20},{18,... | collective-permute-start | bytes 786440 | tf_op jit(solution)/shard_map/ppermute | solution.py:27
  88.2 13.4 %collective-permute-start.8 = (f32[256,256]{1,0:T(8,128)S(1)}, f32[256,256]{1,0:T(8,128)S(1)}, u32[]{:S(2)}, u32[]{:S(2)}) collective-permute-start(f32[256,256]{1,0:T(8,128)S(1)} %pad_maximum_fusion.4), channel_id=1, source_target_pairs={{0,1},{1,0},{2,3},{3,2},{4,5},{5,4},{6,7},{7,6},{8,9},{9,8},{10,11... | collective-permute-start | bytes 786440 | tf_op jit(solution)/shard_map/ppermute | solution.py:27
  101.7 0.7 copy-start.3
  103.4 3.5 %collective-permute-start.11 = (f32[1024,256]{1,0:T(8,128)}, f32[1024,256]{1,0:T(8,128)}, u32[]{:S(2)}, u32[]{:S(2)}) collective-permute-start(f32[1024,256]{1,0:T(8,128)} %pad_maximum_fusion.1), channel_id=1, source_target_pairs={{0,2},{2,0},{4,6},{6,4},{8,10},{10,8},{12,14},{14,12},{16,18},{18,... | collective-permute-start | bytes 3145736 | tf_op jit(solution)/shard_map/ppermute | solution.py:27
  128.8 1.5 copy-start.2
  130.3 41.0 %all-to-all-start.1 = ((f32[16,3,2,16,256]{4,3,2,1,0:T(8,128)}), f32[16,3,2,16,256]{4,3,2,1,0:T(8,128)S(1)}, u32[]{:S(2)}, u32[]{:S(2)}) async-start(f32[16,3,2,16,256]{4,3,2,1,0:T(8,128)} %absorb.2), calls=%async_computation.1 | async-start | bytes 3145728 | tf_op jit(solution)/shard_map/all_to_all | solution.py:262
  171.3 1.1 copy-start
  172.5 63.6 %all-to-all-start.3 = ((f32[16,5,2,16,256]{4,3,2,1,0:T(8,128)}), f32[16,5,2,16,256]{4,3,2,1,0:T(8,128)S(1)}, u32[]{:S(2)}, u32[]{:S(2)}) async-start(f32[16,5,2,16,256]{4,3,2,1,0:T(8,128)} %absorb.3), calls=%async_computation.3 | async-start | bytes 5242880 | tf_op jit(solution)/shard_map/all_to_all | solution.py:262

commit v4 on v3

--- a/solution.py
+++ b/solution.py
@@ -9,6 +9,7 @@
 
 STEPS = 4
 MIB = 1024 * 1024
+WEIGHT = 3.35
 DOT = partial(jnp.dot, precision=lax.Precision.HIGHEST)
 
 
@@ -138,7 +139,7 @@
     return pl.BlockSpec(array.shape, lambda i: (0,) * array.ndim, pipeline_mode=pl.Buffered(1))
 
 
-def absorb(stem, branches, cosine, sine):
+def absorb(stem, branches, cosine, sine, weight=1):
     peers, items, _, block, width = stem.shape
     per = 2 if items % 2 == 0 else 1
     spec = pl.BlockSpec((peers, per, 2, block, width), lambda i: (0, i, 0, 0, 0))
@@ -153,7 +154,7 @@
             pltpu.VMEM((STEPS // 2, 6 * width, 2 * width), jnp.bfloat16),
             pltpu.VMEM((STEPS // 2, 2 * width, 6 * width), jnp.bfloat16),
         ],
-        cost_estimate=pl.CostEstimate(flops=flops, bytes_accessed=8 * stem.size, transcendentals=0),
+        cost_estimate=pl.CostEstimate(flops=int(flops * weight), bytes_accessed=8 * stem.size, transcendentals=0),
         compiler_params=pltpu.CompilerParams(vmem_limit_bytes=32 * MIB),
         name="absorb",
     )(*in_hbm(stem, branches, cosine, sine))
@@ -272,13 +273,16 @@
     stem_low = exchange(sent_low)
     held = scatter_branches(build_branch(factors[0]), branch_owner, rows, cols)
     cosine, sine = jnp.cos(entangle_phase), jnp.sin(entangle_phase)
-    for bit in broadcast_orders(rows, cols)[2]:
+    far = broadcast_orders(rows, cols)[2]
+    for bit in far[:-1]:
         held = held + swap(held, "row", rows, bit)
     sent_high = batch_first(stem_slab, rows * low, rows * high).reshape(rows, high, parts, block, width)
     held, sent_high, cosine, sine = lax.optimization_barrier((held, sent_high, cosine, sine))
+    for bit in far[-1:]:
+        held = held + swap(held, "row", rows, bit)
     stem_high = exchange(sent_high)
     branches = gather_branches(held, rows, cols)
-    back_low = exchange(absorb(stem_low, branches, cosine, sine))
+    back_low = exchange(absorb(stem_low, branches, cosine, sine, WEIGHT))
     back_high = exchange(absorb(stem_high, branches, cosine, sine))
     back_low = rows_first(back_low.reshape(rows * low, parts, block, width))
     return batch_last(back_low, back_high.reshape(rows * high, parts, block, width))

time: 240 us -> 232 us (0.967)
  waiting for transfers between devices: 140 us -> 132 us
    ppermute x12, waiting for transfers between devices: 62 us -> 52.9 us  [swap(): return lax.ppermute(array, axis, [(i, i ^ bit) for i in range(size)])]
where the time goes in v4:
time: 232 us
  waiting for transfers between devices  132 us (57%)
  Pallas kernels  47.3 us (20%)
  starting transfers between devices  36.6 us (16%)
  local copies, waits for them, and re-layouts  8.16 us (4%)
  other arithmetic  6.05 us (3%)
    all_to_all x4, waiting for transfers between devices, exchange(): return lax.all_to_all(parts, 'row', 0, 0, tiled=True)  78.8 us
    ppermute x12, waiting for transfers between devices, swap(): return lax.ppermute(array, axis, [(i, i ^ bit) for i in range(size)])  52.9 us
    pallas_call x2, Pallas kernels, absorb(): pl.pallas_call(absorb_kernel, grid=(items // per,), in_specs=[spec, whole...  31.9 us
    all_to_all x4, starting transfers between devices, exchange(): return lax.all_to_all(parts, 'row', 0, 0, tiled=True)  21.9 us
    ppermute x12, starting transfers between devices, swap(): return lax.ppermute(array, axis, [(i, i ^ bit) for i in range(size)])  14.7 us
    pallas_call x2, Pallas kernels, batch_first(): pl.pallas_call(partial(batch_first_kernel, start), in_specs=[pl.BlockSpec...  8.18 us
  transfers between devices with their start and end apart: 16, of which 11 were waited for; matrix products, arithmetic and copies ran while one was open for 4% of the time, Pallas kernels for 17%

profile of v4, /device:TPU:13, one launch (start us, length us, event | category | flops | bytes accessed | tf_op | source)
XLA Modules:
  0.0 231.8 jit_solution(8501022217120446645)
XLA Ops:
  0.0 3.5 %batch_first.2 = f32[48,2,16,256]{3,2,1,0:T(8,128)} custom-call(f32[2,16,256,128]{3,2,1,0:T(8,128)} %stem_ref.3), custom_call_target="tpu_custom_call" | custom-call | bytes 8388608 | tf_op jit(solution)/shard_map/batch_first/pallas_call | solution.py:188
  6.4 6.0 %all-to-all-start = ((f32[16,3,2,16,256]{4,3,2,1,0:T(8,128)}), f32[16,3,2,16,256]{4,3,2,1,0:T(8,128)}, u32[]{:S(2)}, u32[]{:S(2)}) async-start(f32[16,3,2,16,256]{4,3,2,1,0:T(8,128)} %bitcast.30), calls=%async_computation | async-start | bytes 3145728 | tf_op jit(solution)/shard_map/all_to_all | solution.py:263
  12.4 1.4 dynamic-slice_add_fusion
  14.2 4.7 %batch_first.3 = f32[80,2,16,256]{3,2,1,0:T(8,128)} custom-call(f32[2,16,256,128]{3,2,1,0:T(8,128)} %stem_ref.3), custom_call_target="tpu_custom_call" | custom-call | bytes 8388608 | tf_op jit(solution)/shard_map/batch_first/pallas_call | solution.py:188
  19.0 1.3 collective-permute-start.1
  20.3 7.5 %collective-permute-done.3 = f32[256,256]{1,0:T(8,128)S(1)} collective-permute-done((f32[256,256]{1,0:T(8,128)S(1)}, f32[256,256]{1,0:T(8,128)S(1)}, u32[]{:S(2)}, u32[]{:S(2)}) %collective-permute-start.3) | collective-permute-done | bytes 262176 | tf_op jit(solution)/shard_map/ppermute | solution.py:28
  27.9 1.3 collective-permute-start.4
  29.2 2.3 collective-permute-start.2
  32.2 2.3 collective-permute-done.2
  34.5 3.7 %collective-permute-start.5 = (f32[256,256]{1,0:T(8,128)S(1)}, f32[256,256]{1,0:T(8,128)S(1)}, u32[]{:S(2)}, u32[]{:S(2)}) collective-permute-start(f32[256,256]{1,0:T(8,128)S(1)} %pad_maximum_fusion.3), channel_id=1, source_target_pairs={{0,8},{2,10},{4,12},{6,14},{8,0},{10,2},{12,4},{14,6},{16,24},{18,... | collective-permute-start | bytes 786440 | tf_op jit(solution)/shard_map/ppermute | solution.py:28
  38.2 4.5 %fusion.5 = (f32[4,256,256]{2,1,0:T(8,128)}, f32[4,256,256]{2,1,0:T(8,128)}) fusion(f32[4,256,256]{2,1,0:T(8,128)S(1)} %copy-done.4), kind=kLoop, calls=%fused_computation.39 | loop fusion | bytes 3145728 | tf_op jit(solution)/shard_map/sin | solution.py:275
  42.7 6.5 %collective-permute-done.5 = f32[256,256]{1,0:T(8,128)S(1)} collective-permute-done((f32[256,256]{1,0:T(8,128)S(1)}, f32[256,256]{1,0:T(8,128)S(1)}, u32[]{:S(2)}, u32[]{:S(2)}) %collective-permute-start.5) | collective-permute-done | bytes 262176 | tf_op jit(solution)/shard_map/ppermute | solution.py:28
  49.3 1.9 collective-permute-start.6
  51.1 5.9 %all-to-all-start.2 = ((f32[16,5,2,16,256]{4,3,2,1,0:T(8,128)}), f32[16,5,2,16,256]{4,3,2,1,0:T(8,128)S(1)}, u32[]{:S(2)}, u32[]{:S(2)}) async-start(f32[16,5,2,16,256]{4,3,2,1,0:T(8,128)} %bitcast.9), calls=%async_computation.2 | async-start | bytes 5242880 | tf_op jit(solution)/shard_map/all_to_all | solution.py:263
  57.1 19.7 %collective-permute-done.6 = f32[256,256]{1,0:T(8,128)S(1)} collective-permute-done((f32[256,256]{1,0:T(8,128)S(1)}, f32[256,256]{1,0:T(8,128)S(1)}, u32[]{:S(2)}, u32[]{:S(2)}) %collective-permute-start.6) | collective-permute-done | bytes 262176 | tf_op jit(solution)/shard_map/ppermute | solution.py:28
  77.0 4.6 %collective-permute-done.7 = f32[128,256]{1,0:T(8,128)S(1)} collective-permute-done((f32[128,256]{1,0:T(8,128)S(1)}, f32[128,256]{1,0:T(8,128)S(1)}, u32[]{:S(2)}, u32[]{:S(2)}) %collective-permute-start.7) | collective-permute-done | bytes 131104 | tf_op jit(solution)/shard_map/ppermute | solution.py:28
  81.7 2.3 collective-permute-start.10
  84.1 9.0 %collective-permute-done.10 = f32[256,256]{1,0:T(8,128)S(1)} collective-permute-done((f32[256,256]{1,0:T(8,128)S(1)}, f32[256,256]{1,0:T(8,128)S(1)}, u32[]{:S(2)}, u32[]{:S(2)}) %collective-permute-start.10) | collective-permute-done | bytes 262176 | tf_op jit(solution)/shard_map/ppermute | solution.py:28
  95.6 2.6 %collective-permute-done.11 = f32[1024,256]{1,0:T(8,128)} collective-permute-done((f32[1024,256]{1,0:T(8,128)}, f32[1024,256]{1,0:T(8,128)}, u32[]{:S(2)}, u32[]{:S(2)}) %collective-permute-start.11) | collective-permute-done | bytes 1048608 | tf_op jit(solution)/shard_map/ppermute | solution.py:28
  98.2 1.4 broadcast_select_fusion.1
  99.6 1.5 pad_maximum_fusion
  101.1 12.9 %absorb.2 = f32[16,3,2,16,256]{4,3,2,1,0:T(8,128)} custom-call(f32[16,3,2,16,256]{4,3,2,1,0:T(8,128)} %all-to-all-done.stem_ref, f32[4,2,256,256]{3,2,1,0:T(8,128)} %bitcast.35, f32[4,256,256]{2,1,0:T(8,128)} %get-tuple-element.14.cos_ref, f32[4,256,256]{2,1,0:T(8,128)} %get-tuple-element.15.sin_ref), custom_call_target="tpu_custom_call" | custom-call | flops 16186657792 | bytes 3145728 | tf_op jit(solution)/shard_map/absorb/pallas_call | solution.py:147
  114.0 6.6 %all-to-all-done.2.stem_ref = f32[16,5,2,16,256]{4,3,2,1,0:T(8,128)S(1)} async-done(((f32[16,5,2,16,256]{4,3,2,1,0:T(8,128)}), f32[16,5,2,16,256]{4,3,2,1,0:T(8,128)S(1)}, u32[]{:S(2)}, u32[]{:S(2)}) %all-to-all-start.2) | async-done | bytes 2621472 | tf_op jit(solution)/shard_map/all_to_all | solution.py:263
  120.7 1.5 copy-done.2
  122.2 5.0 %all-to-all-start.1 = ((f32[16,3,2,16,256]{4,3,2,1,0:T(8,128)}), f32[16,3,2,16,256]{4,3,2,1,0:T(8,128)S(1)}, u32[]{:S(2)}, u32[]{:S(2)}) async-start(f32[16,3,2,16,256]{4,3,2,1,0:T(8,128)} %absorb.2), calls=%async_computation.1 | async-start | bytes 3145728 | tf_op jit(solution)/shard_map/all_to_all | solution.py:263
  127.2 18.9 %absorb.3 = f32[16,5,2,16,256]{4,3,2,1,0:T(8,128)} custom-call(f32[16,5,2,16,256]{4,3,2,1,0:T(8,128)} %copy-done.2, f32[4,2,256,256]{3,2,1,0:T(8,128)} %bitcast.36, f32[4,256,256]{2,1,0:T(8,128)} %get-tuple-element.14.cos_ref, f32[4,256,256]{2,1,0:T(8,128)} %get-tuple-element.15.sin_ref), custom_call_target="tpu_custom_call" | custom-call | flops 8053063680 | bytes 5242880 | tf_op jit(solution)/shard_map/absorb/pallas_call | solution.py:147
  146.1 17.2 %all-to-all-done.1 = f32[16,3,2,16,256]{4,3,2,1,0:T(8,128)S(1)} async-done(((f32[16,3,2,16,256]{4,3,2,1,0:T(8,128)}), f32[16,3,2,16,256]{4,3,2,1,0:T(8,128)S(1)}, u32[]{:S(2)}, u32[]{:S(2)}) %all-to-all-start.1) | async-done | bytes 1572896 | tf_op jit(solution)/shard_map/all_to_all | solution.py:263
  163.4 1.1 copy-done
  164.5 4.9 %all-to-all-start.3 = ((f32[16,5,2,16,256]{4,3,2,1,0:T(8,128)}), f32[16,5,2,16,256]{4,3,2,1,0:T(8,128)S(1)}, u32[]{:S(2)}, u32[]{:S(2)}) async-start(f32[16,5,2,16,256]{4,3,2,1,0:T(8,128)} %absorb.3), calls=%async_computation.3 | async-start | bytes 5242880 | tf_op jit(solution)/shard_map/all_to_all | solution.py:263
  169.4 3.8 %rows_first.1.low_ref = f32[2,16,48,256]{3,2,1,0:T(8,128)} custom-call(f32[48,2,16,256]{3,2,1,0:T(8,128)} %bitcast.29), custom_call_target="tpu_custom_call" | custom-call | bytes 3145728 | tf_op jit(solution)/shard_map/rows_first/pallas_call | solution.py:212
  173.2 54.9 %all-to-all-done.3 = f32[16,5,2,16,256]{4,3,2,1,0:T(8,128)S(1)} async-done(((f32[16,5,2,16,256]{4,3,2,1,0:T(8,128)}), f32[16,5,2,16,256]{4,3,2,1,0:T(8,128)S(1)}, u32[]{:S(2)}, u32[]{:S(2)}) %all-to-all-start.3) | async-done | bytes 2621472 | tf_op jit(solution)/shard_map/all_to_all | solution.py:263
  228.1 3.5 %batch_last.1 = f32[2,16,256,128]{3,2,1,0:T(8,128)} custom-call(f32[2,16,48,256]{3,2,1,0:T(8,128)} %rows_first.1.low_ref, f32[80,2,16,256]{3,2,1,0:T(8,128)S(1)} %bitcast.28), custom_call_target="tpu_custom_call" | custom-call | tf_op jit(solution)/shard_map/batch_last/pallas_call | solution.py:246
  (51 shorter events, 7.0 us)
Async XLA Ops:
  0.0 3.5 %copy-start.1 = (f32[1,2,2,256,256]{4,3,2,1,0:T(8,128)S(1)}, f32[1,2,2,256,256]{4,3,2,1,0:T(8,128)}, u32[]{:S(2)}) copy-start(f32[1,2,2,256,256]{4,3,2,1,0:T(8,128)} %param.5) | copy-start | bytes 3145732
  0.0 4.3 %copy-start.5 = (s32[4]{0:T(128)S(1)}, s32[4]{0:T(128)}, u32[]{:S(2)}) copy-start(s32[4]{0:T(128)} %param.6) | copy-start | bytes 52
  5.7 6.7 %collective-permute-start = (f32[1024,256]{1,0:T(8,128)S(1)}, f32[1024,256]{1,0:T(8,128)}, u32[]{:S(2)}, u32[]{:S(2)}) collective-permute-start(f32[1024,256]{1,0:T(8,128)S(1)} %constant_dynamic-slice_fusion.4), channel_id=1, source_target_pairs={{0,2},{2,0},{4,6},{6,4},{8,10},{10,8},{12,14},{14,12},{16,18},{18,... | collective-permute-start | bytes 3145736 | tf_op jit(solution)/shard_map/ppermute | solution.py:28
  6.4 44.7 %all-to-all-start = ((f32[16,3,2,16,256]{4,3,2,1,0:T(8,128)}), f32[16,3,2,16,256]{4,3,2,1,0:T(8,128)}, u32[]{:S(2)}, u32[]{:S(2)}) async-start(f32[16,3,2,16,256]{4,3,2,1,0:T(8,128)} %bitcast.30), calls=%async_computation | async-start | bytes 3145728 | tf_op jit(solution)/shard_map/all_to_all | solution.py:263
  13.9 13.9 %collective-permute-start.3 = (f32[256,256]{1,0:T(8,128)S(1)}, f32[256,256]{1,0:T(8,128)S(1)}, u32[]{:S(2)}, u32[]{:S(2)}) collective-permute-start(f32[256,256]{1,0:T(8,128)S(1)} %constant_dynamic-slice_fusion.1), channel_id=1, source_target_pairs={{0,4},{2,6},{4,0},{6,2},{8,12},{10,14},{12,8},{14,10},{16,20},{18,... | collective-permute-start | bytes 786440 | tf_op jit(solution)/shard_map/ppermute | solution.py:28
  18.9 19.3 %copy-start.4 = (f32[4,256,256]{2,1,0:T(8,128)S(1)}, f32[4,256,256]{2,1,0:T(8,128)}, u32[]{:S(2)}) copy-start(f32[4,256,256]{2,1,0:T(8,128)} %param.7) | copy-start | bytes 3145732
  19.0 10.2 %collective-permute-start.1 = (f32[256,256]{1,0:T(8,128)S(1)}, f32[256,256]{1,0:T(8,128)S(1)}, u32[]{:S(2)}, u32[]{:S(2)}) collective-permute-start(f32[256,256]{1,0:T(8,128)S(1)} %constant_dynamic-slice_fusion.3), channel_id=1, source_target_pairs={{0,1},{1,0},{2,3},{3,2},{4,5},{5,4},{6,7},{7,6},{8,9},{9,8},{10,11... | collective-permute-start | bytes 786440 | tf_op jit(solution)/shard_map/ppermute | solution.py:28
  27.9 4.3 %collective-permute-start.4 = (f32[128,256]{1,0:T(8,128)S(1)}, f32[128,256]{1,0:T(8,128)S(1)}, u32[]{:S(2)}, u32[]{:S(2)}) collective-permute-start(f32[128,256]{1,0:T(8,128)S(1)} %constant_dynamic-slice_fusion), channel_id=1, source_target_pairs={{0,1},{1,0},{2,3},{3,2},{4,5},{5,4},{6,7},{7,6},{8,9},{9,8},{10,11... | collective-permute-start | bytes 393224 | tf_op jit(solution)/shard_map/ppermute | solution.py:28
  29.2 5.2 %collective-permute-start.2 = (f32[128,256]{1,0:T(8,128)S(1)}, f32[128,256]{1,0:T(8,128)S(1)}, u32[]{:S(2)}, u32[]{:S(2)}) collective-permute-start(f32[128,256]{1,0:T(8,128)S(1)} %constant_dynamic-slice_fusion.2), channel_id=1, source_target_pairs={{0,4},{2,6},{4,0},{6,2},{8,12},{10,14},{12,8},{14,10},{16,20},{18,... | collective-permute-start | bytes 393224 | tf_op jit(solution)/shard_map/ppermute | solution.py:28
  34.5 14.7 %collective-permute-start.5 = (f32[256,256]{1,0:T(8,128)S(1)}, f32[256,256]{1,0:T(8,128)S(1)}, u32[]{:S(2)}, u32[]{:S(2)}) collective-permute-start(f32[256,256]{1,0:T(8,128)S(1)} %pad_maximum_fusion.3), channel_id=1, source_target_pairs={{0,8},{2,10},{4,12},{6,14},{8,0},{10,2},{12,4},{14,6},{16,24},{18,... | collective-permute-start | bytes 786440 | tf_op jit(solution)/shard_map/ppermute | solution.py:28
  49.3 27.5 %collective-permute-start.6 = (f32[256,256]{1,0:T(8,128)S(1)}, f32[256,256]{1,0:T(8,128)S(1)}, u32[]{:S(2)}, u32[]{:S(2)}) collective-permute-start(f32[256,256]{1,0:T(8,128)S(1)} %fusion.4), channel_id=1, source_target_pairs={{0,16},{2,18},{4,20},{6,22},{8,24},{10,26},{12,28},{14,30},{16,0},... | collective-permute-start | bytes 786440 | tf_op jit(solution)/shard_map/ppermute | solution.py:28
  51.1 69.5 %all-to-all-start.2 = ((f32[16,5,2,16,256]{4,3,2,1,0:T(8,128)}), f32[16,5,2,16,256]{4,3,2,1,0:T(8,128)S(1)}, u32[]{:S(2)}, u32[]{:S(2)}) async-start(f32[16,5,2,16,256]{4,3,2,1,0:T(8,128)} %bitcast.9), calls=%async_computation.2 | async-start | bytes 5242880 | tf_op jit(solution)/shard_map/all_to_all | solution.py:263
  76.9 4.8 %collective-permute-start.7 = (f32[128,256]{1,0:T(8,128)S(1)}, f32[128,256]{1,0:T(8,128)S(1)}, u32[]{:S(2)}, u32[]{:S(2)}) collective-permute-start(f32[128,256]{1,0:T(8,128)S(1)} %get-tuple-element.33), channel_id=1, source_target_pairs={{0,4},{2,6},{4,0},{6,2},{8,12},{10,14},{12,8},{14,10},{16,20},{18,... | collective-permute-start | bytes 393224 | tf_op jit(solution)/shard_map/ppermute | solution.py:28
  76.9 4.7 %collective-permute-start.9 = (f32[128,256]{1,0:T(8,128)S(1)}, f32[128,256]{1,0:T(8,128)S(1)}, u32[]{:S(2)}, u32[]{:S(2)}) collective-permute-start(f32[128,256]{1,0:T(8,128)S(1)} %get-tuple-element.34), channel_id=1, source_target_pairs={{0,1},{1,0},{2,3},{3,2},{4,5},{5,4},{6,7},{7,6},{8,9},{9,8},{10,11... | collective-permute-start | bytes 393224 | tf_op jit(solution)/shard_map/ppermute | solution.py:28
  81.7 11.3 %collective-permute-start.10 = (f32[256,256]{1,0:T(8,128)S(1)}, f32[256,256]{1,0:T(8,128)S(1)}, u32[]{:S(2)}, u32[]{:S(2)}) collective-permute-start(f32[256,256]{1,0:T(8,128)S(1)} %pad_maximum_fusion.5), channel_id=1, source_target_pairs={{0,4},{2,6},{4,0},{6,2},{8,12},{10,14},{12,8},{14,10},{16,20},{18,... | collective-permute-start | bytes 786440 | tf_op jit(solution)/shard_map/ppermute | solution.py:28
  84.0 9.1 %collective-permute-start.8 = (f32[256,256]{1,0:T(8,128)S(1)}, f32[256,256]{1,0:T(8,128)S(1)}, u32[]{:S(2)}, u32[]{:S(2)}) collective-permute-start(f32[256,256]{1,0:T(8,128)S(1)} %pad_maximum_fusion.4), channel_id=1, source_target_pairs={{0,1},{1,0},{2,3},{3,2},{4,5},{5,4},{6,7},{7,6},{8,9},{9,8},{10,11... | collective-permute-start | bytes 786440 | tf_op jit(solution)/shard_map/ppermute | solution.py:28
  93.1 0.7 copy-start.3
  94.9 3.3 %collective-permute-start.11 = (f32[1024,256]{1,0:T(8,128)}, f32[1024,256]{1,0:T(8,128)}, u32[]{:S(2)}, u32[]{:S(2)}) collective-permute-start(f32[1024,256]{1,0:T(8,128)} %pad_maximum_fusion.1), channel_id=1, source_target_pairs={{0,2},{2,0},{4,6},{6,4},{8,10},{10,8},{12,14},{14,12},{16,18},{18,... | collective-permute-start | bytes 3145736 | tf_op jit(solution)/shard_map/ppermute | solution.py:28
  120.7 1.5 copy-start.2
  122.2 41.2 %all-to-all-start.1 = ((f32[16,3,2,16,256]{4,3,2,1,0:T(8,128)}), f32[16,3,2,16,256]{4,3,2,1,0:T(8,128)S(1)}, u32[]{:S(2)}, u32[]{:S(2)}) async-start(f32[16,3,2,16,256]{4,3,2,1,0:T(8,128)} %absorb.2), calls=%async_computation.1 | async-start | bytes 3145728 | tf_op jit(solution)/shard_map/all_to_all | solution.py:263
  163.4 1.1 copy-start
  164.5 63.6 %all-to-all-start.3 = ((f32[16,5,2,16,256]{4,3,2,1,0:T(8,128)}), f32[16,5,2,16,256]{4,3,2,1,0:T(8,128)S(1)}, u32[]{:S(2)}, u32[]{:S(2)}) async-start(f32[16,5,2,16,256]{4,3,2,1,0:T(8,128)} %absorb.3), calls=%async_computation.3 | async-start | bytes 5242880 | tf_op jit(solution)/shard_map/all_to_all | solution.py:263

commit v5 on v4

v5 whole, which is shorter than its diff:
```python
from functools import partial

import jax
import jax.numpy as jnp
from jax import lax
from jax.experimental import pallas as pl
from jax.experimental.pallas import tpu as pltpu
from jax.sharding import PartitionSpec as P

STEPS = 4
MIB = 1024 * 1024
WEIGHT = 4.5
LAST = 48
PER = (1, 2, 3)
DOT = partial(jnp.dot, precision=lax.Precision.HIGHEST)


def build_branch(owned):
    left_real, left_imag = (owned[0, 0], owned[0, 1])
    right_real, right_imag = (owned[1, 0], owned[1, 1])
    return jnp.stack(
        [
            DOT(left_real, right_real) - DOT(left_imag, right_imag),
            DOT(left_real, right_imag) + DOT(left_imag, right_real),
        ]
    )


def swap(array, axis, size, bit):
    return lax.ppermute(array, axis, [(i, i ^ bit) for i in range(size)])


def bits_of(size):
    return [1 << i for i in range(size.bit_length() - 1)]


def halve(held, stage):
    axis, size, index, bit = stage
    half = held.shape[0] // 2
    high = (index & bit) // bit
    keep = lax.dynamic_slice_in_dim(held, high * half, half, 0)
    send = lax.dynamic_slice_in_dim(held, (1 - high) * half, half, 0)
    return keep + swap(send, axis, size, bit)


def double(held, stage):
    axis, size, index, bit = stage
    other = swap(held, axis, size, bit)
    high = (index & bit) != 0
    return jnp.concatenate([jnp.where(high, other, held), jnp.where(high, held, other)], 0)


def broadcast_orders(rows, cols):
    row, col = lax.axis_index("row"), lax.axis_index("col")
    row_bits = bits_of(rows)
    first = [("row", rows, row, b) for b in row_bits[:1]]
    along_col = [("col", cols, col, b) for b in bits_of(cols)]
    along_row = [("row", rows, row, b) for b in row_bits[1:2]]
    return first, (along_col + along_row, along_row + along_col), row_bits[2:]


def scatter_branches(own, owners, rows, cols):
    first, orders, _ = broadcast_orders(rows, cols)
    me = lax.axis_index("row") * cols + lax.axis_index("col")
    mine = (owners == me).reshape(STEPS, 1, 1, 1)
    held = jnp.where(mine, own[None], 0.0).reshape(-1, own.shape[-1])
    for stage in first:
        held = halve(held, stage)
    halves = list(jnp.split(held, 2))
    for at in range(len(orders[0])):
        halves = [halve(part, order[at]) for part, order in zip(halves, orders)]
    return jnp.concatenate(halves, 0)


def gather_branches(held, rows, cols):
    first, orders, _ = broadcast_orders(rows, cols)
    halves = list(jnp.split(held, 2))
    for at in reversed(range(len(orders[0]))):
        halves = [double(part, order[at]) for part, order in zip(halves, orders)]
    held = jnp.concatenate(halves, 0)
    ((axis, size, _, bit),) = first
    width = held.shape[-1]
    shape = (STEPS // 2, 2, width, width)
    return held.reshape(shape), swap(held, axis, size, bit).reshape(shape)


def split(value):
    high = value.astype(jnp.bfloat16)
    low = (value - high.astype(jnp.float32)).astype(jnp.bfloat16)
    return high, low


def stack_branches(core, mine_ref, other_ref, even_ref, odd_ref):
    pair = STEPS // 2
    for step in range(STEPS):
        here = core == step // pair
        real, imag = (jnp.where(here, mine_ref[step % pair, i], other_ref[step % pair, i]) for i in range(2))
        if step % 2:
            real, imag = real.T, imag.T
        axis = 1 if step % 2 else 0
        (rh, rl), (ih, il) = split(real), split(imag)
        to_real = jnp.concatenate([rh, rh, rl, -ih, -ih, -il], axis)
        to_imag = jnp.concatenate([ih, ih, il, rh, rh, rl], axis)
        out = jnp.concatenate([to_real, to_imag], 1 - axis)
        if step % 2:
            odd_ref[step // 2] = out
        else:
            even_ref[step // 2] = out


def absorb_kernel(core_ref, stem_ref, mine_ref, other_ref, cos_ref, sin_ref, out_ref, even_ref, odd_ref):
    width = cos_ref.shape[1]
    items = range(stem_ref.shape[1])

    @pl.when(pl.program_id(0) == 0)
    def _():
        stack_branches(core_ref[0], mine_ref, other_ref, even_ref, odd_ref)

    held = [[stem_ref[:, item, i].reshape(width, width) for i in range(2)] for item in items]
    for step in range(STEPS):
        cosine, sine = cos_ref[step], sin_ref[step]
        for item in items:
            (rh, rl), (ih, il) = split(held[item][0]), split(held[item][1])
            if step % 2 == 0:
                stacked = jnp.concatenate([rh, rl, rh, ih, il, ih], 1)
                both = jnp.dot(stacked, even_ref[step // 2], preferred_element_type=jnp.float32)
                real, imag = both[:, :width], both[:, width:]
            else:
                stacked = jnp.concatenate([rh, rl, rh, ih, il, ih], 0)
                both = jnp.dot(odd_ref[step // 2], stacked, preferred_element_type=jnp.float32)
                real, imag = both[:width], both[width:]
            held[item] = [real * cosine - imag * sine, real * sine + imag * cosine]
    shape = (stem_ref.shape[0], stem_ref.shape[3], width)
    for item in items:
        for i in range(2):
            out_ref[:, item, i] = held[item][i].reshape(shape)


def in_hbm(*arrays):
    return [pltpu.with_memory_space_constraint(array, pltpu.HBM) for array in arrays]


def whole(array):
    return pl.BlockSpec(array.shape, lambda i: (0,) * array.ndim, pipeline_mode=pl.Buffered(1))


def absorb(stem, branches, cosine, sine, start=0, count=None, weight=1):
    peers, items, _, block, width = stem.shape
    count = items if count is None else count
    per = max(n for n in PER if count % n == 0 and start % n == 0)
    shape = (peers, per, 2, block, width)
    in_spec = pl.BlockSpec(shape, lambda i: (0, i + start // per, 0, 0, 0))
    out_spec = pl.BlockSpec(shape, lambda i: (0, i, 0, 0, 0))
    flops = count * STEPS * 12 * 2 * width**3
    core = (lax.axis_index("row") % 2).astype(jnp.int32).reshape(1)
    arrays = in_hbm(stem, *branches, cosine, sine)
    return pl.pallas_call(
        absorb_kernel,
        grid=(count // per,),
        in_specs=[pl.BlockSpec(memory_space=pltpu.SMEM), in_spec, *(whole(array) for array in arrays[1:])],
        out_specs=out_spec,
        out_shape=pltpu.HBM((peers, count, 2, block, width), jnp.float32),
        scratch_shapes=[
            pltpu.VMEM((STEPS // 2, 6 * width, 2 * width), jnp.bfloat16),
            pltpu.VMEM((STEPS // 2, 2 * width, 6 * width), jnp.bfloat16),
        ],
        cost_estimate=pl.CostEstimate(
            flops=int(flops * weight), bytes_accessed=8 * count * (stem.size // items), transcendentals=0
        ),
        compiler_params=pltpu.CompilerParams(vmem_limit_bytes=40 * MIB),
        name="absorb",
    )(core, *arrays)


def row_groups(parts, rows):
    return [(part, row) for part in range(parts) for row in range(0, rows, 8)]


def batch_first_kernel(start, stem_ref, out_ref, held, made, in_sem, out_sem):
    parts, rows = stem_ref.shape[:2]
    peers, items = out_ref.shape[:2]
    ins, outs = [], []
    for g, (part, row) in enumerate(row_groups(parts, rows)):
        ins.append(pltpu.make_async_copy(stem_ref.at[part, pl.ds(row, 8)], held.at[g], in_sem.at[g]))
        outs.append(
            [
                pltpu.make_async_copy(
                    made.at[g, pl.ds(item * peers, peers)],
                    out_ref.at[:, item, part, pl.ds(row, 8), :],
                    out_sem.at[g, item],
                )
                for item in range(items)
            ]
        )
    for copy in ins:
        copy.start()
    for g, copy in enumerate(ins):
        copy.wait()
        for i in range(8):
            made[g, :, i, :] = held[g, i][:, start : start + peers * items].T
        for out in outs[g]:
            out.start()
    for group in outs:
        for copy in group:
            copy.wait()


def batch_first(stem, peers, start, items):
    parts, rows, width, lanes = stem.shape
    groups = parts * rows // 8
    return pl.pallas_call(
        partial(batch_first_kernel, start * peers),
        in_specs=[pl.BlockSpec(memory_space=pl.ANY)],
        out_specs=pl.BlockSpec(memory_space=pl.ANY),
        out_shape=pltpu.HBM((peers, items, parts, rows, width), jnp.float32),
        scratch_shapes=[
            pltpu.VMEM((groups, 8, width, lanes), jnp.float32),
            pltpu.VMEM((groups, peers * items, 8, width), jnp.float32),
            pltpu.SemaphoreType.DMA((groups,)),
            pltpu.SemaphoreType.DMA((groups, items)),
        ],
        cost_estimate=pl.CostEstimate(flops=0, bytes_accessed=8 * stem.size, transcendentals=0),
        compiler_params=pltpu.CompilerParams(vmem_limit_bytes=24 * MIB),
        name="batch_first",
    )(*in_hbm(stem))


def rows_first_kernel(stem_ref, out_ref):
    peers, items = stem_ref.shape[:2]
    for i in range(out_ref.shape[1]):
        for item in range(items):
            out_ref[0, i, item * peers : (item + 1) * peers] = stem_ref[:, item, 0, i, :]


def rows_first(stem, weight):
    peers, items, parts, rows, width = stem.shape
    return pl.pallas_call(
        rows_first_kernel,
        grid=(parts, rows // 8),
        in_specs=[pl.BlockSpec((peers, items, 1, 8, width), lambda p, r: (0, 0, p, r, 0))],
        out_specs=pl.BlockSpec((1, 8, peers * items, width), lambda p, r: (p, r, 0, 0)),
        out_shape=pltpu.HBM((parts, rows, peers * items, width), jnp.float32),
        cost_estimate=pl.CostEstimate(flops=int(1e9 * weight), bytes_accessed=8 * stem.size, transcendentals=0),
        compiler_params=pltpu.CompilerParams(vmem_limit_bytes=24 * MIB),
        name="rows_first",
    )(*in_hbm(stem))


def batch_last_kernel(low_ref, *refs):
    *others, out_ref, low, made, low_sem, out_sem = refs
    parts, rows = out_ref.shape[:2]
    ins, outs = [], []
    for g, (part, row) in enumerate(row_groups(parts, rows)):
        ins.append(pltpu.make_async_copy(low_ref.at[part, pl.ds(row, 8)], low.at[g], low_sem.at[g]))
        outs.append(pltpu.make_async_copy(made.at[g], out_ref.at[part, pl.ds(row, 8)], out_sem.at[g]))
    for copy in ins:
        copy.start()
    for g, (part, row) in enumerate(row_groups(parts, rows)):
        ins[g].wait()
        for i in range(8):
            found = [ref[:, item, part, row + i, :] for ref in others for item in range(ref.shape[1])]
            made[g, i] = jnp.concatenate([low[g, i], *found], 0).T
        outs[g].start()
    for copy in outs:
        copy.wait()


def batch_last(low, *others):
    parts, rows, batch, width = low.shape
    lanes = batch + sum(other.shape[0] * other.shape[1] for other in others)
    groups = parts * rows // 8
    return pl.pallas_call(
        batch_last_kernel,
        in_specs=[pl.BlockSpec(memory_space=pl.ANY)] + [pl.BlockSpec(memory_space=pltpu.VMEM)] * len(others),
        out_specs=pl.BlockSpec(memory_space=pl.ANY),
        out_shape=jax.ShapeDtypeStruct((parts, rows, width, lanes), jnp.float32),
        scratch_shapes=[
            pltpu.VMEM((groups, 8, batch, width), jnp.float32),
            pltpu.VMEM((groups, 8, width, lanes), jnp.float32),
            pltpu.SemaphoreType.DMA((groups,)),
            pltpu.SemaphoreType.DMA((groups,)),
        ],
        compiler_params=pltpu.CompilerParams(vmem_limit_bytes=24 * MIB),
        name="batch_last",
    )(*in_hbm(low), *others)


def exchange(parts):
    return lax.all_to_all(parts, "row", 0, 0, tiled=True)


def pair_cores(parts):
    rows = parts.shape[0]
    core = lax.axis_index("row") % 2
    chips = parts.reshape(rows // 2, 2, *parts.shape[1:])
    same = lax.dynamic_index_in_dim(chips, core, 1, keepdims=False)
    other = lax.dynamic_index_in_dim(chips, 1 - core, 1, keepdims=False)
    other = swap(other, "row", rows, 1)
    return jnp.stack([jnp.where(core == 0, same, other), jnp.where(core == 0, other, same)], 1)


def send_chips(parts):
    rows = parts.shape[0]
    chip = lax.axis_index("row") // 2
    pairs = pair_cores(parts)
    pieces = {}
    for bit in reversed(range(1, rows // 2)):
        pieces[bit] = swap(lax.dynamic_index_in_dim(pairs, chip ^ bit, 0), "row", rows, 2 * bit)
    return pairs, pieces


def collect_chips(pairs, pieces):
    chip = lax.axis_index("row") // 2
    for bit, piece in pieces.items():
        pairs = lax.dynamic_update_index_in_dim(pairs, piece, chip ^ bit, 0)
    return pairs.reshape(-1, *pairs.shape[2:])


def on_device(stem_slab, factors, branch_owner, entangle_phase, *, rows, cols):
    items = stem_slab.shape[3] // rows
    low = max(1, items * 3 // 8)
    high = items - low
    sent_low = batch_first(stem_slab, rows, 0, low)
    sent_low, factors = lax.optimization_barrier((sent_low, factors))
    stem_low = exchange(sent_low)
    held = scatter_branches(build_branch(factors[0]), branch_owner, rows, cols)
    cosine, sine = jnp.cos(entangle_phase), jnp.sin(entangle_phase)
    far = broadcast_orders(rows, cols)[2]
    for bit in far[:-1]:
        held = held + swap(held, "row", rows, bit)
    sent_high = batch_first(stem_slab, rows, low, high)
    held, sent_high, cosine, sine = lax.optimization_barrier((held, sent_high, cosine, sine))
    for bit in far[-1:]:
        held = held + swap(held, "row", rows, bit)
    stem_high = exchange(sent_high)
    branches = gather_branches(held, rows, cols)
    back_low = exchange(absorb(stem_low, branches, cosine, sine, weight=WEIGHT))
    pairs, pieces = send_chips(absorb(stem_high, branches, cosine, sine, high - 1, 1))
    back_high = exchange(absorb(stem_high, branches, cosine, sine, 0, high - 1))
    order = list(pieces)
    back_low, *came = lax.optimization_barrier((back_low, *[pieces[bit] for bit in order]))
    back_some = collect_chips(pairs, dict(zip(order, came)))
    return batch_last(rows_first(back_low, LAST), back_high, back_some)


def solution(mesh):
    return jax.shard_map(
        partial(on_device, rows=mesh.shape["row"], cols=mesh.shape["col"]),
        mesh=mesh,
        in_specs=(P(None, "row", None, "col"), P(("row", "col"), None, None, None, None), P(), P()),
        out_specs=P(None, "row", None, "col"),
        check_vma=False,
    )
```

time: 232 us -> 225 us (0.970)
  waiting for transfers between devices: 132 us -> 122 us
  starting transfers between devices: 36.6 us -> 46.3 us
  Pallas kernels: 47.3 us -> 43.1 us
    all_to_all x4, waiting for transfers between devices: 78.8 us -> 68.3 us  [exchange(): return lax.all_to_all(parts, 'row', 0, 0, tiled=True)]
    ppermute x12 -> x20, starting transfers between devices: 14.7 us -> 24.9 us  [swap(): return lax.ppermute(array, axis, [(i, i ^ bit) for i in range(size)])]
    pallas_call x4 -> x5, Pallas kernels: 40 us -> 35.8 us  [the longest x3 27.3 us: absorb(): pl.pallas_call(absorb_kernel, grid=(count // per,), in_specs=[pl.BlockSpe...]
    unnamed x12 -> x8, local copies, waits for them, and re-layouts: 3.33 us -> 0.02 us
    ppermute x12 -> x20, waiting for transfers between devices: 52.9 us -> 53.9 us  [swap(): return lax.ppermute(array, axis, [(i, i ^ bit) for i in range(size)])]
  transfers between devices with their start and end apart: 16 -> 24, of which waited for: 11 -> 12; matrix products, arithmetic and copies ran while one was open for 4% -> 4% of each run, Pallas kernels for 17% -> 16%
where the time goes in v5:
time: 225 us; the launch traced here: 224 us
  waiting for transfers between devices  122 us (54%)
  starting transfers between devices  46.3 us (21%)
  Pallas kernels  43.1 us (19%)
  local copies, waits for them, and re-layouts  5.9 us (3%)
  other arithmetic  4.31 us (2%)
    all_to_all x4, waiting for transfers between devices, exchange(): return lax.all_to_all(parts, 'row', 0, 0, tiled=True)  68.3 us
    ppermute x20, waiting for transfers between devices, swap(): return lax.ppermute(array, axis, [(i, i ^ bit) for i in range(size)])  53.9 us
    pallas_call x3, Pallas kernels, absorb(): pl.pallas_call(absorb_kernel, grid=(count // per,), in_specs=[pl.BlockSpe...  27.3 us
    ppermute x20, starting transfers between devices, swap(): return lax.ppermute(array, axis, [(i, i ^ bit) for i in range(size)])  24.9 us
    all_to_all x4, starting transfers between devices, exchange(): return lax.all_to_all(parts, 'row', 0, 0, tiled=True)  21.4 us
    pallas_call x2, Pallas kernels, batch_first(): pl.pallas_call(partial(batch_first_kernel, start * peers), in_specs=[pl.B...  8.42 us
  transfers between devices with their start and end apart: 24, of which 12 were waited for; matrix products, arithmetic and copies ran while one was open for 4% of the time, Pallas kernels for 16%

profile of v5, /device:TPU:13, one launch (start us, length us, event | category | flops | bytes accessed | tf_op | source)
XLA Modules:
  0.0 224.0 jit_solution(9596221252619613783)
XLA Ops:
  0.0 3.6 %batch_first.2 = f32[16,3,2,16,256]{4,3,2,1,0:T(8,128)} custom-call(f32[2,16,256,128]{3,2,1,0:T(8,128)} %stem_ref.3), custom_call_target="tpu_custom_call" | custom-call | bytes 8388608 | tf_op jit(solution)/shard_map/batch_first/pallas_call | solution.py:211
  6.5 6.0 %all-to-all-start = ((f32[16,3,2,16,256]{4,3,2,1,0:T(8,128)}), f32[16,3,2,16,256]{4,3,2,1,0:T(8,128)}, u32[]{:S(2)}, u32[]{:S(2)}) async-start(f32[16,3,2,16,256]{4,3,2,1,0:T(8,128)} %batch_first.2), calls=%async_computation | async-start | bytes 3145728 | tf_op jit(solution)/shard_map/all_to_all | solution.py:289
  12.5 1.4 dynamic-slice_add_fusion
  14.3 4.8 %batch_first.3 = f32[16,5,2,16,256]{4,3,2,1,0:T(8,128)} custom-call(f32[2,16,256,128]{3,2,1,0:T(8,128)} %stem_ref.3), custom_call_target="tpu_custom_call" | custom-call | bytes 8388608 | tf_op jit(solution)/shard_map/batch_first/pallas_call | solution.py:211
  19.2 1.3 collective-permute-start.1
  20.5 7.4 %collective-permute-done.3 = f32[256,256]{1,0:T(8,128)S(1)} collective-permute-done((f32[256,256]{1,0:T(8,128)S(1)}, f32[256,256]{1,0:T(8,128)S(1)}, u32[]{:S(2)}, u32[]{:S(2)}) %collective-permute-start.3) | collective-permute-done | bytes 262176 | tf_op jit(solution)/shard_map/ppermute | solution.py:30
  28.0 1.3 collective-permute-start.4
  29.3 2.3 %collective-permute-start.2 = (f32[128,256]{1,0:T(8,128)S(1)}, f32[128,256]{1,0:T(8,128)S(1)}, u32[]{:S(2)}, u32[]{:S(2)}) collective-permute-start(f32[128,256]{1,0:T(8,128)S(1)} %constant_dynamic-slice_fusion.2), channel_id=1, source_target_pairs={{0,4},{2,6},{4,0},{6,2},{8,12},{10,14},{12,8},{14,10},{16,20},{18,... | collective-permute-start | bytes 393224 | tf_op jit(solution)/shard_map/ppermute | solution.py:30
  32.3 2.3 %collective-permute-done.2 = f32[128,256]{1,0:T(8,128)S(1)} collective-permute-done((f32[128,256]{1,0:T(8,128)S(1)}, f32[128,256]{1,0:T(8,128)S(1)}, u32[]{:S(2)}, u32[]{:S(2)}) %collective-permute-start.2) | collective-permute-done | bytes 131104 | tf_op jit(solution)/shard_map/ppermute | solution.py:30
  34.6 3.7 %collective-permute-start.5 = (f32[256,256]{1,0:T(8,128)S(1)}, f32[256,256]{1,0:T(8,128)S(1)}, u32[]{:S(2)}, u32[]{:S(2)}) collective-permute-start(f32[256,256]{1,0:T(8,128)S(1)} %pad_maximum_fusion.3), channel_id=1, source_target_pairs={{0,8},{2,10},{4,12},{6,14},{8,0},{10,2},{12,4},{14,6},{16,24},{18,... | collective-permute-start | bytes 786440 | tf_op jit(solution)/shard_map/ppermute | solution.py:30
  38.3 4.5 %fusion.14 = (f32[4,256,256]{2,1,0:T(8,128)}, f32[4,256,256]{2,1,0:T(8,128)}) fusion(f32[4,256,256]{2,1,0:T(8,128)S(1)} %copy-done.2), kind=kLoop, calls=%fused_computation.70 | loop fusion | bytes 3145728 | tf_op jit(solution)/shard_map/sin | solution.py:327
  42.8 6.5 %collective-permute-done.5 = f32[256,256]{1,0:T(8,128)S(1)} collective-permute-done((f32[256,256]{1,0:T(8,128)S(1)}, f32[256,256]{1,0:T(8,128)S(1)}, u32[]{:S(2)}, u32[]{:S(2)}) %collective-permute-start.5) | collective-permute-done | bytes 262176 | tf_op jit(solution)/shard_map/ppermute | solution.py:30
  49.4 1.9 collective-permute-start.6
  51.2 5.9 %all-to-all-start.2 = ((f32[16,5,2,16,256]{4,3,2,1,0:T(8,128)}), f32[16,5,2,16,256]{4,3,2,1,0:T(8,128)S(1)}, u32[]{:S(2)}, u32[]{:S(2)}) async-start(f32[16,5,2,16,256]{4,3,2,1,0:T(8,128)} %batch_first.3), calls=%async_computation.2 | async-start | bytes 5242880 | tf_op jit(solution)/shard_map/all_to_all | solution.py:289
  57.2 19.7 %collective-permute-done.6 = f32[256,256]{1,0:T(8,128)S(1)} collective-permute-done((f32[256,256]{1,0:T(8,128)S(1)}, f32[256,256]{1,0:T(8,128)S(1)}, u32[]{:S(2)}, u32[]{:S(2)}) %collective-permute-start.6) | collective-permute-done | bytes 262176 | tf_op jit(solution)/shard_map/ppermute | solution.py:30
  77.1 4.6 %collective-permute-done.7 = f32[128,256]{1,0:T(8,128)S(1)} collective-permute-done((f32[128,256]{1,0:T(8,128)S(1)}, f32[128,256]{1,0:T(8,128)S(1)}, u32[]{:S(2)}, u32[]{:S(2)}) %collective-permute-start.7) | collective-permute-done | bytes 131104 | tf_op jit(solution)/shard_map/ppermute | solution.py:30
  81.8 2.3 %collective-permute-start.10 = (f32[256,256]{1,0:T(8,128)S(1)}, f32[256,256]{1,0:T(8,128)S(1)}, u32[]{:S(2)}, u32[]{:S(2)}) collective-permute-start(f32[256,256]{1,0:T(8,128)S(1)} %pad_maximum_fusion.5), channel_id=1, source_target_pairs={{0,4},{2,6},{4,0},{6,2},{8,12},{10,14},{12,8},{14,10},{16,20},{18,... | collective-permute-start | bytes 786440 | tf_op jit(solution)/shard_map/ppermute | solution.py:30
  84.2 9.0 %collective-permute-done.10 = f32[256,256]{1,0:T(8,128)S(1)} collective-permute-done((f32[256,256]{1,0:T(8,128)S(1)}, f32[256,256]{1,0:T(8,128)S(1)}, u32[]{:S(2)}, u32[]{:S(2)}) %collective-permute-start.10) | collective-permute-done | bytes 262176 | tf_op jit(solution)/shard_map/ppermute | solution.py:30
  95.1 2.6 %collective-permute-done.11 = f32[1024,256]{1,0:T(8,128)} collective-permute-done((f32[1024,256]{1,0:T(8,128)}, f32[1024,256]{1,0:T(8,128)}, u32[]{:S(2)}, u32[]{:S(2)}) %collective-permute-start.11) | collective-permute-done | bytes 1048608 | tf_op jit(solution)/shard_map/ppermute | solution.py:30
  97.7 9.2 %absorb.3 = f32[16,3,2,16,256]{4,3,2,1,0:T(8,128)} custom-call(s32[1]{0:T(128)} %bitcast.core_ref, f32[16,3,2,16,256]{4,3,2,1,0:T(8,128)} %all-to-all-done.stem_ref, f32[2,2,256,256]{3,2,1,0:T(8,128)} %bitcast.9.mine_ref, f32[2,2,256,256]{3,2,1,0:T(8,128)} %bitcast.10.other_ref, f32[4,256,256]{2,1,0:T(8,128)} %get-tuple-element.22.cos_ref, ...), custom_call_target="tpu_custom_call" | custom-call | flops 21743271936 | bytes 3145728 | tf_op jit(solution)/shard_map/absorb/pallas_call | solution.py:157
  106.9 13.8 %all-to-all-done.2.stem_ref = f32[16,5,2,16,256]{4,3,2,1,0:T(8,128)S(1)} async-done(((f32[16,5,2,16,256]{4,3,2,1,0:T(8,128)}), f32[16,5,2,16,256]{4,3,2,1,0:T(8,128)S(1)}, u32[]{:S(2)}, u32[]{:S(2)}) %all-to-all-start.2) | async-done | bytes 2621472 | tf_op jit(solution)/shard_map/all_to_all | solution.py:289
  120.8 4.9 %all-to-all-start.1 = ((f32[16,3,2,16,256]{4,3,2,1,0:T(8,128)}), f32[16,3,2,16,256]{4,3,2,1,0:T(8,128)}, u32[]{:S(2)}, u32[]{:S(2)}) async-start(f32[16,3,2,16,256]{4,3,2,1,0:T(8,128)} %absorb.3), calls=%async_computation.1 | async-start | bytes 3145728 | tf_op jit(solution)/shard_map/all_to_all | solution.py:289
  125.6 6.1 %absorb.4 = f32[16,1,2,16,256]{4,3,2,1,0:T(8,128)} custom-call(s32[1]{0:T(128)} %bitcast.core_ref, f32[16,5,2,16,256]{4,3,2,1,0:T(8,128)} %copy-done, f32[2,2,256,256]{3,2,1,0:T(8,128)} %bitcast.9.mine_ref, f32[2,2,256,256]{3,2,1,0:T(8,128)} %bitcast.10.other_ref, f32[4,256,256]{2,1,0:T(8,128)} %get-tuple-element.22.cos_ref, ...), custom_call_target="tpu_custom_call" | custom-call | flops 1610612736 | bytes 1048576 | tf_op jit(solution)/shard_map/absorb/pallas_call | solution.py:157
  135.9 12.0 %absorb.5 = f32[16,4,2,16,256]{4,3,2,1,0:T(8,128)} custom-call(s32[1]{0:T(128)} %bitcast.core_ref, f32[16,5,2,16,256]{4,3,2,1,0:T(8,128)} %copy-done, f32[2,2,256,256]{3,2,1,0:T(8,128)} %bitcast.9.mine_ref, f32[2,2,256,256]{3,2,1,0:T(8,128)} %bitcast.10.other_ref, f32[4,256,256]{2,1,0:T(8,128)} %get-tuple-element.22.cos_ref, ...), custom_call_target="tpu_custom_call" | custom-call | flops 6442450944 | bytes 4194304 | tf_op jit(solution)/shard_map/absorb/pallas_call | solution.py:157
  147.9 3.2 %collective-permute-start.13 = (f32[1,2,1,2,16,256]{5,4,3,1,0,2:T(8,128)S(1)}, f32[1,2,1,2,16,256]{5,4,3,1,0,2:T(8,128)S(1)}, u32[]{:S(2)}, u32[]{:S(2)}) collective-permute-start(f32[1,2,1,2,16,256]{5,4,3,1,0,2:T(8,128)S(1)} %get-tuple-element.40), channel_id=1, source_target_pairs={{0,28},{2,30},{4,24},{6,26},{8,20},{10,22},{12,16},{14,18},{16,12}... | collective-permute-start | bytes 196616 | tf_op jit(solution)/shard_map/ppermute | solution.py:30
  151.1 3.4 %collective-permute-start.15 = (f32[1,2,1,2,16,256]{5,4,3,1,0,2:T(8,128)S(1)}, f32[1,2,1,2,16,256]{5,4,3,1,0,2:T(8,128)S(1)}, u32[]{:S(2)}, u32[]{:S(2)}) collective-permute-start(f32[1,2,1,2,16,256]{5,4,3,1,0,2:T(8,128)S(1)} %get-tuple-element.42), channel_id=1, source_target_pairs={{0,20},{2,22},{4,16},{6,18},{8,28},{10,30},{12,24},{14,26},{16,4},... | collective-permute-start | bytes 196616 | tf_op jit(solution)/shard_map/ppermute | solution.py:30
  154.9 2.2 collective-permute-start.17
  157.1 11.1 %all-to-all-done.1.stem_ref = f32[16,3,2,16,256]{4,3,2,1,0:T(8,128)} async-done(((f32[16,3,2,16,256]{4,3,2,1,0:T(8,128)}), f32[16,3,2,16,256]{4,3,2,1,0:T(8,128)}, u32[]{:S(2)}, u32[]{:S(2)}) %all-to-all-start.1) | async-done | bytes 1572896 | tf_op jit(solution)/shard_map/all_to_all | solution.py:289
  168.2 4.6 %all-to-all-start.3 = ((f32[16,4,2,16,256]{4,3,2,1,0:T(8,128)}), f32[16,4,2,16,256]{4,3,2,1,0:T(8,128)S(1)}, u32[]{:S(2)}, u32[]{:S(2)}) async-start(f32[16,4,2,16,256]{4,3,2,1,0:T(8,128)} %absorb.5), calls=%async_computation.3 | async-start | bytes 4194304 | tf_op jit(solution)/shard_map/all_to_all | solution.py:289
  173.0 3.8 %rows_first.1.low_ref = f32[2,16,48,256]{3,2,1,0:T(8,128)} custom-call(f32[16,3,2,16,256]{4,3,2,1,0:T(8,128)} %all-to-all-done.1.stem_ref), custom_call_target="tpu_custom_call" | custom-call | flops 48000000000 | bytes 3145728 | tf_op jit(solution)/shard_map/rows_first/pallas_call | solution.py:237
  176.8 43.4 %all-to-all-done.3.refs_0_ = f32[16,4,2,16,256]{4,3,2,1,0:T(8,128)S(1)} async-done(((f32[16,4,2,16,256]{4,3,2,1,0:T(8,128)}), f32[16,4,2,16,256]{4,3,2,1,0:T(8,128)S(1)}, u32[]{:S(2)}, u32[]{:S(2)}) %all-to-all-start.3) | async-done | bytes 2097184 | tf_op jit(solution)/shard_map/all_to_all | solution.py:289
  220.3 3.5 %batch_last.1 = f32[2,16,256,128]{3,2,1,0:T(8,128)} custom-call(f32[2,16,48,256]{3,2,1,0:T(8,128)} %rows_first.1.low_ref, f32[16,4,2,16,256]{4,3,2,1,0:T(8,128)S(1)} %all-to-all-done.3.refs_0_, f32[16,1,2,16,256]{4,3,2,1,0:T(8,128)S(1)} %bitcast.43), custom_call_target="tpu_custom_call" | custom-call | tf_op jit(solution)/shard_map/batch_last/pallas_call | solution.py:272
  (74 shorter events, 11.1 us)
Async XLA Ops:
  0.0 3.6 %copy-start.1 = (f32[1,2,2,256,256]{4,3,2,1,0:T(8,128)S(1)}, f32[1,2,2,256,256]{4,3,2,1,0:T(8,128)}, u32[]{:S(2)}) copy-start(f32[1,2,2,256,256]{4,3,2,1,0:T(8,128)} %param.5) | copy-start | bytes 3145732
  0.0 4.4 %copy-start.3 = (s32[4]{0:T(128)S(1)}, s32[4]{0:T(128)}, u32[]{:S(2)}) copy-start(s32[4]{0:T(128)} %param.6) | copy-start | bytes 52
  5.8 6.7 %collective-permute-start = (f32[1024,256]{1,0:T(8,128)S(1)}, f32[1024,256]{1,0:T(8,128)}, u32[]{:S(2)}, u32[]{:S(2)}) collective-permute-start(f32[1024,256]{1,0:T(8,128)S(1)} %constant_dynamic-slice_fusion.4), channel_id=1, source_target_pairs={{0,2},{2,0},{4,6},{6,4},{8,10},{10,8},{12,14},{14,12},{16,18},{18,... | collective-permute-start | bytes 3145736 | tf_op jit(solution)/shard_map/ppermute | solution.py:30
  6.5 44.7 %all-to-all-start = ((f32[16,3,2,16,256]{4,3,2,1,0:T(8,128)}), f32[16,3,2,16,256]{4,3,2,1,0:T(8,128)}, u32[]{:S(2)}, u32[]{:S(2)}) async-start(f32[16,3,2,16,256]{4,3,2,1,0:T(8,128)} %batch_first.2), calls=%async_computation | async-start | bytes 3145728 | tf_op jit(solution)/shard_map/all_to_all | solution.py:289
  14.0 13.9 %collective-permute-start.3 = (f32[256,256]{1,0:T(8,128)S(1)}, f32[256,256]{1,0:T(8,128)S(1)}, u32[]{:S(2)}, u32[]{:S(2)}) collective-permute-start(f32[256,256]{1,0:T(8,128)S(1)} %constant_dynamic-slice_fusion.1), channel_id=1, source_target_pairs={{0,4},{2,6},{4,0},{6,2},{8,12},{10,14},{12,8},{14,10},{16,20},{18,... | collective-permute-start | bytes 786440 | tf_op jit(solution)/shard_map/ppermute | solution.py:30
  19.2 19.1 %copy-start.2 = (f32[4,256,256]{2,1,0:T(8,128)S(1)}, f32[4,256,256]{2,1,0:T(8,128)}, u32[]{:S(2)}) copy-start(f32[4,256,256]{2,1,0:T(8,128)} %param.7) | copy-start | bytes 3145732
  19.2 10.0 %collective-permute-start.1 = (f32[256,256]{1,0:T(8,128)S(1)}, f32[256,256]{1,0:T(8,128)S(1)}, u32[]{:S(2)}, u32[]{:S(2)}) collective-permute-start(f32[256,256]{1,0:T(8,128)S(1)} %constant_dynamic-slice_fusion.3), channel_id=1, source_target_pairs={{0,1},{1,0},{2,3},{3,2},{4,5},{5,4},{6,7},{7,6},{8,9},{9,8},{10,11... | collective-permute-start | bytes 786440 | tf_op jit(solution)/shard_map/ppermute | solution.py:30
  28.0 4.3 %collective-permute-start.4 = (f32[128,256]{1,0:T(8,128)S(1)}, f32[128,256]{1,0:T(8,128)S(1)}, u32[]{:S(2)}, u32[]{:S(2)}) collective-permute-start(f32[128,256]{1,0:T(8,128)S(1)} %constant_dynamic-slice_fusion), channel_id=1, source_target_pairs={{0,1},{1,0},{2,3},{3,2},{4,5},{5,4},{6,7},{7,6},{8,9},{9,8},{10,11... | collective-permute-start | bytes 393224 | tf_op jit(solution)/shard_map/ppermute | solution.py:30
  29.3 5.2 %collective-permute-start.2 = (f32[128,256]{1,0:T(8,128)S(1)}, f32[128,256]{1,0:T(8,128)S(1)}, u32[]{:S(2)}, u32[]{:S(2)}) collective-permute-start(f32[128,256]{1,0:T(8,128)S(1)} %constant_dynamic-slice_fusion.2), channel_id=1, source_target_pairs={{0,4},{2,6},{4,0},{6,2},{8,12},{10,14},{12,8},{14,10},{16,20},{18,... | collective-permute-start | bytes 393224 | tf_op jit(solution)/shard_map/ppermute | solution.py:30
  34.6 14.7 %collective-permute-start.5 = (f32[256,256]{1,0:T(8,128)S(1)}, f32[256,256]{1,0:T(8,128)S(1)}, u32[]{:S(2)}, u32[]{:S(2)}) collective-permute-start(f32[256,256]{1,0:T(8,128)S(1)} %pad_maximum_fusion.3), channel_id=1, source_target_pairs={{0,8},{2,10},{4,12},{6,14},{8,0},{10,2},{12,4},{14,6},{16,24},{18,... | collective-permute-start | bytes 786440 | tf_op jit(solution)/shard_map/ppermute | solution.py:30
  49.4 27.5 %collective-permute-start.6 = (f32[256,256]{1,0:T(8,128)S(1)}, f32[256,256]{1,0:T(8,128)S(1)}, u32[]{:S(2)}, u32[]{:S(2)}) collective-permute-start(f32[256,256]{1,0:T(8,128)S(1)} %fusion.13), channel_id=1, source_target_pairs={{0,16},{2,18},{4,20},{6,22},{8,24},{10,26},{12,28},{14,30},{16,0},... | collective-permute-start | bytes 786440 | tf_op jit(solution)/shard_map/ppermute | solution.py:30
  51.2 69.5 %all-to-all-start.2 = ((f32[16,5,2,16,256]{4,3,2,1,0:T(8,128)}), f32[16,5,2,16,256]{4,3,2,1,0:T(8,128)S(1)}, u32[]{:S(2)}, u32[]{:S(2)}) async-start(f32[16,5,2,16,256]{4,3,2,1,0:T(8,128)} %batch_first.3), calls=%async_computation.2 | async-start | bytes 5242880 | tf_op jit(solution)/shard_map/all_to_all | solution.py:289
  77.0 4.8 %collective-permute-start.7 = (f32[128,256]{1,0:T(8,128)S(1)}, f32[128,256]{1,0:T(8,128)S(1)}, u32[]{:S(2)}, u32[]{:S(2)}) collective-permute-start(f32[128,256]{1,0:T(8,128)S(1)} %get-tuple-element.55), channel_id=1, source_target_pairs={{0,4},{2,6},{4,0},{6,2},{8,12},{10,14},{12,8},{14,10},{16,20},{18,... | collective-permute-start | bytes 393224 | tf_op jit(solution)/shard_map/ppermute | solution.py:30
  77.0 4.7 %collective-permute-start.9 = (f32[128,256]{1,0:T(8,128)S(1)}, f32[128,256]{1,0:T(8,128)S(1)}, u32[]{:S(2)}, u32[]{:S(2)}) collective-permute-start(f32[128,256]{1,0:T(8,128)S(1)} %get-tuple-element.56), channel_id=1, source_target_pairs={{0,1},{1,0},{2,3},{3,2},{4,5},{5,4},{6,7},{7,6},{8,9},{9,8},{10,11... | collective-permute-start | bytes 393224 | tf_op jit(solution)/shard_map/ppermute | solution.py:30
  81.8 11.3 %collective-permute-start.10 = (f32[256,256]{1,0:T(8,128)S(1)}, f32[256,256]{1,0:T(8,128)S(1)}, u32[]{:S(2)}, u32[]{:S(2)}) collective-permute-start(f32[256,256]{1,0:T(8,128)S(1)} %pad_maximum_fusion.5), channel_id=1, source_target_pairs={{0,4},{2,6},{4,0},{6,2},{8,12},{10,14},{12,8},{14,10},{16,20},{18,... | collective-permute-start | bytes 786440 | tf_op jit(solution)/shard_map/ppermute | solution.py:30
  84.1 9.1 %collective-permute-start.8 = (f32[256,256]{1,0:T(8,128)S(1)}, f32[256,256]{1,0:T(8,128)S(1)}, u32[]{:S(2)}, u32[]{:S(2)}) collective-permute-start(f32[256,256]{1,0:T(8,128)S(1)} %pad_maximum_fusion.4), channel_id=1, source_target_pairs={{0,1},{1,0},{2,3},{3,2},{4,5},{5,4},{6,7},{7,6},{8,9},{9,8},{10,11... | collective-permute-start | bytes 786440 | tf_op jit(solution)/shard_map/ppermute | solution.py:30
  94.4 3.3 %collective-permute-start.11 = (f32[1024,256]{1,0:T(8,128)}, f32[1024,256]{1,0:T(8,128)}, u32[]{:S(2)}, u32[]{:S(2)}) collective-permute-start(f32[1024,256]{1,0:T(8,128)} %pad_maximum_fusion.1), channel_id=1, source_target_pairs={{0,2},{2,0},{4,6},{6,4},{8,10},{10,8},{12,14},{14,12},{16,18},{18,... | collective-permute-start | bytes 3145736 | tf_op jit(solution)/shard_map/ppermute | solution.py:30
  120.8 4.9 %copy-start = (f32[16,5,2,16,256]{4,3,2,1,0:T(8,128)}, f32[16,5,2,16,256]{4,3,2,1,0:T(8,128)S(1)}, u32[]{:S(2)}) copy-start(f32[16,5,2,16,256]{4,3,2,1,0:T(8,128)S(1)} %all-to-all-done.2.stem_ref) | copy-start | bytes 7864324
  120.8 47.4 %all-to-all-start.1 = ((f32[16,3,2,16,256]{4,3,2,1,0:T(8,128)}), f32[16,3,2,16,256]{4,3,2,1,0:T(8,128)}, u32[]{:S(2)}, u32[]{:S(2)}) async-start(f32[16,3,2,16,256]{4,3,2,1,0:T(8,128)} %absorb.3), calls=%async_computation.1 | async-start | bytes 3145728 | tf_op jit(solution)/shard_map/all_to_all | solution.py:289
  132.7 1.6 collective-permute-start.12
  135.4 19.1 %collective-permute-start.18 = (f32[1,2,1,2,16,256]{5,4,3,1,0,2:T(8,128)S(1)}, f32[1,2,1,2,16,256]{5,4,3,1,0,2:T(8,128)S(1)}, u32[]{:S(2)}, u32[]{:S(2)}) collective-permute-start(f32[1,2,1,2,16,256]{5,4,3,1,0,2:T(8,128)S(1)} %fusion.11), channel_id=1, source_target_pairs={{0,8},{2,10},{4,12},{6,14},{8,0},{10,2},{12,4},{14,6},{16,24},{18,... | collective-permute-start | bytes 196616 | tf_op jit(solution)/shard_map/ppermute | solution.py:30
  135.7 19.2 %collective-permute-start.19 = (f32[1,2,1,2,16,256]{5,4,3,1,0,2:T(8,128)S(1)}, f32[1,2,1,2,16,256]{5,4,3,1,0,2:T(8,128)S(1)}, u32[]{:S(2)}, u32[]{:S(2)}) collective-permute-start(f32[1,2,1,2,16,256]{5,4,3,1,0,2:T(8,128)S(1)} %get-tuple-element.39), channel_id=1, source_target_pairs={{0,4},{2,6},{4,0},{6,2},{8,12},{10,14},{12,8},{14,10},{16,20},{18,... | collective-permute-start | bytes 196616 | tf_op jit(solution)/shard_map/ppermute | solution.py:30
  147.9 25.0 %collective-permute-start.13 = (f32[1,2,1,2,16,256]{5,4,3,1,0,2:T(8,128)S(1)}, f32[1,2,1,2,16,256]{5,4,3,1,0,2:T(8,128)S(1)}, u32[]{:S(2)}, u32[]{:S(2)}) collective-permute-start(f32[1,2,1,2,16,256]{5,4,3,1,0,2:T(8,128)S(1)} %get-tuple-element.40), channel_id=1, source_target_pairs={{0,28},{2,30},{4,24},{6,26},{8,20},{10,22},{12,16},{14,18},{16,12}... | collective-permute-start | bytes 196616 | tf_op jit(solution)/shard_map/ppermute | solution.py:30
  151.1 21.8 %collective-permute-start.14 = (f32[1,2,1,2,16,256]{5,4,3,1,0,2:T(8,128)S(1)}, f32[1,2,1,2,16,256]{5,4,3,1,0,2:T(8,128)S(1)}, u32[]{:S(2)}, u32[]{:S(2)}) collective-permute-start(f32[1,2,1,2,16,256]{5,4,3,1,0,2:T(8,128)S(1)} %get-tuple-element.41), channel_id=1, source_target_pairs={{0,24},{2,26},{4,28},{6,30},{8,16},{10,18},{12,20},{14,22},{16,8},... | collective-permute-start | bytes 196616 | tf_op jit(solution)/shard_map/ppermute | solution.py:30
  151.1 21.8 %collective-permute-start.15 = (f32[1,2,1,2,16,256]{5,4,3,1,0,2:T(8,128)S(1)}, f32[1,2,1,2,16,256]{5,4,3,1,0,2:T(8,128)S(1)}, u32[]{:S(2)}, u32[]{:S(2)}) collective-permute-start(f32[1,2,1,2,16,256]{5,4,3,1,0,2:T(8,128)S(1)} %get-tuple-element.42), channel_id=1, source_target_pairs={{0,20},{2,22},{4,16},{6,18},{8,28},{10,30},{12,24},{14,26},{16,4},... | collective-permute-start | bytes 196616 | tf_op jit(solution)/shard_map/ppermute | solution.py:30
  154.5 18.4 %collective-permute-start.16 = (f32[1,2,1,2,16,256]{5,4,3,1,0,2:T(8,128)S(1)}, f32[1,2,1,2,16,256]{5,4,3,1,0,2:T(8,128)S(1)}, u32[]{:S(2)}, u32[]{:S(2)}) collective-permute-start(f32[1,2,1,2,16,256]{5,4,3,1,0,2:T(8,128)S(1)} %get-tuple-element.43), channel_id=1, source_target_pairs={{0,16},{2,18},{4,20},{6,22},{8,24},{10,26},{12,28},{14,30},{16,0},... | collective-permute-start | bytes 196616 | tf_op jit(solution)/shard_map/ppermute | solution.py:30
  154.9 18.0 %collective-permute-start.17 = (f32[1,2,1,2,16,256]{5,4,3,1,0,2:T(8,128)S(1)}, f32[1,2,1,2,16,256]{5,4,3,1,0,2:T(8,128)S(1)}, u32[]{:S(2)}, u32[]{:S(2)}) collective-permute-start(f32[1,2,1,2,16,256]{5,4,3,1,0,2:T(8,128)S(1)} %get-tuple-element.44), channel_id=1, source_target_pairs={{0,12},{2,14},{4,8},{6,10},{8,4},{10,6},{12,0},{14,2},{16,28},{18,... | collective-permute-start | bytes 196616 | tf_op jit(solution)/shard_map/ppermute | solution.py:30
  168.2 52.1 %all-to-all-start.3 = ((f32[16,4,2,16,256]{4,3,2,1,0:T(8,128)}), f32[16,4,2,16,256]{4,3,2,1,0:T(8,128)S(1)}, u32[]{:S(2)}, u32[]{:S(2)}) async-start(f32[16,4,2,16,256]{4,3,2,1,0:T(8,128)} %absorb.5), calls=%async_computation.3 | async-start | bytes 4194304 | tf_op jit(solution)/shard_map/all_to_all | solution.py:289

commit v6 on v5

--- a/solution.py
+++ b/solution.py
@@ -335,8 +335,9 @@
     stem_high = exchange(sent_high)
     branches = gather_branches(held, rows, cols)
     back_low = exchange(absorb(stem_low, branches, cosine, sine, weight=WEIGHT))
-    pairs, pieces = send_chips(absorb(stem_high, branches, cosine, sine, high - 1, 1))
-    back_high = exchange(absorb(stem_high, branches, cosine, sine, 0, high - 1))
+    some = min(2, high - 1)
+    pairs, pieces = send_chips(absorb(stem_high, branches, cosine, sine, high - some, some))
+    back_high = exchange(absorb(stem_high, branches, cosine, sine, 0, high - some))
     order = list(pieces)
     back_low, *came = lax.optimization_barrier((back_low, *[pieces[bit] for bit in order]))
     back_some = collect_chips(pairs, dict(zip(order, came)))

time: 225 us -> 223 us (level)
  waiting for transfers between devices: 122 us -> 119 us
    all_to_all x4, waiting for transfers between devices: 68.3 us -> 52.7 us  [exchange(): return lax.all_to_all(parts, 'row', 0, 0, tiled=True)]
    ppermute x20, waiting for transfers between devices: 53.9 us -> 66.7 us  [swap(): return lax.ppermute(array, axis, [(i, i ^ bit) for i in range(size)])]
  transfers between devices with their start and end apart: 24 -> 24, of which waited for: 12 -> 15; matrix products, arithmetic and copies ran while one was open for 4% -> 5% of each run, Pallas kernels for 16% -> 17%
where the time goes in v6:
time: 223 us; the launch traced here: 222 us
  waiting for transfers between devices  119 us (53%)
  starting transfers between devices  45.5 us (20%)
  Pallas kernels  44.1 us (20%)
  local copies, waits for them, and re-layouts  6.04 us (3%)
  other arithmetic  5.26 us (2%)
    ppermute x20, waiting for transfers between devices, swap(): return lax.ppermute(array, axis, [(i, i ^ bit) for i in range(size)])  66.7 us
    all_to_all x4, waiting for transfers between devices, exchange(): return lax.all_to_all(parts, 'row', 0, 0, tiled=True)  52.7 us
    pallas_call x3, Pallas kernels, absorb(): pl.pallas_call(absorb_kernel, grid=(count // per,), in_specs=[pl.BlockSpe...  28.4 us
    ppermute x20, starting transfers between devices, swap(): return lax.ppermute(array, axis, [(i, i ^ bit) for i in range(size)])  24.4 us
    all_to_all x4, starting transfers between devices, exchange(): return lax.all_to_all(parts, 'row', 0, 0, tiled=True)  21.1 us
    pallas_call x2, Pallas kernels, batch_first(): pl.pallas_call(partial(batch_first_kernel, start * peers), in_specs=[pl.B...  8.42 us
    sin x1, local copies, waits for them, and re-layouts, on_device(): cosine, sine = (jnp.cos(entangle_phase), jnp.sin(entangle_phase))  4.49 us
  transfers between devices with their start and end apart: 24, of which 15 were waited for; matrix products, arithmetic and copies ran while one was open for 5% of the time, Pallas kernels for 17%

profile of v6, /device:TPU:13, one launch (start us, length us, event | category | flops | bytes accessed | tf_op | source)
XLA Modules:
  0.0 222.4 jit_solution(737571149102326544)
XLA Ops:
  0.0 3.6 %batch_first.2 = f32[16,3,2,16,256]{4,3,2,1,0:T(8,128)} custom-call(f32[2,16,256,128]{3,2,1,0:T(8,128)} %stem_ref.3), custom_call_target="tpu_custom_call" | custom-call | bytes 8388608 | tf_op jit(solution)/shard_map/batch_first/pallas_call | solution.py:211
  6.5 6.0 %all-to-all-start = ((f32[16,3,2,16,256]{4,3,2,1,0:T(8,128)}), f32[16,3,2,16,256]{4,3,2,1,0:T(8,128)}, u32[]{:S(2)}, u32[]{:S(2)}) async-start(f32[16,3,2,16,256]{4,3,2,1,0:T(8,128)} %batch_first.2), calls=%async_computation | async-start | bytes 3145728 | tf_op jit(solution)/shard_map/all_to_all | solution.py:289
  12.5 1.4 dynamic-slice_add_fusion
  14.3 4.8 %batch_first.3 = f32[16,5,2,16,256]{4,3,2,1,0:T(8,128)} custom-call(f32[2,16,256,128]{3,2,1,0:T(8,128)} %stem_ref.3), custom_call_target="tpu_custom_call" | custom-call | bytes 8388608 | tf_op jit(solution)/shard_map/batch_first/pallas_call | solution.py:211
  20.5 7.4 %collective-permute-done.3 = f32[256,256]{1,0:T(8,128)S(1)} collective-permute-done((f32[256,256]{1,0:T(8,128)S(1)}, f32[256,256]{1,0:T(8,128)S(1)}, u32[]{:S(2)}, u32[]{:S(2)}) %collective-permute-start.3) | collective-permute-done | bytes 262176 | tf_op jit(solution)/shard_map/ppermute | solution.py:30
  29.3 2.3 %collective-permute-start.2 = (f32[128,256]{1,0:T(8,128)S(1)}, f32[128,256]{1,0:T(8,128)S(1)}, u32[]{:S(2)}, u32[]{:S(2)}) collective-permute-start(f32[128,256]{1,0:T(8,128)S(1)} %constant_dynamic-slice_fusion.2), channel_id=1, source_target_pairs={{0,4},{2,6},{4,0},{6,2},{8,12},{10,14},{12,8},{14,10},{16,20},{18,... | collective-permute-start | bytes 393224 | tf_op jit(solution)/shard_map/ppermute | solution.py:30
  32.3 2.3 %collective-permute-done.2 = f32[128,256]{1,0:T(8,128)S(1)} collective-permute-done((f32[128,256]{1,0:T(8,128)S(1)}, f32[128,256]{1,0:T(8,128)S(1)}, u32[]{:S(2)}, u32[]{:S(2)}) %collective-permute-start.2) | collective-permute-done | bytes 131104 | tf_op jit(solution)/shard_map/ppermute | solution.py:30
  34.6 3.7 %collective-permute-start.5 = (f32[256,256]{1,0:T(8,128)S(1)}, f32[256,256]{1,0:T(8,128)S(1)}, u32[]{:S(2)}, u32[]{:S(2)}) collective-permute-start(f32[256,256]{1,0:T(8,128)S(1)} %pad_maximum_fusion.3), channel_id=1, source_target_pairs={{0,8},{2,10},{4,12},{6,14},{8,0},{10,2},{12,4},{14,6},{16,24},{18,... | collective-permute-start | bytes 786440 | tf_op jit(solution)/shard_map/ppermute | solution.py:30
  38.3 4.5 %fusion.14 = (f32[4,256,256]{2,1,0:T(8,128)}, f32[4,256,256]{2,1,0:T(8,128)}) fusion(f32[4,256,256]{2,1,0:T(8,128)S(1)} %copy-done.2), kind=kLoop, calls=%fused_computation.70 | loop fusion | bytes 3145728 | tf_op jit(solution)/shard_map/sin | solution.py:327
  42.8 6.5 %collective-permute-done.5 = f32[256,256]{1,0:T(8,128)S(1)} collective-permute-done((f32[256,256]{1,0:T(8,128)S(1)}, f32[256,256]{1,0:T(8,128)S(1)}, u32[]{:S(2)}, u32[]{:S(2)}) %collective-permute-start.5) | collective-permute-done | bytes 262176 | tf_op jit(solution)/shard_map/ppermute | solution.py:30
  49.4 1.9 collective-permute-start.6
  51.2 5.9 %all-to-all-start.2 = ((f32[16,5,2,16,256]{4,3,2,1,0:T(8,128)}), f32[16,5,2,16,256]{4,3,2,1,0:T(8,128)S(1)}, u32[]{:S(2)}, u32[]{:S(2)}) async-start(f32[16,5,2,16,256]{4,3,2,1,0:T(8,128)} %batch_first.3), calls=%async_computation.2 | async-start | bytes 5242880 | tf_op jit(solution)/shard_map/all_to_all | solution.py:289
  57.2 19.7 %collective-permute-done.6 = f32[256,256]{1,0:T(8,128)S(1)} collective-permute-done((f32[256,256]{1,0:T(8,128)S(1)}, f32[256,256]{1,0:T(8,128)S(1)}, u32[]{:S(2)}, u32[]{:S(2)}) %collective-permute-start.6) | collective-permute-done | bytes 262176 | tf_op jit(solution)/shard_map/ppermute | solution.py:30
  77.1 4.6 %collective-permute-done.7 = f32[128,256]{1,0:T(8,128)S(1)} collective-permute-done((f32[128,256]{1,0:T(8,128)S(1)}, f32[128,256]{1,0:T(8,128)S(1)}, u32[]{:S(2)}, u32[]{:S(2)}) %collective-permute-start.7) | collective-permute-done | bytes 131104 | tf_op jit(solution)/shard_map/ppermute | solution.py:30
  81.8 2.3 %collective-permute-start.10 = (f32[256,256]{1,0:T(8,128)S(1)}, f32[256,256]{1,0:T(8,128)S(1)}, u32[]{:S(2)}, u32[]{:S(2)}) collective-permute-start(f32[256,256]{1,0:T(8,128)S(1)} %pad_maximum_fusion.5), channel_id=1, source_target_pairs={{0,4},{2,6},{4,0},{6,2},{8,12},{10,14},{12,8},{14,10},{16,20},{18,... | collective-permute-start | bytes 786440 | tf_op jit(solution)/shard_map/ppermute | solution.py:30
  84.2 9.0 %collective-permute-done.10 = f32[256,256]{1,0:T(8,128)S(1)} collective-permute-done((f32[256,256]{1,0:T(8,128)S(1)}, f32[256,256]{1,0:T(8,128)S(1)}, u32[]{:S(2)}, u32[]{:S(2)}) %collective-permute-start.10) | collective-permute-done | bytes 262176 | tf_op jit(solution)/shard_map/ppermute | solution.py:30
  95.0 2.6 %collective-permute-done.11 = f32[1024,256]{1,0:T(8,128)} collective-permute-done((f32[1024,256]{1,0:T(8,128)}, f32[1024,256]{1,0:T(8,128)}, u32[]{:S(2)}, u32[]{:S(2)}) %collective-permute-start.11) | collective-permute-done | bytes 1048608 | tf_op jit(solution)/shard_map/ppermute | solution.py:30
  97.6 9.2 %absorb.3 = f32[16,3,2,16,256]{4,3,2,1,0:T(8,128)} custom-call(s32[1]{0:T(128)} %bitcast.core_ref, f32[16,3,2,16,256]{4,3,2,1,0:T(8,128)} %all-to-all-done.stem_ref, f32[2,2,256,256]{3,2,1,0:T(8,128)} %bitcast.9.mine_ref, f32[2,2,256,256]{3,2,1,0:T(8,128)} %bitcast.10.other_ref, f32[4,256,256]{2,1,0:T(8,128)} %get-tuple-element.22.cos_ref, ...), custom_call_target="tpu_custom_call" | custom-call | flops 21743271936 | bytes 3145728 | tf_op jit(solution)/shard_map/absorb/pallas_call | solution.py:157
  106.8 13.9 %all-to-all-done.2.stem_ref = f32[16,5,2,16,256]{4,3,2,1,0:T(8,128)S(1)} async-done(((f32[16,5,2,16,256]{4,3,2,1,0:T(8,128)}), f32[16,5,2,16,256]{4,3,2,1,0:T(8,128)S(1)}, u32[]{:S(2)}, u32[]{:S(2)}) %all-to-all-start.2) | async-done | bytes 2621472 | tf_op jit(solution)/shard_map/all_to_all | solution.py:289
  120.8 4.9 %all-to-all-start.1 = ((f32[16,3,2,16,256]{4,3,2,1,0:T(8,128)}), f32[16,3,2,16,256]{4,3,2,1,0:T(8,128)}, u32[]{:S(2)}, u32[]{:S(2)}) async-start(f32[16,3,2,16,256]{4,3,2,1,0:T(8,128)} %absorb.3), calls=%async_computation.1 | async-start | bytes 3145728 | tf_op jit(solution)/shard_map/all_to_all | solution.py:289
  125.6 10.0 %absorb.4 = f32[16,2,2,16,256]{4,3,2,1,0:T(8,128)} custom-call(s32[1]{0:T(128)} %bitcast.core_ref, f32[16,5,2,16,256]{4,3,2,1,0:T(8,128)} %copy-done.1, f32[2,2,256,256]{3,2,1,0:T(8,128)} %bitcast.9.mine_ref, f32[2,2,256,256]{3,2,1,0:T(8,128)} %bitcast.10.other_ref, f32[4,256,256]{2,1,0:T(8,128)} %get-tuple-element.22.cos_ref, ...), custom_call_target="tpu_custom_call" | custom-call | flops 3221225472 | bytes 2097152 | tf_op jit(solution)/shard_map/absorb/pallas_call | solution.py:157
  137.1 1.5 collective-permute-done.12
  141.1 9.2 %absorb.5 = f32[16,3,2,16,256]{4,3,2,1,0:T(8,128)} custom-call(s32[1]{0:T(128)} %bitcast.core_ref, f32[16,5,2,16,256]{4,3,2,1,0:T(8,128)} %copy-done.1, f32[2,2,256,256]{3,2,1,0:T(8,128)} %bitcast.9.mine_ref, f32[2,2,256,256]{3,2,1,0:T(8,128)} %bitcast.10.other_ref, f32[4,256,256]{2,1,0:T(8,128)} %get-tuple-element.22.cos_ref, ...), custom_call_target="tpu_custom_call" | custom-call | flops 4831838208 | bytes 3145728 | tf_op jit(solution)/shard_map/absorb/pallas_call | solution.py:157
  150.3 3.2 %collective-permute-start.13 = (f32[1,2,2,2,16,256]{5,4,3,2,1,0:T(8,128)}, f32[1,2,2,2,16,256]{5,4,3,2,1,0:T(8,128)S(1)}, u32[]{:S(2)}, u32[]{:S(2)}) collective-permute-start(f32[1,2,2,2,16,256]{5,4,3,2,1,0:T(8,128)} %get-tuple-element.36), channel_id=1, source_target_pairs={{0,28},{2,30},{4,24},{6,26},{8,20},{10,22},{12,16},{14,18},{16,12}... | collective-permute-start | bytes 393224 | tf_op jit(solution)/shard_map/ppermute | solution.py:30
  153.5 3.4 %collective-permute-start.15 = (f32[1,2,2,2,16,256]{5,4,3,2,1,0:T(8,128)}, f32[1,2,2,2,16,256]{5,4,3,2,1,0:T(8,128)S(1)}, u32[]{:S(2)}, u32[]{:S(2)}) collective-permute-start(f32[1,2,2,2,16,256]{5,4,3,2,1,0:T(8,128)} %get-tuple-element.38), channel_id=1, source_target_pairs={{0,20},{2,22},{4,16},{6,18},{8,28},{10,30},{12,24},{14,26},{16,4},... | collective-permute-start | bytes 393224 | tf_op jit(solution)/shard_map/ppermute | solution.py:30
  156.9 2.2 %collective-permute-start.17 = (f32[1,2,2,2,16,256]{5,4,3,2,1,0:T(8,128)}, f32[1,2,2,2,16,256]{5,4,3,2,1,0:T(8,128)S(1)}, u32[]{:S(2)}, u32[]{:S(2)}) collective-permute-start(f32[1,2,2,2,16,256]{5,4,3,2,1,0:T(8,128)} %get-tuple-element.40), channel_id=1, source_target_pairs={{0,12},{2,14},{4,8},{6,10},{8,4},{10,6},{12,0},{14,2},{16,28},{18,... | collective-permute-start | bytes 393224 | tf_op jit(solution)/shard_map/ppermute | solution.py:30
  159.2 15.1 %all-to-all-done.1.stem_ref = f32[16,3,2,16,256]{4,3,2,1,0:T(8,128)} async-done(((f32[16,3,2,16,256]{4,3,2,1,0:T(8,128)}), f32[16,3,2,16,256]{4,3,2,1,0:T(8,128)}, u32[]{:S(2)}, u32[]{:S(2)}) %all-to-all-start.1) | async-done | bytes 1572896 | tf_op jit(solution)/shard_map/all_to_all | solution.py:289
  174.3 4.3 %all-to-all-start.3 = ((f32[16,3,2,16,256]{4,3,2,1,0:T(8,128)}), f32[16,3,2,16,256]{4,3,2,1,0:T(8,128)S(1)}, u32[]{:S(2)}, u32[]{:S(2)}) async-start(f32[16,3,2,16,256]{4,3,2,1,0:T(8,128)} %absorb.5), calls=%async_computation.3 | async-start | bytes 3145728 | tf_op jit(solution)/shard_map/all_to_all | solution.py:289
  179.9 11.2 %collective-permute-done.16 = f32[1,2,2,2,16,256]{5,4,3,2,1,0:T(8,128)S(1)} collective-permute-done((f32[1,2,2,2,16,256]{5,4,3,2,1,0:T(8,128)}, f32[1,2,2,2,16,256]{5,4,3,2,1,0:T(8,128)S(1)}, u32[]{:S(2)}, u32[]{:S(2)}) %collective-permute-start.16) | collective-permute-done | bytes 131104 | tf_op jit(solution)/shard_map/ppermute | solution.py:30
  191.2 3.8 %rows_first.1.low_ref = f32[2,16,48,256]{3,2,1,0:T(8,128)} custom-call(f32[16,3,2,16,256]{4,3,2,1,0:T(8,128)} %all-to-all-done.1.stem_ref), custom_call_target="tpu_custom_call" | custom-call | flops 48000000000 | bytes 3145728 | tf_op jit(solution)/shard_map/rows_first/pallas_call | solution.py:237
  195.0 23.7 %all-to-all-done.3.refs_0_ = f32[16,3,2,16,256]{4,3,2,1,0:T(8,128)S(1)} async-done(((f32[16,3,2,16,256]{4,3,2,1,0:T(8,128)}), f32[16,3,2,16,256]{4,3,2,1,0:T(8,128)S(1)}, u32[]{:S(2)}, u32[]{:S(2)}) %all-to-all-start.3) | async-done | bytes 1572896 | tf_op jit(solution)/shard_map/all_to_all | solution.py:289
  218.6 3.5 %batch_last.1 = f32[2,16,256,128]{3,2,1,0:T(8,128)} custom-call(f32[2,16,48,256]{3,2,1,0:T(8,128)} %rows_first.1.low_ref, f32[16,3,2,16,256]{4,3,2,1,0:T(8,128)S(1)} %all-to-all-done.3.refs_0_, f32[16,2,2,16,256]{4,3,2,1,0:T(8,128)S(1)} %bitcast.43), custom_call_target="tpu_custom_call" | custom-call | tf_op jit(solution)/shard_map/batch_last/pallas_call | solution.py:272
  (74 shorter events, 14.3 us)
Async XLA Ops:
  0.0 3.6 %copy-start = (f32[1,2,2,256,256]{4,3,2,1,0:T(8,128)S(1)}, f32[1,2,2,256,256]{4,3,2,1,0:T(8,128)}, u32[]{:S(2)}) copy-start(f32[1,2,2,256,256]{4,3,2,1,0:T(8,128)} %param.5) | copy-start | bytes 3145732
  0.0 4.4 %copy-start.3 = (s32[4]{0:T(128)S(1)}, s32[4]{0:T(128)}, u32[]{:S(2)}) copy-start(s32[4]{0:T(128)} %param.6) | copy-start | bytes 52
  5.8 6.7 %collective-permute-start = (f32[1024,256]{1,0:T(8,128)S(1)}, f32[1024,256]{1,0:T(8,128)}, u32[]{:S(2)}, u32[]{:S(2)}) collective-permute-start(f32[1024,256]{1,0:T(8,128)S(1)} %constant_dynamic-slice_fusion.4), channel_id=1, source_target_pairs={{0,2},{2,0},{4,6},{6,4},{8,10},{10,8},{12,14},{14,12},{16,18},{18,... | collective-permute-start | bytes 3145736 | tf_op jit(solution)/shard_map/ppermute | solution.py:30
  6.5 44.7 %all-to-all-start = ((f32[16,3,2,16,256]{4,3,2,1,0:T(8,128)}), f32[16,3,2,16,256]{4,3,2,1,0:T(8,128)}, u32[]{:S(2)}, u32[]{:S(2)}) async-start(f32[16,3,2,16,256]{4,3,2,1,0:T(8,128)} %batch_first.2), calls=%async_computation | async-start | bytes 3145728 | tf_op jit(solution)/shard_map/all_to_all | solution.py:289
  14.0 13.9 %collective-permute-start.3 = (f32[256,256]{1,0:T(8,128)S(1)}, f32[256,256]{1,0:T(8,128)S(1)}, u32[]{:S(2)}, u32[]{:S(2)}) collective-permute-start(f32[256,256]{1,0:T(8,128)S(1)} %constant_dynamic-slice_fusion.1), channel_id=1, source_target_pairs={{0,4},{2,6},{4,0},{6,2},{8,12},{10,14},{12,8},{14,10},{16,20},{18,... | collective-permute-start | bytes 786440 | tf_op jit(solution)/shard_map/ppermute | solution.py:30
  19.2 19.1 %copy-start.2 = (f32[4,256,256]{2,1,0:T(8,128)S(1)}, f32[4,256,256]{2,1,0:T(8,128)}, u32[]{:S(2)}) copy-start(f32[4,256,256]{2,1,0:T(8,128)} %param.7) | copy-start | bytes 3145732
  19.2 10.0 %collective-permute-start.1 = (f32[256,256]{1,0:T(8,128)S(1)}, f32[256,256]{1,0:T(8,128)S(1)}, u32[]{:S(2)}, u32[]{:S(2)}) collective-permute-start(f32[256,256]{1,0:T(8,128)S(1)} %constant_dynamic-slice_fusion.3), channel_id=1, source_target_pairs={{0,1},{1,0},{2,3},{3,2},{4,5},{5,4},{6,7},{7,6},{8,9},{9,8},{10,11... | collective-permute-start | bytes 786440 | tf_op jit(solution)/shard_map/ppermute | solution.py:30
  28.0 4.3 %collective-permute-start.4 = (f32[128,256]{1,0:T(8,128)S(1)}, f32[128,256]{1,0:T(8,128)S(1)}, u32[]{:S(2)}, u32[]{:S(2)}) collective-permute-start(f32[128,256]{1,0:T(8,128)S(1)} %constant_dynamic-slice_fusion), channel_id=1, source_target_pairs={{0,1},{1,0},{2,3},{3,2},{4,5},{5,4},{6,7},{7,6},{8,9},{9,8},{10,11... | collective-permute-start | bytes 393224 | tf_op jit(solution)/shard_map/ppermute | solution.py:30
  29.3 5.2 %collective-permute-start.2 = (f32[128,256]{1,0:T(8,128)S(1)}, f32[128,256]{1,0:T(8,128)S(1)}, u32[]{:S(2)}, u32[]{:S(2)}) collective-permute-start(f32[128,256]{1,0:T(8,128)S(1)} %constant_dynamic-slice_fusion.2), channel_id=1, source_target_pairs={{0,4},{2,6},{4,0},{6,2},{8,12},{10,14},{12,8},{14,10},{16,20},{18,... | collective-permute-start | bytes 393224 | tf_op jit(solution)/shard_map/ppermute | solution.py:30
  34.6 14.7 %collective-permute-start.5 = (f32[256,256]{1,0:T(8,128)S(1)}, f32[256,256]{1,0:T(8,128)S(1)}, u32[]{:S(2)}, u32[]{:S(2)}) collective-permute-start(f32[256,256]{1,0:T(8,128)S(1)} %pad_maximum_fusion.3), channel_id=1, source_target_pairs={{0,8},{2,10},{4,12},{6,14},{8,0},{10,2},{12,4},{14,6},{16,24},{18,... | collective-permute-start | bytes 786440 | tf_op jit(solution)/shard_map/ppermute | solution.py:30
  49.4 27.5 %collective-permute-start.6 = (f32[256,256]{1,0:T(8,128)S(1)}, f32[256,256]{1,0:T(8,128)S(1)}, u32[]{:S(2)}, u32[]{:S(2)}) collective-permute-start(f32[256,256]{1,0:T(8,128)S(1)} %fusion.13), channel_id=1, source_target_pairs={{0,16},{2,18},{4,20},{6,22},{8,24},{10,26},{12,28},{14,30},{16,0},... | collective-permute-start | bytes 786440 | tf_op jit(solution)/shard_map/ppermute | solution.py:30
  51.2 69.5 %all-to-all-start.2 = ((f32[16,5,2,16,256]{4,3,2,1,0:T(8,128)}), f32[16,5,2,16,256]{4,3,2,1,0:T(8,128)S(1)}, u32[]{:S(2)}, u32[]{:S(2)}) async-start(f32[16,5,2,16,256]{4,3,2,1,0:T(8,128)} %batch_first.3), calls=%async_computation.2 | async-start | bytes 5242880 | tf_op jit(solution)/shard_map/all_to_all | solution.py:289
  77.0 4.8 %collective-permute-start.7 = (f32[128,256]{1,0:T(8,128)S(1)}, f32[128,256]{1,0:T(8,128)S(1)}, u32[]{:S(2)}, u32[]{:S(2)}) collective-permute-start(f32[128,256]{1,0:T(8,128)S(1)} %get-tuple-element.55), channel_id=1, source_target_pairs={{0,4},{2,6},{4,0},{6,2},{8,12},{10,14},{12,8},{14,10},{16,20},{18,... | collective-permute-start | bytes 393224 | tf_op jit(solution)/shard_map/ppermute | solution.py:30
  77.0 4.7 %collective-permute-start.9 = (f32[128,256]{1,0:T(8,128)S(1)}, f32[128,256]{1,0:T(8,128)S(1)}, u32[]{:S(2)}, u32[]{:S(2)}) collective-permute-start(f32[128,256]{1,0:T(8,128)S(1)} %get-tuple-element.56), channel_id=1, source_target_pairs={{0,1},{1,0},{2,3},{3,2},{4,5},{5,4},{6,7},{7,6},{8,9},{9,8},{10,11... | collective-permute-start | bytes 393224 | tf_op jit(solution)/shard_map/ppermute | solution.py:30
  81.8 11.3 %collective-permute-start.10 = (f32[256,256]{1,0:T(8,128)S(1)}, f32[256,256]{1,0:T(8,128)S(1)}, u32[]{:S(2)}, u32[]{:S(2)}) collective-permute-start(f32[256,256]{1,0:T(8,128)S(1)} %pad_maximum_fusion.5), channel_id=1, source_target_pairs={{0,4},{2,6},{4,0},{6,2},{8,12},{10,14},{12,8},{14,10},{16,20},{18,... | collective-permute-start | bytes 786440 | tf_op jit(solution)/shard_map/ppermute | solution.py:30
  84.1 9.1 %collective-permute-start.8 = (f32[256,256]{1,0:T(8,128)S(1)}, f32[256,256]{1,0:T(8,128)S(1)}, u32[]{:S(2)}, u32[]{:S(2)}) collective-permute-start(f32[256,256]{1,0:T(8,128)S(1)} %pad_maximum_fusion.4), channel_id=1, source_target_pairs={{0,1},{1,0},{2,3},{3,2},{4,5},{5,4},{6,7},{7,6},{8,9},{9,8},{10,11... | collective-permute-start | bytes 786440 | tf_op jit(solution)/shard_map/ppermute | solution.py:30
  94.3 3.3 %collective-permute-start.11 = (f32[1024,256]{1,0:T(8,128)}, f32[1024,256]{1,0:T(8,128)}, u32[]{:S(2)}, u32[]{:S(2)}) collective-permute-start(f32[1024,256]{1,0:T(8,128)} %pad_maximum_fusion.1), channel_id=1, source_target_pairs={{0,2},{2,0},{4,6},{6,4},{8,10},{10,8},{12,14},{14,12},{16,18},{18,... | collective-permute-start | bytes 3145736 | tf_op jit(solution)/shard_map/ppermute | solution.py:30
  120.8 4.9 %copy-start.1 = (f32[16,5,2,16,256]{4,3,2,1,0:T(8,128)}, f32[16,5,2,16,256]{4,3,2,1,0:T(8,128)S(1)}, u32[]{:S(2)}) copy-start(f32[16,5,2,16,256]{4,3,2,1,0:T(8,128)S(1)} %all-to-all-done.2.stem_ref) | copy-start | bytes 7864324
  120.8 53.6 %all-to-all-start.1 = ((f32[16,3,2,16,256]{4,3,2,1,0:T(8,128)}), f32[16,3,2,16,256]{4,3,2,1,0:T(8,128)}, u32[]{:S(2)}, u32[]{:S(2)}) async-start(f32[16,3,2,16,256]{4,3,2,1,0:T(8,128)} %absorb.3), calls=%async_computation.1 | async-start | bytes 3145728 | tf_op jit(solution)/shard_map/all_to_all | solution.py:289
  136.7 2.0 collective-permute-start.12
  139.9 17.1 %collective-permute-start.18 = (f32[1,2,2,2,16,256]{5,4,3,2,1,0:T(8,128)S(1)}, f32[1,2,2,2,16,256]{5,4,3,2,1,0:T(8,128)S(1)}, u32[]{:S(2)}, u32[]{:S(2)}) collective-permute-start(f32[1,2,2,2,16,256]{5,4,3,2,1,0:T(8,128)S(1)} %fusion.11), channel_id=1, source_target_pairs={{0,8},{2,10},{4,12},{6,14},{8,0},{10,2},{12,4},{14,6},{16,24},{18,... | collective-permute-start | bytes 393224 | tf_op jit(solution)/shard_map/ppermute | solution.py:30
  141.1 15.9 %collective-permute-start.19 = (f32[1,2,2,2,16,256]{5,4,3,2,1,0:T(8,128)S(1)}, f32[1,2,2,2,16,256]{5,4,3,2,1,0:T(8,128)S(1)}, u32[]{:S(2)}, u32[]{:S(2)}) collective-permute-start(f32[1,2,2,2,16,256]{5,4,3,2,1,0:T(8,128)S(1)} %get-tuple-element.35), channel_id=1, source_target_pairs={{0,4},{2,6},{4,0},{6,2},{8,12},{10,14},{12,8},{14,10},{16,20},{18,... | collective-permute-start | bytes 393224 | tf_op jit(solution)/shard_map/ppermute | solution.py:30
  150.3 28.3 %collective-permute-start.13 = (f32[1,2,2,2,16,256]{5,4,3,2,1,0:T(8,128)}, f32[1,2,2,2,16,256]{5,4,3,2,1,0:T(8,128)S(1)}, u32[]{:S(2)}, u32[]{:S(2)}) collective-permute-start(f32[1,2,2,2,16,256]{5,4,3,2,1,0:T(8,128)} %get-tuple-element.36), channel_id=1, source_target_pairs={{0,28},{2,30},{4,24},{6,26},{8,20},{10,22},{12,16},{14,18},{16,12}... | collective-permute-start | bytes 393224 | tf_op jit(solution)/shard_map/ppermute | solution.py:30
  153.5 25.5 %collective-permute-start.14 = (f32[1,2,2,2,16,256]{5,4,3,2,1,0:T(8,128)}, f32[1,2,2,2,16,256]{5,4,3,2,1,0:T(8,128)S(1)}, u32[]{:S(2)}, u32[]{:S(2)}) collective-permute-start(f32[1,2,2,2,16,256]{5,4,3,2,1,0:T(8,128)} %get-tuple-element.37), channel_id=1, source_target_pairs={{0,24},{2,26},{4,28},{6,30},{8,16},{10,18},{12,20},{14,22},{16,8},... | collective-permute-start | bytes 393224 | tf_op jit(solution)/shard_map/ppermute | solution.py:30
  153.5 26.4 %collective-permute-start.15 = (f32[1,2,2,2,16,256]{5,4,3,2,1,0:T(8,128)}, f32[1,2,2,2,16,256]{5,4,3,2,1,0:T(8,128)S(1)}, u32[]{:S(2)}, u32[]{:S(2)}) collective-permute-start(f32[1,2,2,2,16,256]{5,4,3,2,1,0:T(8,128)} %get-tuple-element.38), channel_id=1, source_target_pairs={{0,20},{2,22},{4,16},{6,18},{8,28},{10,30},{12,24},{14,26},{16,4},... | collective-permute-start | bytes 393224 | tf_op jit(solution)/shard_map/ppermute | solution.py:30
  156.9 34.1 %collective-permute-start.16 = (f32[1,2,2,2,16,256]{5,4,3,2,1,0:T(8,128)}, f32[1,2,2,2,16,256]{5,4,3,2,1,0:T(8,128)S(1)}, u32[]{:S(2)}, u32[]{:S(2)}) collective-permute-start(f32[1,2,2,2,16,256]{5,4,3,2,1,0:T(8,128)} %get-tuple-element.39), channel_id=1, source_target_pairs={{0,16},{2,18},{4,20},{6,22},{8,24},{10,26},{12,28},{14,30},{16,0},... | collective-permute-start | bytes 393224 | tf_op jit(solution)/shard_map/ppermute | solution.py:30
  156.9 34.1 %collective-permute-start.17 = (f32[1,2,2,2,16,256]{5,4,3,2,1,0:T(8,128)}, f32[1,2,2,2,16,256]{5,4,3,2,1,0:T(8,128)S(1)}, u32[]{:S(2)}, u32[]{:S(2)}) collective-permute-start(f32[1,2,2,2,16,256]{5,4,3,2,1,0:T(8,128)} %get-tuple-element.40), channel_id=1, source_target_pairs={{0,12},{2,14},{4,8},{6,10},{8,4},{10,6},{12,0},{14,2},{16,28},{18,... | collective-permute-start | bytes 393224 | tf_op jit(solution)/shard_map/ppermute | solution.py:30
  174.3 44.3 %all-to-all-start.3 = ((f32[16,3,2,16,256]{4,3,2,1,0:T(8,128)}), f32[16,3,2,16,256]{4,3,2,1,0:T(8,128)S(1)}, u32[]{:S(2)}, u32[]{:S(2)}) async-start(f32[16,3,2,16,256]{4,3,2,1,0:T(8,128)} %absorb.5), calls=%async_computation.3 | async-start | bytes 3145728 | tf_op jit(solution)/shard_map/all_to_all | solution.py:289

commit v7 on v6

--- a/solution.py
+++ b/solution.py
@@ -9,7 +9,7 @@
 
 STEPS = 4
 MIB = 1024 * 1024
-WEIGHT = 4.5
+WEIGHT = 1.8
 LAST = 48
 PER = (1, 2, 3)
 DOT = partial(jnp.dot, precision=lax.Precision.HIGHEST)
@@ -318,7 +318,7 @@
 
 def on_device(stem_slab, factors, branch_owner, entangle_phase, *, rows, cols):
     items = stem_slab.shape[3] // rows
-    low = max(1, items * 3 // 8)
+    low = max(1, items // 2)
     high = items - low
     sent_low = batch_first(stem_slab, rows, 0, low)
     sent_low, factors = lax.optimization_barrier((sent_low, factors))

time: 223 us -> 219 us (0.982)
    all_to_all x4, waiting for transfers between devices: 52.7 us -> 46.3 us  [exchange(): return lax.all_to_all(parts, 'row', 0, 0, tiled=True)]
    ppermute x20, waiting for transfers between devices: 66.7 us -> 71.6 us  [swap(): return lax.ppermute(array, axis, [(i, i ^ bit) for i in range(size)])]
  transfers between devices with their start and end apart: 24 -> 24, of which waited for: 15 -> 16; matrix products, arithmetic and copies ran while one was open for 5% -> 5% of each run, Pallas kernels for 17% -> 16%
where the time goes in v7:
time: 219 us
  waiting for transfers between devices  118 us (54%)
  starting transfers between devices  44.7 us (20%)
  Pallas kernels  42.5 us (19%)
  local copies, waits for them, and re-layouts  7.38 us (3%)
  other arithmetic  4.13 us (2%)
    ppermute x20, waiting for transfers between devices, swap(): return lax.ppermute(array, axis, [(i, i ^ bit) for i in range(size)])  71.6 us
    all_to_all x4, waiting for transfers between devices, exchange(): return lax.all_to_all(parts, 'row', 0, 0, tiled=True)  46.3 us
    pallas_call x3, Pallas kernels, absorb(): pl.pallas_call(absorb_kernel, grid=(count // per,), in_specs=[pl.BlockSpe...  26.6 us
    ppermute x20, starting transfers between devices, swap(): return lax.ppermute(array, axis, [(i, i ^ bit) for i in range(size)])  23.6 us
    all_to_all x4, starting transfers between devices, exchange(): return lax.all_to_all(parts, 'row', 0, 0, tiled=True)  21.1 us
    pallas_call x2, Pallas kernels, batch_first(): pl.pallas_call(partial(batch_first_kernel, start * peers), in_specs=[pl.B...  8.35 us
    sin x1, local copies, waits for them, and re-layouts, on_device(): cosine, sine = (jnp.cos(entangle_phase), jnp.sin(entangle_phase))  4.48 us
  transfers between devices with their start and end apart: 24, of which 16 were waited for; matrix products, arithmetic and copies ran while one was open for 5% of the time, Pallas kernels for 16%

profile of v7, /device:TPU:13, one launch (start us, length us, event | category | flops | bytes accessed | tf_op | source)
XLA Modules:
  0.0 218.8 jit_solution(11108231526479812306)
XLA Ops:
  0.0 3.5 %batch_first.2 = f32[16,4,2,16,256]{4,3,2,1,0:T(8,128)} custom-call(f32[2,16,256,128]{3,2,1,0:T(8,128)} %stem_ref.3), custom_call_target="tpu_custom_call" | custom-call | bytes 8388608 | tf_op jit(solution)/shard_map/batch_first/pallas_call | solution.py:211
  3.6 6.7 %all-to-all-start = ((f32[16,4,2,16,256]{4,3,2,1,0:T(8,128)}), f32[16,4,2,16,256]{4,3,2,1,0:T(8,128)}, u32[]{:S(2)}, u32[]{:S(2)}) async-start(f32[16,4,2,16,256]{4,3,2,1,0:T(8,128)} %batch_first.2), calls=%async_computation | async-start | bytes 4194304 | tf_op jit(solution)/shard_map/all_to_all | solution.py:289
  12.9 2.4 %collective-permute-done = f32[1024,256]{1,0:T(8,128)} collective-permute-done((f32[1024,256]{1,0:T(8,128)S(1)}, f32[1024,256]{1,0:T(8,128)}, u32[]{:S(2)}, u32[]{:S(2)}) %collective-permute-start) | collective-permute-done | bytes 1048608 | tf_op jit(solution)/shard_map/ppermute | solution.py:30
  15.3 1.4 dynamic-slice_add_fusion
  17.1 4.8 %batch_first.3 = f32[16,4,2,16,256]{4,3,2,1,0:T(8,128)} custom-call(f32[2,16,256,128]{3,2,1,0:T(8,128)} %stem_ref.3), custom_call_target="tpu_custom_call" | custom-call | bytes 8388608 | tf_op jit(solution)/shard_map/batch_first/pallas_call | solution.py:211
  23.3 5.1 %collective-permute-done.3 = f32[256,256]{1,0:T(8,128)S(1)} collective-permute-done((f32[256,256]{1,0:T(8,128)S(1)}, f32[256,256]{1,0:T(8,128)S(1)}, u32[]{:S(2)}, u32[]{:S(2)}) %collective-permute-start.3) | collective-permute-done | bytes 262176 | tf_op jit(solution)/shard_map/ppermute | solution.py:30
  30.7 2.1 collective-permute-done.4
  32.8 4.4 %collective-permute-done.2 = f32[128,256]{1,0:T(8,128)S(1)} collective-permute-done((f32[128,256]{1,0:T(8,128)S(1)}, f32[128,256]{1,0:T(8,128)S(1)}, u32[]{:S(2)}, u32[]{:S(2)}) %collective-permute-start.2) | collective-permute-done | bytes 131104 | tf_op jit(solution)/shard_map/ppermute | solution.py:30
  37.3 5.7 %collective-permute-start.5 = (f32[256,256]{1,0:T(8,128)S(1)}, f32[256,256]{1,0:T(8,128)S(1)}, u32[]{:S(2)}, u32[]{:S(2)}) collective-permute-start(f32[256,256]{1,0:T(8,128)S(1)} %pad_maximum_fusion.3), channel_id=1, source_target_pairs={{0,8},{2,10},{4,12},{6,14},{8,0},{10,2},{12,4},{14,6},{16,24},{18,... | collective-permute-start | bytes 786440 | tf_op jit(solution)/shard_map/ppermute | solution.py:30
  43.0 4.5 %fusion.14 = (f32[4,256,256]{2,1,0:T(8,128)}, f32[4,256,256]{2,1,0:T(8,128)}) fusion(f32[4,256,256]{2,1,0:T(8,128)S(1)} %copy-done.2), kind=kLoop, calls=%fused_computation.70 | loop fusion | bytes 3145728 | tf_op jit(solution)/shard_map/sin | solution.py:327
  47.5 9.4 %collective-permute-done.5 = f32[256,256]{1,0:T(8,128)S(1)} collective-permute-done((f32[256,256]{1,0:T(8,128)S(1)}, f32[256,256]{1,0:T(8,128)S(1)}, u32[]{:S(2)}, u32[]{:S(2)}) %collective-permute-start.5) | collective-permute-done | bytes 262176 | tf_op jit(solution)/shard_map/ppermute | solution.py:30
  57.0 7.0 %all-to-all-done.stem_ref = f32[16,4,2,16,256]{4,3,2,1,0:T(8,128)} async-done(((f32[16,4,2,16,256]{4,3,2,1,0:T(8,128)}), f32[16,4,2,16,256]{4,3,2,1,0:T(8,128)}, u32[]{:S(2)}, u32[]{:S(2)}) %all-to-all-start) | async-done | bytes 2097184 | tf_op jit(solution)/shard_map/all_to_all | solution.py:289
  64.1 4.8 %all-to-all-start.2 = ((f32[16,4,2,16,256]{4,3,2,1,0:T(8,128)}), f32[16,4,2,16,256]{4,3,2,1,0:T(8,128)S(1)}, u32[]{:S(2)}, u32[]{:S(2)}) async-start(f32[16,4,2,16,256]{4,3,2,1,0:T(8,128)} %batch_first.3), calls=%async_computation.2 | async-start | bytes 4194304 | tf_op jit(solution)/shard_map/all_to_all | solution.py:289
  70.5 13.6 %collective-permute-done.7 = f32[128,256]{1,0:T(8,128)S(1)} collective-permute-done((f32[128,256]{1,0:T(8,128)S(1)}, f32[128,256]{1,0:T(8,128)S(1)}, u32[]{:S(2)}, u32[]{:S(2)}) %collective-permute-start.7) | collective-permute-done | bytes 131104 | tf_op jit(solution)/shard_map/ppermute | solution.py:30
  85.6 10.0 %collective-permute-done.10 = f32[256,256]{1,0:T(8,128)S(1)} collective-permute-done((f32[256,256]{1,0:T(8,128)S(1)}, f32[256,256]{1,0:T(8,128)S(1)}, u32[]{:S(2)}, u32[]{:S(2)}) %collective-permute-start.10) | collective-permute-done | bytes 262176 | tf_op jit(solution)/shard_map/ppermute | solution.py:30
  96.3 2.4 %collective-permute-done.11 = f32[1024,256]{1,0:T(8,128)} collective-permute-done((f32[1024,256]{1,0:T(8,128)S(1)}, f32[1024,256]{1,0:T(8,128)}, u32[]{:S(2)}, u32[]{:S(2)}) %collective-permute-start.11) | collective-permute-done | bytes 1048608 | tf_op jit(solution)/shard_map/ppermute | solution.py:30
  98.7 11.9 %absorb.3 = f32[16,4,2,16,256]{4,3,2,1,0:T(8,128)} custom-call(s32[1]{0:T(128)} %bitcast.core_ref, f32[16,4,2,16,256]{4,3,2,1,0:T(8,128)} %all-to-all-done.stem_ref, f32[2,2,256,256]{3,2,1,0:T(8,128)} %bitcast.48, f32[2,2,256,256]{3,2,1,0:T(8,128)} %bitcast.10.other_ref, f32[4,256,256]{2,1,0:T(8,128)} %get-tuple-element.22.cos_ref, ...), custom_call_target="tpu_custom_call" | custom-call | flops 11596411904 | bytes 4194304 | tf_op jit(solution)/shard_map/absorb/pallas_call | solution.py:157
  110.7 6.0 %all-to-all-done.2.stem_ref = f32[16,4,2,16,256]{4,3,2,1,0:T(8,128)S(1)} async-done(((f32[16,4,2,16,256]{4,3,2,1,0:T(8,128)}), f32[16,4,2,16,256]{4,3,2,1,0:T(8,128)S(1)}, u32[]{:S(2)}, u32[]{:S(2)}) %all-to-all-start.2) | async-done | bytes 2097184 | tf_op jit(solution)/shard_map/all_to_all | solution.py:289
  118.0 4.6 %all-to-all-start.1 = ((f32[16,4,2,16,256]{4,3,2,1,0:T(8,128)}), f32[16,4,2,16,256]{4,3,2,1,0:T(8,128)}, u32[]{:S(2)}, u32[]{:S(2)}) async-start(f32[16,4,2,16,256]{4,3,2,1,0:T(8,128)} %absorb.3), calls=%async_computation.1 | async-start | bytes 4194304 | tf_op jit(solution)/shard_map/all_to_all | solution.py:289
  122.6 7.4 %absorb.4 = f32[16,2,2,16,256]{4,3,2,1,0:T(8,128)} custom-call(s32[1]{0:T(128)} %bitcast.core_ref, f32[16,4,2,16,256]{4,3,2,1,0:T(8,128)} %copy-done.1, f32[2,2,256,256]{3,2,1,0:T(8,128)} %bitcast.49, f32[2,2,256,256]{3,2,1,0:T(8,128)} %bitcast.10.other_ref, f32[4,256,256]{2,1,0:T(8,128)} %get-tuple-element.22.cos_ref, f32[4,256,256]{2,1,0:T(8,128)} %get-tuple-element.23.sin_ref), custom_call_target="tpu_custom_call" | custom-call | flops 3221225472 | bytes 2097152 | tf_op jit(solution)/shard_map/absorb/pallas_call | solution.py:157
  131.5 1.5 collective-permute-done.12
  135.3 7.3 %absorb.5 = f32[16,2,2,16,256]{4,3,2,1,0:T(8,128)} custom-call(s32[1]{0:T(128)} %bitcast.core_ref, f32[16,4,2,16,256]{4,3,2,1,0:T(8,128)} %copy-done.1, f32[2,2,256,256]{3,2,1,0:T(8,128)} %bitcast.50, f32[2,2,256,256]{3,2,1,0:T(8,128)} %bitcast.10.other_ref, f32[4,256,256]{2,1,0:T(8,128)} %get-tuple-element.22.cos_ref, f32[4,256,256]{2,1,0:T(8,128)} %get-tuple-element.23.sin_ref), custom_call_target="tpu_custom_call" | custom-call | flops 3221225472 | bytes 2097152 | tf_op jit(solution)/shard_map/absorb/pallas_call | solution.py:157
  142.7 3.2 %collective-permute-start.13 = (f32[1,2,2,2,16,256]{5,4,3,2,1,0:T(8,128)}, f32[1,2,2,2,16,256]{5,4,3,2,1,0:T(8,128)S(1)}, u32[]{:S(2)}, u32[]{:S(2)}) collective-permute-start(f32[1,2,2,2,16,256]{5,4,3,2,1,0:T(8,128)} %get-tuple-element.36), channel_id=1, source_target_pairs={{0,28},{2,30},{4,24},{6,26},{8,20},{10,22},{12,16},{14,18},{16,12}... | collective-permute-start | bytes 393224 | tf_op jit(solution)/shard_map/ppermute | solution.py:30
  145.9 3.3 %collective-permute-start.15 = (f32[1,2,2,2,16,256]{5,4,3,2,1,0:T(8,128)S(1)}, f32[1,2,2,2,16,256]{5,4,3,2,1,0:T(8,128)S(1)}, u32[]{:S(2)}, u32[]{:S(2)}) collective-permute-start(f32[1,2,2,2,16,256]{5,4,3,2,1,0:T(8,128)S(1)} %get-tuple-element.38), channel_id=1, source_target_pairs={{0,20},{2,22},{4,16},{6,18},{8,28},{10,30},{12,24},{14,26},{16,4},... | collective-permute-start | bytes 393224 | tf_op jit(solution)/shard_map/ppermute | solution.py:30
  149.1 11.8 %collective-permute-done.18 = f32[1,2,2,2,16,256]{5,4,3,2,1,0:T(8,128)S(1)} collective-permute-done((f32[1,2,2,2,16,256]{5,4,3,2,1,0:T(8,128)S(1)}, f32[1,2,2,2,16,256]{5,4,3,2,1,0:T(8,128)S(1)}, u32[]{:S(2)}, u32[]{:S(2)}) %collective-permute-start.18) | collective-permute-done | bytes 131104 | tf_op jit(solution)/shard_map/ppermute | solution.py:30
  161.7 2.1 collective-permute-start.17
  163.9 18.2 %all-to-all-done.1.stem_ref = f32[16,4,2,16,256]{4,3,2,1,0:T(8,128)} async-done(((f32[16,4,2,16,256]{4,3,2,1,0:T(8,128)}), f32[16,4,2,16,256]{4,3,2,1,0:T(8,128)}, u32[]{:S(2)}, u32[]{:S(2)}) %all-to-all-start.1) | async-done | bytes 2097184 | tf_op jit(solution)/shard_map/all_to_all | solution.py:289
  182.1 5.1 %all-to-all-start.3 = ((f32[16,2,2,16,256]{4,3,2,1,0:T(8,128)}), f32[16,2,2,16,256]{4,3,2,1,0:T(8,128)S(1)}, u32[]{:S(2)}, u32[]{:S(2)}) async-start(f32[16,2,2,16,256]{4,3,2,1,0:T(8,128)} %absorb.5), calls=%async_computation.3 | async-start | bytes 2097152 | tf_op jit(solution)/shard_map/all_to_all | solution.py:289
  187.5 8.3 %collective-permute-done.16 = f32[1,2,2,2,16,256]{5,4,3,2,1,0:T(8,128)S(1)} collective-permute-done((f32[1,2,2,2,16,256]{5,4,3,2,1,0:T(8,128)S(1)}, f32[1,2,2,2,16,256]{5,4,3,2,1,0:T(8,128)S(1)}, u32[]{:S(2)}, u32[]{:S(2)}) %collective-permute-start.16) | collective-permute-done | bytes 131104 | tf_op jit(solution)/shard_map/ppermute | solution.py:30
  195.8 4.1 %rows_first.1.low_ref = f32[2,16,64,256]{3,2,1,0:T(8,128)} custom-call(f32[16,4,2,16,256]{4,3,2,1,0:T(8,128)} %all-to-all-done.1.stem_ref), custom_call_target="tpu_custom_call" | custom-call | flops 48000000000 | bytes 4194304 | tf_op jit(solution)/shard_map/rows_first/pallas_call | solution.py:237
  200.0 15.1 %all-to-all-done.3.refs_0_ = f32[16,2,2,16,256]{4,3,2,1,0:T(8,128)S(1)} async-done(((f32[16,2,2,16,256]{4,3,2,1,0:T(8,128)}), f32[16,2,2,16,256]{4,3,2,1,0:T(8,128)S(1)}, u32[]{:S(2)}, u32[]{:S(2)}) %all-to-all-start.3) | async-done | bytes 1048608 | tf_op jit(solution)/shard_map/all_to_all | solution.py:289
  215.1 3.5 %batch_last.1 = f32[2,16,256,128]{3,2,1,0:T(8,128)} custom-call(f32[2,16,64,256]{3,2,1,0:T(8,128)} %rows_first.1.low_ref, f32[16,2,2,16,256]{4,3,2,1,0:T(8,128)S(1)} %all-to-all-done.3.refs_0_, f32[16,2,2,16,256]{4,3,2,1,0:T(8,128)S(1)} %bitcast.43), custom_call_target="tpu_custom_call" | custom-call | tf_op jit(solution)/shard_map/batch_last/pallas_call | solution.py:272
  (76 shorter events, 16.9 us)
Async XLA Ops:
  3.6 6.7 %copy-start = (f32[1,2,2,256,256]{4,3,2,1,0:T(8,128)S(1)}, f32[1,2,2,256,256]{4,3,2,1,0:T(8,128)}, u32[]{:S(2)}) copy-start(f32[1,2,2,256,256]{4,3,2,1,0:T(8,128)} %param.5) | copy-start | bytes 3145732
  3.6 7.5 %copy-start.4 = (s32[4]{0:T(128)S(1)}, s32[4]{0:T(128)}, u32[]{:S(2)}) copy-start(s32[4]{0:T(128)} %param.6) | copy-start | bytes 52
  3.6 60.5 %all-to-all-start = ((f32[16,4,2,16,256]{4,3,2,1,0:T(8,128)}), f32[16,4,2,16,256]{4,3,2,1,0:T(8,128)}, u32[]{:S(2)}, u32[]{:S(2)}) async-start(f32[16,4,2,16,256]{4,3,2,1,0:T(8,128)} %batch_first.2), calls=%async_computation | async-start | bytes 4194304 | tf_op jit(solution)/shard_map/all_to_all | solution.py:289
  12.4 2.9 %collective-permute-start = (f32[1024,256]{1,0:T(8,128)S(1)}, f32[1024,256]{1,0:T(8,128)}, u32[]{:S(2)}, u32[]{:S(2)}) collective-permute-start(f32[1024,256]{1,0:T(8,128)S(1)} %constant_dynamic-slice_fusion.4), channel_id=1, source_target_pairs={{0,2},{2,0},{4,6},{6,4},{8,10},{10,8},{12,14},{14,12},{16,18},{18,... | collective-permute-start | bytes 3145736 | tf_op jit(solution)/shard_map/ppermute | solution.py:30
  16.8 11.6 %collective-permute-start.3 = (f32[256,256]{1,0:T(8,128)S(1)}, f32[256,256]{1,0:T(8,128)S(1)}, u32[]{:S(2)}, u32[]{:S(2)}) collective-permute-start(f32[256,256]{1,0:T(8,128)S(1)} %constant_dynamic-slice_fusion.1), channel_id=1, source_target_pairs={{0,4},{2,6},{4,0},{6,2},{8,12},{10,14},{12,8},{14,10},{16,20},{18,... | collective-permute-start | bytes 786440 | tf_op jit(solution)/shard_map/ppermute | solution.py:30
  21.9 21.1 %copy-start.2 = (f32[4,256,256]{2,1,0:T(8,128)S(1)}, f32[4,256,256]{2,1,0:T(8,128)}, u32[]{:S(2)}) copy-start(f32[4,256,256]{2,1,0:T(8,128)} %param.7) | copy-start | bytes 3145732
  22.0 7.7 %collective-permute-start.1 = (f32[256,256]{1,0:T(8,128)S(1)}, f32[256,256]{1,0:T(8,128)S(1)}, u32[]{:S(2)}, u32[]{:S(2)}) collective-permute-start(f32[256,256]{1,0:T(8,128)S(1)} %constant_dynamic-slice_fusion.3), channel_id=1, source_target_pairs={{0,1},{1,0},{2,3},{3,2},{4,5},{5,4},{6,7},{7,6},{8,9},{9,8},{10,11... | collective-permute-start | bytes 786440 | tf_op jit(solution)/shard_map/ppermute | solution.py:30
  28.4 4.3 %collective-permute-start.4 = (f32[128,256]{1,0:T(8,128)S(1)}, f32[128,256]{1,0:T(8,128)S(1)}, u32[]{:S(2)}, u32[]{:S(2)}) collective-permute-start(f32[128,256]{1,0:T(8,128)S(1)} %constant_dynamic-slice_fusion), channel_id=1, source_target_pairs={{0,1},{1,0},{2,3},{3,2},{4,5},{5,4},{6,7},{7,6},{8,9},{9,8},{10,11... | collective-permute-start | bytes 393224 | tf_op jit(solution)/shard_map/ppermute | solution.py:30
  29.8 7.4 %collective-permute-start.2 = (f32[128,256]{1,0:T(8,128)S(1)}, f32[128,256]{1,0:T(8,128)S(1)}, u32[]{:S(2)}, u32[]{:S(2)}) collective-permute-start(f32[128,256]{1,0:T(8,128)S(1)} %constant_dynamic-slice_fusion.2), channel_id=1, source_target_pairs={{0,4},{2,6},{4,0},{6,2},{8,12},{10,14},{12,8},{14,10},{16,20},{18,... | collective-permute-start | bytes 393224 | tf_op jit(solution)/shard_map/ppermute | solution.py:30
  37.3 19.6 %collective-permute-start.5 = (f32[256,256]{1,0:T(8,128)S(1)}, f32[256,256]{1,0:T(8,128)S(1)}, u32[]{:S(2)}, u32[]{:S(2)}) collective-permute-start(f32[256,256]{1,0:T(8,128)S(1)} %pad_maximum_fusion.3), channel_id=1, source_target_pairs={{0,8},{2,10},{4,12},{6,14},{8,0},{10,2},{12,4},{14,6},{16,24},{18,... | collective-permute-start | bytes 786440 | tf_op jit(solution)/shard_map/ppermute | solution.py:30
  57.0 11.9 %collective-permute-start.6 = (f32[256,256]{1,0:T(8,128)S(1)}, f32[256,256]{1,0:T(8,128)S(1)}, u32[]{:S(2)}, u32[]{:S(2)}) collective-permute-start(f32[256,256]{1,0:T(8,128)S(1)} %fusion.13), channel_id=1, source_target_pairs={{0,16},{2,18},{4,20},{6,22},{8,24},{10,26},{12,28},{14,30},{16,0},... | collective-permute-start | bytes 786440 | tf_op jit(solution)/shard_map/ppermute | solution.py:30
  64.1 52.6 %all-to-all-start.2 = ((f32[16,4,2,16,256]{4,3,2,1,0:T(8,128)}), f32[16,4,2,16,256]{4,3,2,1,0:T(8,128)S(1)}, u32[]{:S(2)}, u32[]{:S(2)}) async-start(f32[16,4,2,16,256]{4,3,2,1,0:T(8,128)} %batch_first.3), calls=%async_computation.2 | async-start | bytes 4194304 | tf_op jit(solution)/shard_map/all_to_all | solution.py:289
  69.0 15.2 %collective-permute-start.7 = (f32[128,256]{1,0:T(8,128)S(1)}, f32[128,256]{1,0:T(8,128)S(1)}, u32[]{:S(2)}, u32[]{:S(2)}) collective-permute-start(f32[128,256]{1,0:T(8,128)S(1)} %get-tuple-element.55), channel_id=1, source_target_pairs={{0,4},{2,6},{4,0},{6,2},{8,12},{10,14},{12,8},{14,10},{16,20},{18,... | collective-permute-start | bytes 393224 | tf_op jit(solution)/shard_map/ppermute | solution.py:30
  69.3 14.8 %collective-permute-start.9 = (f32[128,256]{1,0:T(8,128)S(1)}, f32[128,256]{1,0:T(8,128)S(1)}, u32[]{:S(2)}, u32[]{:S(2)}) collective-permute-start(f32[128,256]{1,0:T(8,128)S(1)} %get-tuple-element.56), channel_id=1, source_target_pairs={{0,1},{1,0},{2,3},{3,2},{4,5},{5,4},{6,7},{7,6},{8,9},{9,8},{10,11... | collective-permute-start | bytes 393224 | tf_op jit(solution)/shard_map/ppermute | solution.py:30
  84.2 11.4 %collective-permute-start.10 = (f32[256,256]{1,0:T(8,128)S(1)}, f32[256,256]{1,0:T(8,128)S(1)}, u32[]{:S(2)}, u32[]{:S(2)}) collective-permute-start(f32[256,256]{1,0:T(8,128)S(1)} %pad_maximum_fusion.5), channel_id=1, source_target_pairs={{0,4},{2,6},{4,0},{6,2},{8,12},{10,14},{12,8},{14,10},{16,20},{18,... | collective-permute-start | bytes 786440 | tf_op jit(solution)/shard_map/ppermute | solution.py:30
  84.3 11.3 %collective-permute-start.8 = (f32[256,256]{1,0:T(8,128)S(1)}, f32[256,256]{1,0:T(8,128)S(1)}, u32[]{:S(2)}, u32[]{:S(2)}) collective-permute-start(f32[256,256]{1,0:T(8,128)S(1)} %pad_maximum_fusion.4), channel_id=1, source_target_pairs={{0,1},{1,0},{2,3},{3,2},{4,5},{5,4},{6,7},{7,6},{8,9},{9,8},{10,11... | collective-permute-start | bytes 786440 | tf_op jit(solution)/shard_map/ppermute | solution.py:30
  95.7 3.0 %copy-start.3 = (f32[1024,256]{1,0:T(8,128)}, f32[1024,256]{1,0:T(8,128)S(1)}, u32[]{:S(2)}) copy-start(f32[1024,256]{1,0:T(8,128)S(1)} %pad_maximum_fusion.1) | copy-start | bytes 3145732
  95.8 3.0 %collective-permute-start.11 = (f32[1024,256]{1,0:T(8,128)S(1)}, f32[1024,256]{1,0:T(8,128)}, u32[]{:S(2)}, u32[]{:S(2)}) collective-permute-start(f32[1024,256]{1,0:T(8,128)S(1)} %pad_maximum_fusion.1), channel_id=1, source_target_pairs={{0,2},{2,0},{4,6},{6,4},{8,10},{10,8},{12,14},{14,12},{16,18},{18,... | collective-permute-start | bytes 3145736 | tf_op jit(solution)/shard_map/ppermute | solution.py:30
  116.7 1.3 copy-start.1
  118.0 64.0 %all-to-all-start.1 = ((f32[16,4,2,16,256]{4,3,2,1,0:T(8,128)}), f32[16,4,2,16,256]{4,3,2,1,0:T(8,128)}, u32[]{:S(2)}, u32[]{:S(2)}) async-start(f32[16,4,2,16,256]{4,3,2,1,0:T(8,128)} %absorb.3), calls=%async_computation.1 | async-start | bytes 4194304 | tf_op jit(solution)/shard_map/all_to_all | solution.py:289
  131.0 2.0 collective-permute-start.12
  134.2 26.7 %collective-permute-start.18 = (f32[1,2,2,2,16,256]{5,4,3,2,1,0:T(8,128)S(1)}, f32[1,2,2,2,16,256]{5,4,3,2,1,0:T(8,128)S(1)}, u32[]{:S(2)}, u32[]{:S(2)}) collective-permute-start(f32[1,2,2,2,16,256]{5,4,3,2,1,0:T(8,128)S(1)} %fusion.11), channel_id=1, source_target_pairs={{0,8},{2,10},{4,12},{6,14},{8,0},{10,2},{12,4},{14,6},{16,24},{18,... | collective-permute-start | bytes 393224 | tf_op jit(solution)/shard_map/ppermute | solution.py:30
  135.3 26.5 %collective-permute-start.19 = (f32[1,2,2,2,16,256]{5,4,3,2,1,0:T(8,128)S(1)}, f32[1,2,2,2,16,256]{5,4,3,2,1,0:T(8,128)S(1)}, u32[]{:S(2)}, u32[]{:S(2)}) collective-permute-start(f32[1,2,2,2,16,256]{5,4,3,2,1,0:T(8,128)S(1)} %get-tuple-element.35), channel_id=1, source_target_pairs={{0,4},{2,6},{4,0},{6,2},{8,12},{10,14},{12,8},{14,10},{16,20},{18,... | collective-permute-start | bytes 393224 | tf_op jit(solution)/shard_map/ppermute | solution.py:30
  142.7 44.4 %collective-permute-start.13 = (f32[1,2,2,2,16,256]{5,4,3,2,1,0:T(8,128)}, f32[1,2,2,2,16,256]{5,4,3,2,1,0:T(8,128)S(1)}, u32[]{:S(2)}, u32[]{:S(2)}) collective-permute-start(f32[1,2,2,2,16,256]{5,4,3,2,1,0:T(8,128)} %get-tuple-element.36), channel_id=1, source_target_pairs={{0,28},{2,30},{4,24},{6,26},{8,20},{10,22},{12,16},{14,18},{16,12}... | collective-permute-start | bytes 393224 | tf_op jit(solution)/shard_map/ppermute | solution.py:30
  145.9 41.2 %collective-permute-start.14 = (f32[1,2,2,2,16,256]{5,4,3,2,1,0:T(8,128)S(1)}, f32[1,2,2,2,16,256]{5,4,3,2,1,0:T(8,128)S(1)}, u32[]{:S(2)}, u32[]{:S(2)}) collective-permute-start(f32[1,2,2,2,16,256]{5,4,3,2,1,0:T(8,128)S(1)} %get-tuple-element.37), channel_id=1, source_target_pairs={{0,24},{2,26},{4,28},{6,30},{8,16},{10,18},{12,20},{14,22},{16,8},... | collective-permute-start | bytes 393224 | tf_op jit(solution)/shard_map/ppermute | solution.py:30
  145.9 41.6 %collective-permute-start.15 = (f32[1,2,2,2,16,256]{5,4,3,2,1,0:T(8,128)S(1)}, f32[1,2,2,2,16,256]{5,4,3,2,1,0:T(8,128)S(1)}, u32[]{:S(2)}, u32[]{:S(2)}) collective-permute-start(f32[1,2,2,2,16,256]{5,4,3,2,1,0:T(8,128)S(1)} %get-tuple-element.38), channel_id=1, source_target_pairs={{0,20},{2,22},{4,16},{6,18},{8,28},{10,30},{12,24},{14,26},{16,4},... | collective-permute-start | bytes 393224 | tf_op jit(solution)/shard_map/ppermute | solution.py:30
  161.0 34.8 %collective-permute-start.16 = (f32[1,2,2,2,16,256]{5,4,3,2,1,0:T(8,128)S(1)}, f32[1,2,2,2,16,256]{5,4,3,2,1,0:T(8,128)S(1)}, u32[]{:S(2)}, u32[]{:S(2)}) collective-permute-start(f32[1,2,2,2,16,256]{5,4,3,2,1,0:T(8,128)S(1)} %get-tuple-element.39), channel_id=1, source_target_pairs={{0,16},{2,18},{4,20},{6,22},{8,24},{10,26},{12,28},{14,30},{16,0},... | collective-permute-start | bytes 393224 | tf_op jit(solution)/shard_map/ppermute | solution.py:30
  161.7 34.1 %collective-permute-start.17 = (f32[1,2,2,2,16,256]{5,4,3,2,1,0:T(8,128)S(1)}, f32[1,2,2,2,16,256]{5,4,3,2,1,0:T(8,128)S(1)}, u32[]{:S(2)}, u32[]{:S(2)}) collective-permute-start(f32[1,2,2,2,16,256]{5,4,3,2,1,0:T(8,128)S(1)} %get-tuple-element.40), channel_id=1, source_target_pairs={{0,12},{2,14},{4,8},{6,10},{8,4},{10,6},{12,0},{14,2},{16,28},{18,... | collective-permute-start | bytes 393224 | tf_op jit(solution)/shard_map/ppermute | solution.py:30
  182.1 33.0 %all-to-all-start.3 = ((f32[16,2,2,16,256]{4,3,2,1,0:T(8,128)}), f32[16,2,2,16,256]{4,3,2,1,0:T(8,128)S(1)}, u32[]{:S(2)}, u32[]{:S(2)}) async-start(f32[16,2,2,16,256]{4,3,2,1,0:T(8,128)} %absorb.5), calls=%async_computation.3 | async-start | bytes 2097152 | tf_op jit(solution)/shard_map/all_to_all | solution.py:289

commit v8 on v7

--- a/solution.py
+++ b/solution.py
@@ -69,12 +69,11 @@
     halves = list(jnp.split(held, 2))
     for at in range(len(orders[0])):
         halves = [halve(part, order[at]) for part, order in zip(halves, orders)]
-    return jnp.concatenate(halves, 0)
-
-
-def gather_branches(held, rows, cols):
+    return halves
+
+
+def gather_branches(halves, rows, cols):
     first, orders, _ = broadcast_orders(rows, cols)
-    halves = list(jnp.split(held, 2))
     for at in reversed(range(len(orders[0]))):
         halves = [double(part, order[at]) for part, order in zip(halves, orders)]
     held = jnp.concatenate(halves, 0)
@@ -323,17 +322,18 @@
     sent_low = batch_first(stem_slab, rows, 0, low)
     sent_low, factors = lax.optimization_barrier((sent_low, factors))
     stem_low = exchange(sent_low)
-    held = scatter_branches(build_branch(factors[0]), branch_owner, rows, cols)
+    halves = scatter_branches(build_branch(factors[0]), branch_owner, rows, cols)
     cosine, sine = jnp.cos(entangle_phase), jnp.sin(entangle_phase)
     far = broadcast_orders(rows, cols)[2]
     for bit in far[:-1]:
-        held = held + swap(held, "row", rows, bit)
+        halves = [half + swap(half, "row", rows, bit) for half in halves]
     sent_high = batch_first(stem_slab, rows, low, high)
+    held = jnp.concatenate(halves, 0)
     held, sent_high, cosine, sine = lax.optimization_barrier((held, sent_high, cosine, sine))
     for bit in far[-1:]:
         held = held + swap(held, "row", rows, bit)
     stem_high = exchange(sent_high)
-    branches = gather_branches(held, rows, cols)
+    branches = gather_branches(jnp.split(held, 2), rows, cols)
     back_low = exchange(absorb(stem_low, branches, cosine, sine, weight=WEIGHT))
     some = min(2, high - 1)
     pairs, pieces = send_chips(absorb(stem_high, branches, cosine, sine, high - some, some))

time: 219 us -> 219 us (level)
  starting transfers between devices: 44.7 us -> 51 us
  waiting for transfers between devices: 118 us -> 112 us
    ppermute x20 -> x21, starting transfers between devices: 23.6 us -> 29.4 us  [swap(): return lax.ppermute(array, axis, [(i, i ^ bit) for i in range(size)])]
    ppermute x20 -> x21, waiting for transfers between devices: 71.6 us -> 65.9 us  [swap(): return lax.ppermute(array, axis, [(i, i ^ bit) for i in range(size)])]
  transfers between devices with their start and end apart: 24 -> 25, of which waited for: 16 -> 16; matrix products, arithmetic and copies ran while one was open for 5% -> 5% of each run, Pallas kernels for 16% -> 16%
where the time goes in v8:
time: 219 us
  waiting for transfers between devices  112 us (51%)
  starting transfers between devices  51 us (23%)
  Pallas kernels  42.5 us (19%)
  local copies, waits for them, and re-layouts  7.38 us (3%)
  other arithmetic  4.13 us (2%)
    ppermute x21, waiting for transfers between devices, swap(): return lax.ppermute(array, axis, [(i, i ^ bit) for i in range(size)])  65.9 us
    all_to_all x4, waiting for transfers between devices, exchange(): return lax.all_to_all(parts, 'row', 0, 0, tiled=True)  45.7 us
    ppermute x21, starting transfers between devices, swap(): return lax.ppermute(array, axis, [(i, i ^ bit) for i in range(size)])  29.4 us
    pallas_call x3, Pallas kernels, absorb(): pl.pallas_call(absorb_kernel, grid=(count // per,), in_specs=[pl.BlockSpe...  26.6 us
    all_to_all x4, starting transfers between devices, exchange(): return lax.all_to_all(parts, 'row', 0, 0, tiled=True)  21.6 us
    pallas_call x2, Pallas kernels, batch_first(): pl.pallas_call(partial(batch_first_kernel, start * peers), in_specs=[pl.B...  8.34 us
    sin x1, local copies, waits for them, and re-layouts, on_device(): cosine, sine = (jnp.cos(entangle_phase), jnp.sin(entangle_phase))  4.49 us
  transfers between devices with their start and end apart: 25, of which 16 were waited for; matrix products, arithmetic and copies ran while one was open for 5% of the time, Pallas kernels for 16%

profile of v8, /device:TPU:13, one launch (start us, length us, event | category | flops | bytes accessed | tf_op | source)
XLA Modules:
  0.0 218.7 jit_solution(16666569834804106779)
XLA Ops:
  0.0 3.5 %batch_first.2 = f32[16,4,2,16,256]{4,3,2,1,0:T(8,128)} custom-call(f32[2,16,256,128]{3,2,1,0:T(8,128)} %stem_ref.3), custom_call_target="tpu_custom_call" | custom-call | bytes 8388608 | tf_op jit(solution)/shard_map/batch_first/pallas_call | solution.py:210
  3.6 6.7 %all-to-all-start = ((f32[16,4,2,16,256]{4,3,2,1,0:T(8,128)}), f32[16,4,2,16,256]{4,3,2,1,0:T(8,128)}, u32[]{:S(2)}, u32[]{:S(2)}) async-start(f32[16,4,2,16,256]{4,3,2,1,0:T(8,128)} %batch_first.2), calls=%async_computation | async-start | bytes 4194304 | tf_op jit(solution)/shard_map/all_to_all | solution.py:288
  12.9 2.4 %collective-permute-done = f32[1024,256]{1,0:T(8,128)} collective-permute-done((f32[1024,256]{1,0:T(8,128)S(1)}, f32[1024,256]{1,0:T(8,128)}, u32[]{:S(2)}, u32[]{:S(2)}) %collective-permute-start) | collective-permute-done | bytes 1048608 | tf_op jit(solution)/shard_map/ppermute | solution.py:30
  18.5 9.9 %collective-permute-done.4 = f32[256,256]{1,0:T(8,128)S(1)} collective-permute-done((f32[256,256]{1,0:T(8,128)S(1)}, f32[256,256]{1,0:T(8,128)S(1)}, u32[]{:S(2)}, u32[]{:S(2)}) %collective-permute-start.4) | collective-permute-done | bytes 262176 | tf_op jit(solution)/shard_map/ppermute | solution.py:30
  29.9 2.9 %collective-permute-done.5 = f32[128,256]{1,0:T(8,128)S(1)} collective-permute-done((f32[128,256]{1,0:T(8,128)S(1)}, f32[128,256]{1,0:T(8,128)S(1)}, u32[]{:S(2)}, u32[]{:S(2)}) %collective-permute-start.5) | collective-permute-done | bytes 131104 | tf_op jit(solution)/shard_map/ppermute | solution.py:30
  32.8 4.1 %collective-permute-start.6 = (f32[128,256]{1,0:T(8,128)S(1)}, f32[128,256]{1,0:T(8,128)S(1)}, u32[]{:S(2)}, u32[]{:S(2)}) collective-permute-start(f32[128,256]{1,0:T(8,128)S(1)} %dynamic-slice_add_fusion.3), channel_id=1, source_target_pairs={{0,8},{2,10},{4,12},{6,14},{8,0},{10,2},{12,4},{14,6},{16,24},{18,... | collective-permute-start | bytes 393224 | tf_op jit(solution)/shard_map/ppermute | solution.py:30
  37.3 5.7 %collective-permute-start.3 = (f32[128,256]{1,0:T(8,128)S(1)}, f32[128,256]{1,0:T(8,128)S(1)}, u32[]{:S(2)}, u32[]{:S(2)}) collective-permute-start(f32[128,256]{1,0:T(8,128)S(1)} %dynamic-slice_add_fusion.4), channel_id=1, source_target_pairs={{0,8},{2,10},{4,12},{6,14},{8,0},{10,2},{12,4},{14,6},{16,24},{18,... | collective-permute-start | bytes 393224 | tf_op jit(solution)/shard_map/ppermute | solution.py:30
  43.0 4.5 %fusion.13 = (f32[4,256,256]{2,1,0:T(8,128)}, f32[4,256,256]{2,1,0:T(8,128)}) fusion(f32[4,256,256]{2,1,0:T(8,128)S(1)} %copy-done.2), kind=kLoop, calls=%fused_computation.69 | loop fusion | bytes 3145728 | tf_op jit(solution)/shard_map/sin | solution.py:326
  47.5 4.8 %batch_first.3 = f32[16,4,2,16,256]{4,3,2,1,0:T(8,128)} custom-call(f32[2,16,256,128]{3,2,1,0:T(8,128)} %stem_ref.3), custom_call_target="tpu_custom_call" | custom-call | bytes 8388608 | tf_op jit(solution)/shard_map/batch_first/pallas_call | solution.py:210
  52.3 1.8 collective-permute-done.3
  54.2 2.6 %collective-permute-start.7 = (f32[256,256]{1,0:T(8,128)S(1)}, f32[256,256]{1,0:T(8,128)S(1)}, u32[]{:S(2)}, u32[]{:S(2)}) collective-permute-start(f32[256,256]{1,0:T(8,128)S(1)} %pad_maximum_fusion.3), channel_id=1, source_target_pairs={{0,16},{2,18},{4,20},{6,22},{8,24},{10,26},{12,28},{14,30},{16,0},... | collective-permute-start | bytes 786440 | tf_op jit(solution)/shard_map/ppermute | solution.py:30
  56.8 7.1 %all-to-all-done.stem_ref = f32[16,4,2,16,256]{4,3,2,1,0:T(8,128)} async-done(((f32[16,4,2,16,256]{4,3,2,1,0:T(8,128)}), f32[16,4,2,16,256]{4,3,2,1,0:T(8,128)}, u32[]{:S(2)}, u32[]{:S(2)}) %all-to-all-start) | async-done | bytes 2097184 | tf_op jit(solution)/shard_map/all_to_all | solution.py:288
  63.9 4.9 %all-to-all-start.2 = ((f32[16,4,2,16,256]{4,3,2,1,0:T(8,128)}), f32[16,4,2,16,256]{4,3,2,1,0:T(8,128)S(1)}, u32[]{:S(2)}, u32[]{:S(2)}) async-start(f32[16,4,2,16,256]{4,3,2,1,0:T(8,128)} %batch_first.3), calls=%async_computation.2 | async-start | bytes 4194304 | tf_op jit(solution)/shard_map/all_to_all | solution.py:288
  70.5 13.6 %collective-permute-done.8 = f32[128,256]{1,0:T(8,128)S(1)} collective-permute-done((f32[128,256]{1,0:T(8,128)S(1)}, f32[128,256]{1,0:T(8,128)S(1)}, u32[]{:S(2)}, u32[]{:S(2)}) %collective-permute-start.8) | collective-permute-done | bytes 131104 | tf_op jit(solution)/shard_map/ppermute | solution.py:30
  85.5 10.3 %collective-permute-done.11 = f32[256,256]{1,0:T(8,128)S(1)} collective-permute-done((f32[256,256]{1,0:T(8,128)S(1)}, f32[256,256]{1,0:T(8,128)S(1)}, u32[]{:S(2)}, u32[]{:S(2)}) %collective-permute-start.11) | collective-permute-done | bytes 262176 | tf_op jit(solution)/shard_map/ppermute | solution.py:30
  96.6 2.4 %collective-permute-done.12 = f32[1024,256]{1,0:T(8,128)} collective-permute-done((f32[1024,256]{1,0:T(8,128)S(1)}, f32[1024,256]{1,0:T(8,128)}, u32[]{:S(2)}, u32[]{:S(2)}) %collective-permute-start.12) | collective-permute-done | bytes 1048608 | tf_op jit(solution)/shard_map/ppermute | solution.py:30
  99.0 11.9 %absorb.3 = f32[16,4,2,16,256]{4,3,2,1,0:T(8,128)} custom-call(s32[1]{0:T(128)} %bitcast.core_ref, f32[16,4,2,16,256]{4,3,2,1,0:T(8,128)} %all-to-all-done.stem_ref, f32[2,2,256,256]{3,2,1,0:T(8,128)} %bitcast.48, f32[2,2,256,256]{3,2,1,0:T(8,128)} %bitcast.10.other_ref, f32[4,256,256]{2,1,0:T(8,128)} %get-tuple-element.22.cos_ref, ...), custom_call_target="tpu_custom_call" | custom-call | flops 11596411904 | bytes 4194304 | tf_op jit(solution)/shard_map/absorb/pallas_call | solution.py:156
  111.0 5.4 %all-to-all-done.2.stem_ref = f32[16,4,2,16,256]{4,3,2,1,0:T(8,128)S(1)} async-done(((f32[16,4,2,16,256]{4,3,2,1,0:T(8,128)}), f32[16,4,2,16,256]{4,3,2,1,0:T(8,128)S(1)}, u32[]{:S(2)}, u32[]{:S(2)}) %all-to-all-start.2) | async-done | bytes 2097184 | tf_op jit(solution)/shard_map/all_to_all | solution.py:288
  117.7 4.9 %all-to-all-start.1 = ((f32[16,4,2,16,256]{4,3,2,1,0:T(8,128)}), f32[16,4,2,16,256]{4,3,2,1,0:T(8,128)}, u32[]{:S(2)}, u32[]{:S(2)}) async-start(f32[16,4,2,16,256]{4,3,2,1,0:T(8,128)} %absorb.3), calls=%async_computation.1 | async-start | bytes 4194304 | tf_op jit(solution)/shard_map/all_to_all | solution.py:288
  122.5 7.3 %absorb.4 = f32[16,2,2,16,256]{4,3,2,1,0:T(8,128)} custom-call(s32[1]{0:T(128)} %bitcast.core_ref, f32[16,4,2,16,256]{4,3,2,1,0:T(8,128)} %copy-done.1, f32[2,2,256,256]{3,2,1,0:T(8,128)} %bitcast.49, f32[2,2,256,256]{3,2,1,0:T(8,128)} %bitcast.10.other_ref, f32[4,256,256]{2,1,0:T(8,128)} %get-tuple-element.22.cos_ref, f32[4,256,256]{2,1,0:T(8,128)} %get-tuple-element.23.sin_ref), custom_call_target="tpu_custom_call" | custom-call | flops 3221225472 | bytes 2097152 | tf_op jit(solution)/shard_map/absorb/pallas_call | solution.py:156
  131.4 1.5 collective-permute-done.13
  135.3 7.3 %absorb.5 = f32[16,2,2,16,256]{4,3,2,1,0:T(8,128)} custom-call(s32[1]{0:T(128)} %bitcast.core_ref, f32[16,4,2,16,256]{4,3,2,1,0:T(8,128)} %copy-done.1, f32[2,2,256,256]{3,2,1,0:T(8,128)} %bitcast.50, f32[2,2,256,256]{3,2,1,0:T(8,128)} %bitcast.10.other_ref, f32[4,256,256]{2,1,0:T(8,128)} %get-tuple-element.22.cos_ref, f32[4,256,256]{2,1,0:T(8,128)} %get-tuple-element.23.sin_ref), custom_call_target="tpu_custom_call" | custom-call | flops 3221225472 | bytes 2097152 | tf_op jit(solution)/shard_map/absorb/pallas_call | solution.py:156
  142.6 3.2 %collective-permute-start.14 = (f32[1,2,2,2,16,256]{5,4,3,2,1,0:T(8,128)}, f32[1,2,2,2,16,256]{5,4,3,2,1,0:T(8,128)S(1)}, u32[]{:S(2)}, u32[]{:S(2)}) collective-permute-start(f32[1,2,2,2,16,256]{5,4,3,2,1,0:T(8,128)} %get-tuple-element.36), channel_id=1, source_target_pairs={{0,28},{2,30},{4,24},{6,26},{8,20},{10,22},{12,16},{14,18},{16,12}... | collective-permute-start | bytes 393224 | tf_op jit(solution)/shard_map/ppermute | solution.py:30
  145.8 3.3 %collective-permute-start.16 = (f32[1,2,2,2,16,256]{5,4,3,2,1,0:T(8,128)S(1)}, f32[1,2,2,2,16,256]{5,4,3,2,1,0:T(8,128)S(1)}, u32[]{:S(2)}, u32[]{:S(2)}) collective-permute-start(f32[1,2,2,2,16,256]{5,4,3,2,1,0:T(8,128)S(1)} %get-tuple-element.38), channel_id=1, source_target_pairs={{0,20},{2,22},{4,16},{6,18},{8,28},{10,30},{12,24},{14,26},{16,4},... | collective-permute-start | bytes 393224 | tf_op jit(solution)/shard_map/ppermute | solution.py:30
  149.1 11.9 %collective-permute-done.19 = f32[1,2,2,2,16,256]{5,4,3,2,1,0:T(8,128)S(1)} collective-permute-done((f32[1,2,2,2,16,256]{5,4,3,2,1,0:T(8,128)S(1)}, f32[1,2,2,2,16,256]{5,4,3,2,1,0:T(8,128)S(1)}, u32[]{:S(2)}, u32[]{:S(2)}) %collective-permute-start.19) | collective-permute-done | bytes 131104 | tf_op jit(solution)/shard_map/ppermute | solution.py:30
  161.7 2.1 collective-permute-start.18
  163.8 18.2 %all-to-all-done.1.stem_ref = f32[16,4,2,16,256]{4,3,2,1,0:T(8,128)} async-done(((f32[16,4,2,16,256]{4,3,2,1,0:T(8,128)}), f32[16,4,2,16,256]{4,3,2,1,0:T(8,128)}, u32[]{:S(2)}, u32[]{:S(2)}) %all-to-all-start.1) | async-done | bytes 2097184 | tf_op jit(solution)/shard_map/all_to_all | solution.py:288
  182.0 5.1 %all-to-all-start.3 = ((f32[16,2,2,16,256]{4,3,2,1,0:T(8,128)}), f32[16,2,2,16,256]{4,3,2,1,0:T(8,128)S(1)}, u32[]{:S(2)}, u32[]{:S(2)}) async-start(f32[16,2,2,16,256]{4,3,2,1,0:T(8,128)} %absorb.5), calls=%async_computation.3 | async-start | bytes 2097152 | tf_op jit(solution)/shard_map/all_to_all | solution.py:288
  187.5 8.3 %collective-permute-done.17 = f32[1,2,2,2,16,256]{5,4,3,2,1,0:T(8,128)S(1)} collective-permute-done((f32[1,2,2,2,16,256]{5,4,3,2,1,0:T(8,128)S(1)}, f32[1,2,2,2,16,256]{5,4,3,2,1,0:T(8,128)S(1)}, u32[]{:S(2)}, u32[]{:S(2)}) %collective-permute-start.17) | collective-permute-done | bytes 131104 | tf_op jit(solution)/shard_map/ppermute | solution.py:30
  195.7 4.1 %rows_first.1.low_ref = f32[2,16,64,256]{3,2,1,0:T(8,128)} custom-call(f32[16,4,2,16,256]{4,3,2,1,0:T(8,128)} %all-to-all-done.1.stem_ref), custom_call_target="tpu_custom_call" | custom-call | flops 48000000000 | bytes 4194304 | tf_op jit(solution)/shard_map/rows_first/pallas_call | solution.py:236
  200.0 15.1 %all-to-all-done.3.refs_0_ = f32[16,2,2,16,256]{4,3,2,1,0:T(8,128)S(1)} async-done(((f32[16,2,2,16,256]{4,3,2,1,0:T(8,128)}), f32[16,2,2,16,256]{4,3,2,1,0:T(8,128)S(1)}, u32[]{:S(2)}, u32[]{:S(2)}) %all-to-all-start.3) | async-done | bytes 1048608 | tf_op jit(solution)/shard_map/all_to_all | solution.py:288
  215.0 3.5 %batch_last.1 = f32[2,16,256,128]{3,2,1,0:T(8,128)} custom-call(f32[2,16,64,256]{3,2,1,0:T(8,128)} %rows_first.1.low_ref, f32[16,2,2,16,256]{4,3,2,1,0:T(8,128)S(1)} %all-to-all-done.3.refs_0_, f32[16,2,2,16,256]{4,3,2,1,0:T(8,128)S(1)} %bitcast.43), custom_call_target="tpu_custom_call" | custom-call | tf_op jit(solution)/shard_map/batch_last/pallas_call | solution.py:271
  (79 shorter events, 17.7 us)
Async XLA Ops:
  3.6 6.7 %copy-start = (f32[1,2,2,256,256]{4,3,2,1,0:T(8,128)S(1)}, f32[1,2,2,256,256]{4,3,2,1,0:T(8,128)}, u32[]{:S(2)}) copy-start(f32[1,2,2,256,256]{4,3,2,1,0:T(8,128)} %param.5) | copy-start | bytes 3145732
  3.6 60.3 %all-to-all-start = ((f32[16,4,2,16,256]{4,3,2,1,0:T(8,128)}), f32[16,4,2,16,256]{4,3,2,1,0:T(8,128)}, u32[]{:S(2)}, u32[]{:S(2)}) async-start(f32[16,4,2,16,256]{4,3,2,1,0:T(8,128)} %batch_first.2), calls=%async_computation | async-start | bytes 4194304 | tf_op jit(solution)/shard_map/all_to_all | solution.py:288
  10.3 1.2 copy-start.4
  12.5 2.9 %collective-permute-start = (f32[1024,256]{1,0:T(8,128)S(1)}, f32[1024,256]{1,0:T(8,128)}, u32[]{:S(2)}, u32[]{:S(2)}) collective-permute-start(f32[1024,256]{1,0:T(8,128)S(1)} %constant_dynamic-slice_fusion.4), channel_id=1, source_target_pairs={{0,2},{2,0},{4,6},{6,4},{8,10},{10,8},{12,14},{14,12},{16,18},{18,... | collective-permute-start | bytes 3145736 | tf_op jit(solution)/shard_map/ppermute | solution.py:30
  16.8 26.2 %copy-start.2 = (f32[4,256,256]{2,1,0:T(8,128)S(1)}, f32[4,256,256]{2,1,0:T(8,128)}, u32[]{:S(2)}) copy-start(f32[4,256,256]{2,1,0:T(8,128)} %param.7) | copy-start | bytes 3145732
  16.8 11.6 %collective-permute-start.4 = (f32[256,256]{1,0:T(8,128)S(1)}, f32[256,256]{1,0:T(8,128)S(1)}, u32[]{:S(2)}, u32[]{:S(2)}) collective-permute-start(f32[256,256]{1,0:T(8,128)S(1)} %constant_dynamic-slice_fusion.1), channel_id=1, source_target_pairs={{0,4},{2,6},{4,0},{6,2},{8,12},{10,14},{12,8},{14,10},{16,20},{18,... | collective-permute-start | bytes 786440 | tf_op jit(solution)/shard_map/ppermute | solution.py:30
  17.2 12.5 %collective-permute-start.1 = (f32[256,256]{1,0:T(8,128)S(1)}, f32[256,256]{1,0:T(8,128)S(1)}, u32[]{:S(2)}, u32[]{:S(2)}) collective-permute-start(f32[256,256]{1,0:T(8,128)S(1)} %constant_dynamic-slice_fusion.3), channel_id=1, source_target_pairs={{0,1},{1,0},{2,3},{3,2},{4,5},{5,4},{6,7},{7,6},{8,9},{9,8},{10,11... | collective-permute-start | bytes 786440 | tf_op jit(solution)/shard_map/ppermute | solution.py:30
  28.4 4.3 %collective-permute-start.5 = (f32[128,256]{1,0:T(8,128)S(1)}, f32[128,256]{1,0:T(8,128)S(1)}, u32[]{:S(2)}, u32[]{:S(2)}) collective-permute-start(f32[128,256]{1,0:T(8,128)S(1)} %constant_dynamic-slice_fusion), channel_id=1, source_target_pairs={{0,1},{1,0},{2,3},{3,2},{4,5},{5,4},{6,7},{7,6},{8,9},{9,8},{10,11... | collective-permute-start | bytes 393224 | tf_op jit(solution)/shard_map/ppermute | solution.py:30
  29.8 7.5 %collective-permute-start.2 = (f32[128,256]{1,0:T(8,128)S(1)}, f32[128,256]{1,0:T(8,128)S(1)}, u32[]{:S(2)}, u32[]{:S(2)}) collective-permute-start(f32[128,256]{1,0:T(8,128)S(1)} %constant_dynamic-slice_fusion.2), channel_id=1, source_target_pairs={{0,4},{2,6},{4,0},{6,2},{8,12},{10,14},{12,8},{14,10},{16,20},{18,... | collective-permute-start | bytes 393224 | tf_op jit(solution)/shard_map/ppermute | solution.py:30
  32.8 19.5 %collective-permute-start.6 = (f32[128,256]{1,0:T(8,128)S(1)}, f32[128,256]{1,0:T(8,128)S(1)}, u32[]{:S(2)}, u32[]{:S(2)}) collective-permute-start(f32[128,256]{1,0:T(8,128)S(1)} %dynamic-slice_add_fusion.3), channel_id=1, source_target_pairs={{0,8},{2,10},{4,12},{6,14},{8,0},{10,2},{12,4},{14,6},{16,24},{18,... | collective-permute-start | bytes 393224 | tf_op jit(solution)/shard_map/ppermute | solution.py:30
  37.3 16.9 %collective-permute-start.3 = (f32[128,256]{1,0:T(8,128)S(1)}, f32[128,256]{1,0:T(8,128)S(1)}, u32[]{:S(2)}, u32[]{:S(2)}) collective-permute-start(f32[128,256]{1,0:T(8,128)S(1)} %dynamic-slice_add_fusion.4), channel_id=1, source_target_pairs={{0,8},{2,10},{4,12},{6,14},{8,0},{10,2},{12,4},{14,6},{16,24},{18,... | collective-permute-start | bytes 393224 | tf_op jit(solution)/shard_map/ppermute | solution.py:30
  54.2 14.6 %collective-permute-start.7 = (f32[256,256]{1,0:T(8,128)S(1)}, f32[256,256]{1,0:T(8,128)S(1)}, u32[]{:S(2)}, u32[]{:S(2)}) collective-permute-start(f32[256,256]{1,0:T(8,128)S(1)} %pad_maximum_fusion.3), channel_id=1, source_target_pairs={{0,16},{2,18},{4,20},{6,22},{8,24},{10,26},{12,28},{14,30},{16,0},... | collective-permute-start | bytes 786440 | tf_op jit(solution)/shard_map/ppermute | solution.py:30
  63.9 52.5 %all-to-all-start.2 = ((f32[16,4,2,16,256]{4,3,2,1,0:T(8,128)}), f32[16,4,2,16,256]{4,3,2,1,0:T(8,128)S(1)}, u32[]{:S(2)}, u32[]{:S(2)}) async-start(f32[16,4,2,16,256]{4,3,2,1,0:T(8,128)} %batch_first.3), calls=%async_computation.2 | async-start | bytes 4194304 | tf_op jit(solution)/shard_map/all_to_all | solution.py:288
  68.9 15.2 %collective-permute-start.8 = (f32[128,256]{1,0:T(8,128)S(1)}, f32[128,256]{1,0:T(8,128)S(1)}, u32[]{:S(2)}, u32[]{:S(2)}) collective-permute-start(f32[128,256]{1,0:T(8,128)S(1)} %get-tuple-element.55), channel_id=1, source_target_pairs={{0,4},{2,6},{4,0},{6,2},{8,12},{10,14},{12,8},{14,10},{16,20},{18,... | collective-permute-start | bytes 393224 | tf_op jit(solution)/shard_map/ppermute | solution.py:30
  69.2 14.8 %collective-permute-start.10 = (f32[128,256]{1,0:T(8,128)S(1)}, f32[128,256]{1,0:T(8,128)S(1)}, u32[]{:S(2)}, u32[]{:S(2)}) collective-permute-start(f32[128,256]{1,0:T(8,128)S(1)} %get-tuple-element.56), channel_id=1, source_target_pairs={{0,1},{1,0},{2,3},{3,2},{4,5},{5,4},{6,7},{7,6},{8,9},{9,8},{10,11... | collective-permute-start | bytes 393224 | tf_op jit(solution)/shard_map/ppermute | solution.py:30
  84.2 11.7 %collective-permute-start.11 = (f32[256,256]{1,0:T(8,128)S(1)}, f32[256,256]{1,0:T(8,128)S(1)}, u32[]{:S(2)}, u32[]{:S(2)}) collective-permute-start(f32[256,256]{1,0:T(8,128)S(1)} %pad_maximum_fusion.5), channel_id=1, source_target_pairs={{0,4},{2,6},{4,0},{6,2},{8,12},{10,14},{12,8},{14,10},{16,20},{18,... | collective-permute-start | bytes 786440 | tf_op jit(solution)/shard_map/ppermute | solution.py:30
  84.3 11.6 %collective-permute-start.9 = (f32[256,256]{1,0:T(8,128)S(1)}, f32[256,256]{1,0:T(8,128)S(1)}, u32[]{:S(2)}, u32[]{:S(2)}) collective-permute-start(f32[256,256]{1,0:T(8,128)S(1)} %pad_maximum_fusion.4), channel_id=1, source_target_pairs={{0,1},{1,0},{2,3},{3,2},{4,5},{5,4},{6,7},{7,6},{8,9},{9,8},{10,11... | collective-permute-start | bytes 786440 | tf_op jit(solution)/shard_map/ppermute | solution.py:30
  96.0 3.0 %copy-start.3 = (f32[1024,256]{1,0:T(8,128)}, f32[1024,256]{1,0:T(8,128)S(1)}, u32[]{:S(2)}) copy-start(f32[1024,256]{1,0:T(8,128)S(1)} %pad_maximum_fusion.1) | copy-start | bytes 3145732
  96.1 3.0 %collective-permute-start.12 = (f32[1024,256]{1,0:T(8,128)S(1)}, f32[1024,256]{1,0:T(8,128)}, u32[]{:S(2)}, u32[]{:S(2)}) collective-permute-start(f32[1024,256]{1,0:T(8,128)S(1)} %pad_maximum_fusion.1), channel_id=1, source_target_pairs={{0,2},{2,0},{4,6},{6,4},{8,10},{10,8},{12,14},{14,12},{16,18},{18,... | collective-permute-start | bytes 3145736 | tf_op jit(solution)/shard_map/ppermute | solution.py:30
  116.3 1.3 copy-start.1
  117.7 64.3 %all-to-all-start.1 = ((f32[16,4,2,16,256]{4,3,2,1,0:T(8,128)}), f32[16,4,2,16,256]{4,3,2,1,0:T(8,128)}, u32[]{:S(2)}, u32[]{:S(2)}) async-start(f32[16,4,2,16,256]{4,3,2,1,0:T(8,128)} %absorb.3), calls=%async_computation.1 | async-start | bytes 4194304 | tf_op jit(solution)/shard_map/all_to_all | solution.py:288
  131.0 2.0 collective-permute-start.13
  134.1 26.8 %collective-permute-start.19 = (f32[1,2,2,2,16,256]{5,4,3,2,1,0:T(8,128)S(1)}, f32[1,2,2,2,16,256]{5,4,3,2,1,0:T(8,128)S(1)}, u32[]{:S(2)}, u32[]{:S(2)}) collective-permute-start(f32[1,2,2,2,16,256]{5,4,3,2,1,0:T(8,128)S(1)} %fusion.11), channel_id=1, source_target_pairs={{0,8},{2,10},{4,12},{6,14},{8,0},{10,2},{12,4},{14,6},{16,24},{18,... | collective-permute-start | bytes 393224 | tf_op jit(solution)/shard_map/ppermute | solution.py:30
  135.2 26.5 %collective-permute-start.20 = (f32[1,2,2,2,16,256]{5,4,3,2,1,0:T(8,128)S(1)}, f32[1,2,2,2,16,256]{5,4,3,2,1,0:T(8,128)S(1)}, u32[]{:S(2)}, u32[]{:S(2)}) collective-permute-start(f32[1,2,2,2,16,256]{5,4,3,2,1,0:T(8,128)S(1)} %get-tuple-element.35), channel_id=1, source_target_pairs={{0,4},{2,6},{4,0},{6,2},{8,12},{10,14},{12,8},{14,10},{16,20},{18,... | collective-permute-start | bytes 393224 | tf_op jit(solution)/shard_map/ppermute | solution.py:30
  142.6 44.4 %collective-permute-start.14 = (f32[1,2,2,2,16,256]{5,4,3,2,1,0:T(8,128)}, f32[1,2,2,2,16,256]{5,4,3,2,1,0:T(8,128)S(1)}, u32[]{:S(2)}, u32[]{:S(2)}) collective-permute-start(f32[1,2,2,2,16,256]{5,4,3,2,1,0:T(8,128)} %get-tuple-element.36), channel_id=1, source_target_pairs={{0,28},{2,30},{4,24},{6,26},{8,20},{10,22},{12,16},{14,18},{16,12}... | collective-permute-start | bytes 393224 | tf_op jit(solution)/shard_map/ppermute | solution.py:30
  145.8 41.3 %collective-permute-start.15 = (f32[1,2,2,2,16,256]{5,4,3,2,1,0:T(8,128)S(1)}, f32[1,2,2,2,16,256]{5,4,3,2,1,0:T(8,128)S(1)}, u32[]{:S(2)}, u32[]{:S(2)}) collective-permute-start(f32[1,2,2,2,16,256]{5,4,3,2,1,0:T(8,128)S(1)} %get-tuple-element.37), channel_id=1, source_target_pairs={{0,24},{2,26},{4,28},{6,30},{8,16},{10,18},{12,20},{14,22},{16,8},... | collective-permute-start | bytes 393224 | tf_op jit(solution)/shard_map/ppermute | solution.py:30
  145.8 41.7 %collective-permute-start.16 = (f32[1,2,2,2,16,256]{5,4,3,2,1,0:T(8,128)S(1)}, f32[1,2,2,2,16,256]{5,4,3,2,1,0:T(8,128)S(1)}, u32[]{:S(2)}, u32[]{:S(2)}) collective-permute-start(f32[1,2,2,2,16,256]{5,4,3,2,1,0:T(8,128)S(1)} %get-tuple-element.38), channel_id=1, source_target_pairs={{0,20},{2,22},{4,16},{6,18},{8,28},{10,30},{12,24},{14,26},{16,4},... | collective-permute-start | bytes 393224 | tf_op jit(solution)/shard_map/ppermute | solution.py:30
  160.9 34.8 %collective-permute-start.17 = (f32[1,2,2,2,16,256]{5,4,3,2,1,0:T(8,128)S(1)}, f32[1,2,2,2,16,256]{5,4,3,2,1,0:T(8,128)S(1)}, u32[]{:S(2)}, u32[]{:S(2)}) collective-permute-start(f32[1,2,2,2,16,256]{5,4,3,2,1,0:T(8,128)S(1)} %get-tuple-element.39), channel_id=1, source_target_pairs={{0,16},{2,18},{4,20},{6,22},{8,24},{10,26},{12,28},{14,30},{16,0},... | collective-permute-start | bytes 393224 | tf_op jit(solution)/shard_map/ppermute | solution.py:30
  161.7 34.1 %collective-permute-start.18 = (f32[1,2,2,2,16,256]{5,4,3,2,1,0:T(8,128)S(1)}, f32[1,2,2,2,16,256]{5,4,3,2,1,0:T(8,128)S(1)}, u32[]{:S(2)}, u32[]{:S(2)}) collective-permute-start(f32[1,2,2,2,16,256]{5,4,3,2,1,0:T(8,128)S(1)} %get-tuple-element.40), channel_id=1, source_target_pairs={{0,12},{2,14},{4,8},{6,10},{8,4},{10,6},{12,0},{14,2},{16,28},{18,... | collective-permute-start | bytes 393224 | tf_op jit(solution)/shard_map/ppermute | solution.py:30
  182.0 33.0 %all-to-all-start.3 = ((f32[16,2,2,16,256]{4,3,2,1,0:T(8,128)}), f32[16,2,2,16,256]{4,3,2,1,0:T(8,128)S(1)}, u32[]{:S(2)}, u32[]{:S(2)}) async-start(f32[16,2,2,16,256]{4,3,2,1,0:T(8,128)} %absorb.5), calls=%async_computation.3 | async-start | bytes 2097152 | tf_op jit(solution)/shard_map/all_to_all | solution.py:288
